TPU v7x, 512 devices: a whole 4x8x8 slice. The times are simulated.
512 devices in a mesh: dp: 32 (over y, z_lo), seq: 16 (over x, z_hi, core).
Axes of the slice: x: 4, y: 8, z: 8 (z_hi: 2, z_lo: 4; z = z_hi * 4 + z_lo), core: 2. Of those that a mesh axis runs over, the one named last changes fastest.
Arguments:
- queries: bfloat16 [32, 2048, 768], P('dp', 'seq'), may hold values from -8 to 8
- keys: bfloat16 [32, 2048, 768], P('dp', 'seq'), may hold values from -8 to 8
- values: bfloat16 [32, 2048, 768], P('dp', 'seq'), may hold values from -6 to 6
- cotangent: bfloat16 [32, 2048, 768], P('dp', 'seq'), may hold values from -6 to 6
- pair: bfloat16 [32, 128, 128, 128], P('dp', 'seq'), may hold values from -6 to 6
- pair_weight: float32 [128, 4], replicated, may hold values from -0.5 to 0.5
Outputs:
- attended: bfloat16 [32, 2048, 768], P('dp', 'seq')
- grad_queries: bfloat16 [32, 2048, 768], P('dp', 'seq')
- grad_keys: bfloat16 [32, 2048, 768], P('dp', 'seq')
- grad_values: bfloat16 [32, 2048, 768], P('dp', 'seq')
- grad_pair: bfloat16 [32, 128, 128, 128], P('dp', 'seq')
- grad_weight: float32 [128, 4], replicated
All inputs are finite; a program needn't handle non-finite values.
Results may differ from a plain program's by a relative error of at most 0.023.
Values may be sent and summed in bfloat16 or wider, within the bound.
No kernel may reach another device: no remote copies, remote signals or barrier semaphores. Data moves between devices by JAX's collectives and lax.ppermute only.
A program may use at most 64 MiB of HBM per device.

v0:
```python
import jax
import jax.numpy as jnp
from jax import lax
from jax.sharding import PartitionSpec as P


def expand_table(cells, pool):
    return (jnp.arange(cells)[None, :] // pool == jnp.arange(cells // pool)[:, None]).astype(
        jnp.float32
    )


def add_pooled(products, bias_block, pool):
    heads, qrows, kcols = products.shape
    widened = jnp.einsum(
        "hij,jk->hik", bias_block, expand_table(kcols, pool), precision=lax.Precision.HIGHEST
    )
    shaped = products.reshape(heads, qrows // pool, pool, kcols)
    return (shaped + widened[:, :, None, :]).reshape(heads, qrows, kcols)


def pool_both(dscores, pool):
    heads, qrows, kcols = dscores.shape
    summed = dscores.reshape(heads, qrows // pool, pool, kcols).sum(axis=2)
    return jnp.einsum(
        "hik,jk->hij", summed, expand_table(kcols, pool), precision=lax.Precision.HIGHEST
    )


def local_blocks(step_fn, init, arrays):
    total_rows = arrays[0].shape[0]
    block = min(512, total_rows)

    def advance(index, carry):
        start = (index * block).astype(jnp.int32)
        pieces = tuple((lax.dynamic_slice_in_dim(item, start, block, 0) for item in arrays))
        return step_fn(carry, pieces, start)

    return lax.fori_loop(0, total_rows // block, advance, init)


def body(queries, keys, values, cotangent, pair, pair_weight):
    query_rows = queries[0]
    key_rows = keys[0]
    value_rows = values[0]
    cot_rows = cotangent[0]
    pair_rows = pair[0]
    tokens, width = query_rows.shape
    heads = pair_weight.shape[1]
    hdim = width // heads
    prow = pair_rows.shape[0]
    pcols = pair_rows.shape[1]
    pool = tokens // prow
    scale = hdim ** (-0.5)
    qhead = query_rows.reshape(tokens, heads, hdim)
    khead = key_rows.reshape(tokens, heads, hdim)
    vhead = value_rows.reshape(tokens, heads, hdim)
    chead = cot_rows.reshape(tokens, heads, hdim)
    pair_f = pair_rows.astype(jnp.float32)
    bias_rows = jnp.einsum("ijc,ch->hij", pair_f, pair_weight, precision=lax.Precision.HIGHEST)

    def local_scores(kpiece, start):
        count = kpiece.shape[0]
        products = jnp.einsum(
            "qhe,khe->hqk",
            qhead,
            kpiece.reshape(count, heads, hdim),
            preferred_element_type=jnp.float32,
        )
        bias_block = lax.dynamic_slice_in_dim(bias_rows, start // pool, count // pool, 2)
        return add_pooled(products * scale, bias_block, pool)

    def attend(carry, pieces, start):
        kpiece, vpiece = pieces
        count = kpiece.shape[0]
        old_max, old_total, accum = carry
        scores = local_scores(kpiece, start)
        new_max = jnp.maximum(old_max, jnp.max(scores, axis=-1))
        shrink = jnp.exp(old_max - new_max)
        weights = jnp.exp(scores - new_max[:, :, None])
        new_total = old_total * shrink + jnp.sum(weights, axis=-1)
        accum = accum * shrink[:, :, None] + jnp.einsum(
            "hqk,khe->hqe",
            weights.astype(jnp.bfloat16),
            vpiece.reshape(count, heads, hdim),
            preferred_element_type=jnp.float32,
        )
        return (new_max, new_total, accum)

    start_state = (
        jnp.full((heads, tokens), -1e30, jnp.float32),
        jnp.zeros((heads, tokens), jnp.float32),
        jnp.zeros((heads, tokens, hdim), jnp.float32),
    )
    key_all, value_all = (
        lax.all_gather(key_rows, "seq", axis=0, tiled=True),
        lax.all_gather(value_rows, "seq", axis=0, tiled=True),
    )
    state = local_blocks(attend, start_state, (key_all, value_all))
    run_max, run_total, accum = state
    lse = run_max + jnp.log(run_total)
    attended = jnp.transpose(accum / run_total[:, :, None], (1, 0, 2)).astype(jnp.bfloat16)
    delta = jnp.einsum("qhe,qhe->hq", chead.astype(jnp.float32), attended.astype(jnp.float32))

    def query_back(carry, pieces, start):
        kpiece, vpiece = pieces
        count = kpiece.shape[0]
        dq_acc, dbias_acc = carry
        scores = local_scores(kpiece, start)
        probs = jnp.exp(scores - lse[:, :, None])
        dprod = jnp.einsum(
            "qhe,khe->hqk",
            chead,
            vpiece.reshape(count, heads, hdim),
            preferred_element_type=jnp.float32,
        )
        dscores = probs * (dprod - delta[:, :, None])
        dq_acc = dq_acc + jnp.einsum(
            "hqk,khe->qhe",
            dscores.astype(jnp.bfloat16),
            kpiece.reshape(count, heads, hdim),
            preferred_element_type=jnp.float32,
        )
        pooled = pool_both(dscores, pool)
        column = start // pool
        current = lax.dynamic_slice_in_dim(dbias_acc, column, count // pool, 2)
        dbias_acc = lax.dynamic_update_slice_in_dim(dbias_acc, current + pooled, column, 2)
        return (dq_acc, dbias_acc)

    dq_acc, grad_bias = local_blocks(
        query_back,
        (
            jnp.zeros((tokens, heads, hdim), jnp.float32),
            jnp.zeros((heads, prow, pcols), jnp.float32),
        ),
        (key_all, value_all),
    )
    grad_queries = (dq_acc * scale).reshape(tokens, width).astype(jnp.bfloat16)
    grad_pair = jnp.einsum(
        "hij,ch->ijc", grad_bias, pair_weight, precision=lax.Precision.HIGHEST
    ).astype(jnp.bfloat16)
    weight_term = jnp.einsum("ijc,hij->ch", pair_f, grad_bias, precision=lax.Precision.HIGHEST)
    grad_weight = lax.psum(weight_term, ("dp", "seq"))
    lse_all, delta_all, bias_all = (
        lax.all_gather(lse, "seq", axis=1, tiled=True),
        lax.all_gather(delta, "seq", axis=1, tiled=True),
        lax.all_gather(bias_rows, "seq", axis=1, tiled=True),
    )
    own_cols = lax.axis_index("seq") * prow
    bias_cols = lax.dynamic_slice_in_dim(bias_all, own_cols, prow, 2)
    qpiece = lax.all_gather(query_rows, "seq", axis=0, tiled=True)
    cpiece = lax.all_gather(cot_rows, "seq", axis=0, tiled=True)
    count = qpiece.shape[0]
    qsplit = qpiece.reshape(count, heads, hdim)
    csplit = cpiece.reshape(count, heads, hdim)
    products = jnp.einsum("qhe,khe->hqk", qsplit, khead, preferred_element_type=jnp.float32)
    bias_block = bias_cols
    scores = add_pooled(products * scale, bias_block, pool)
    probs = jnp.exp(scores - lse_all[:, :, None])
    dv_acc = jnp.einsum(
        "hqk,qhe->khe", probs.astype(jnp.bfloat16), csplit, preferred_element_type=jnp.float32
    )
    dprod = jnp.einsum("qhe,khe->hqk", csplit, vhead, preferred_element_type=jnp.float32)
    dscores = probs * (dprod - delta_all[:, :, None])
    dk_acc = jnp.einsum(
        "hqk,qhe->khe", dscores.astype(jnp.bfloat16), qsplit, preferred_element_type=jnp.float32
    )
    dk_acc, dv_acc = (dk_acc, dv_acc)
    grad_keys = (dk_acc * scale).reshape(tokens, width).astype(jnp.bfloat16)
    grad_values = dv_acc.reshape(tokens, width).astype(jnp.bfloat16)
    return (
        attended.reshape(tokens, width)[None],
        grad_queries[None],
        grad_keys[None],
        grad_values[None],
        grad_pair[None],
        grad_weight,
    )


def solution(mesh):
    placed = (
        P("dp", "seq", None),
        P("dp", "seq", None),
        P("dp", "seq", None),
        P("dp", "seq", None),
        P("dp", "seq", None, None),
        P(),
    )
    return jax.shard_map(
        body,
        mesh=mesh,
        in_specs=placed,
        out_specs=(
            P("dp", "seq", None),
            P("dp", "seq", None),
            P("dp", "seq", None),
            P("dp", "seq", None),
            P("dp", "seq", None, None),
            P(),
        ),
        check_vma=False,
    )
```

profile of v0, /device:TPU:1, one launch (start us, length us, event | category | flops | bytes accessed | tf_op | source)
XLA Modules:
  0.0 440.9 jit_solution(14608742824111677596)
XLA Ops:
  7.2 1.8 copy.51
  9.1 1.7 copy.53
  15.4 38.5 %all_gather.24 = f32[4,128,128]{2,0,1:T(4,128)S(1)} all-gather(f32[4,8,128]{2,0,1:T(4,128)S(1)} %fusion.50), channel_id=1, replica_groups=mesh['dp'=32,'seq'=16] {'seq'}, dimensions={1}, use_global_device_ids=true | all-gather | bytes 278528 | tf_op jit(solution)/shard_map/all_gather | solution.py:147
  55.0 39.0 %all-gather.9.cloned.1.call-done = bf16[1,2048,768]{1,2,0:T(8,128)(2,1)} async-done(((bf16[1,128,768]{1,2,0:T(8,128)(2,1)}), bf16[1,2048,768]{1,2,0:T(8,128)(2,1)}) %all-gather.9.cloned.1.call-update) | async-done | bytes 3145744 | tf_op jit(solution)/shard_map/all_gather | solution.py:96
  94.1 75.9 %all-gather.11.cloned.1.call-done = bf16[1,2048,768]{1,2,0:T(8,128)(2,1)} async-done(((bf16[1,128,768]{1,2,0:T(8,128)(2,1)}), bf16[1,2048,768]{1,2,0:T(8,128)(2,1)}) %all-gather.11.cloned.1.call-update) | async-done | bytes 3145744 | tf_op jit(solution)/shard_map/all_gather | solution.py:97
  170.0 31.2 %while.40 = (s32[]{:T(128)}, f32[4,128]{1,0:T(4,128)}, f32[4,128]{1,0:T(4,128)}, f32[4,128,192]{1,2,0:T(8,128)}, bf16[2048,768]{0,1:T(8,128)(2,1)}, /*index=5*/b...) while((s32[]{:T(128)}, f32[4,128]{1,0:T(4,128)}, ...), condition=%wide.region_3.4_spmd.clone, body=%wide.region_0.3_spmd.clone.sunk | while | flops 209771040 | bytes 13226382 | solution.py:39
  170.7 1.5 constant_dynamic-slice_fusion.9
  177.2 1.5 constant_dynamic-slice_fusion.9
  182.6 2.2 convolution_add_fusion.4
  185.4 1.5 constant_dynamic-slice_fusion.9
  190.8 2.2 convolution_add_fusion.4
  193.7 1.5 constant_dynamic-slice_fusion.9
  199.0 2.2 convolution_add_fusion.4
  203.8 18.6 %while.41 = (s32[]{:T(128)}, f32[128,4,192]{0,2,1:T(8,128)}, f32[4,8,128]{2,0,1:T(4,128)S(1)}, bf16[2048,768]{0,1:T(8,128)(2,1)}, bf16[128,4,192]{0,2,1:T(8,128)...) while((s32[]{:T(128)}, f32[128,4,192]{0,2,1:T(8,128)}, ...), condition=%wide.region_6.7_spmd.clone, body=%wide.region_4.6_spmd.clone.sunk | while | flops 316625952 | bytes 15395292 | solution.py:39
  203.8 1.5 constant_dynamic-slice_fusion.10
  207.8 1.5 constant_dynamic-slice_fusion.10
  211.3 1.3 dynamic_update_slice.13
  212.7 1.5 constant_dynamic-slice_fusion.10
  217.6 1.5 constant_dynamic-slice_fusion.10
  224.3 21.1 %all-gather.13.cloned.1.call-done = bf16[1,2048,768]{2,1,0:T(8,128)(2,1)} async-done(((bf16[1,128,768]{2,1,0:T(8,128)(2,1)}), bf16[1,2048,768]{2,1,0:T(8,128)(2,1)}) %all-gather.13.cloned.1.call-update) | async-done | bytes 3145744 | tf_op jit(solution)/shard_map/all_gather | solution.py:151
  245.4 3.2 copy.57
  248.6 24.9 %all_gather.25 = f32[4,2048]{1,0:T(4,128)S(1)} all-gather(f32[4,128]{1,0:T(4,128)S(1)} %copy-done.9), channel_id=1, replica_groups=mesh['dp'=32,'seq'=16] {'seq'}, dimensions={1}, use_global_device_ids=true | all-gather | bytes 34816 | tf_op jit(solution)/shard_map/all_gather | solution.py:145
  273.5 5.2 %fusion.36 = f32[4,2048,128]{2,1,0:T(8,128)} fusion(bf16[2048,4,192]{0,2,1:T(8,128)(2,1)S(1)} %bitcast.154, bf16[128,4,192]{0,2,1:T(8,128)(2,1)} %bitcast.162, f32[4,2048]{1,0:T(4,128)S(1)} %all_gather.25, f32[4,128,128]{2,1,0:T(8,128)} %fusion.47), kind=kOutput, calls=%fused_computation.60 | convolution fusion | flops 405798912 | bytes 7831552 | tf_op jit(solution)/shard_map/qhe,khe->hqk/dot_general | solution.py:156
  278.7 35.1 %all_gather.27 = f32[4,2048]{1,0:T(4,128)S(1)} all-gather(f32[4,128]{1,0:T(4,128)S(1)} %copy-done.7), channel_id=1, replica_groups=mesh['dp'=32,'seq'=16] {'seq'}, dimensions={1}, use_global_device_ids=true | all-gather | bytes 34816 | tf_op jit(solution)/shard_map/all_gather | solution.py:146
  313.8 1.7 fusion.45
  315.7 5.1 %all-gather.15.cloned.1.call-done = bf16[1,2048,768]{2,1,0:T(8,128)(2,1)} async-done(((bf16[1,128,768]{2,1,0:T(8,128)(2,1)}), bf16[1,2048,768]{2,1,0:T(8,128)(2,1)}) %all-gather.15.cloned.1.call-update) | async-done | bytes 3145744 | tf_op jit(solution)/shard_map/all_gather | solution.py:152
  320.7 3.2 copy.60
  323.9 3.8 fusion.42
  327.8 6.5 %fusion.41 = bf16[4,128,192]{1,2,0:T(8,128)(2,1)} fusion(bf16[2048,4,192]{0,2,1:T(8,128)(2,1)} %bitcast.155, f32[4,2048,128]{2,1,0:T(8,128)} %fusion.36, bf16[2048,4,192]{0,2,1:T(8,128)(2,1)S(1)} %bitcast.153, bf16[128,4,192]{0,2,1:T(8,128)(2,1)} %bitcast.161, f32[4,2048]{1,0:T(4,128)S(1)} %all_gather.27), kind=kOutput, calls=%fused_computation.67 | convolution fusion | flops 808648704 | bytes 10911744 | tf_op jit(solution)/shard_map/hqk,qhe->khe/dot_general | solution.py:165
  334.3 1.7 copy.66
  336.0 1.7 copy.67
  337.7 96.6 %psum.7 = f32[128,4]{0,1:T(4,128)} all-reduce(f32[128,4]{0,1:T(4,128)S(1)} %convolution_bitcast_fusion.1), channel_id=1, replica_groups=mesh['dp'=32,'seq'=16] {'dp','seq'}, use_global_device_ids=true, to_apply=%region_7.8 | all-reduce | flops 512 | bytes 4096 | tf_op jit(solution)/shard_map/psum | solution.py:143
  (136 shorter events, 39.9 us)
Async XLA Ops:
  7.2 7.2 %copy-start = (bf16[1,8,128,128]{3,2,1,0:T(8,128)(2,1)S(1)}, bf16[1,8,128,128]{3,2,1,0:T(8,128)(2,1)}, u32[]{:S(2)}) copy-start(bf16[1,8,128,128]{3,2,1,0:T(8,128)(2,1)} %param.14) | copy-start | bytes 786436
  7.2 86.9 %all-gather.9.cloned.1.call-start = ((), (), s32[]{:S(2)}) async-start(), calls=%async_computation | async-start | bytes 3342336 | tf_op jit(solution)/shard_map/all_gather | solution.py:96
  9.0 160.9 %all-gather.11.cloned.1.call-start = ((), (), s32[]{:S(2)}) async-start(), calls=%async_computation.1 | async-start | bytes 3342336 | tf_op jit(solution)/shard_map/all_gather | solution.py:97
  10.8 234.5 %all-gather.13.cloned.1.call-start = ((), (), s32[]{:S(2)}) async-start(), calls=%async_computation.2 | async-start | bytes 3342336 | tf_op jit(solution)/shard_map/all_gather | solution.py:151
  11.6 309.1 %all-gather.15.cloned.1.call-start = ((), (), s32[]{:S(2)}) async-start(), calls=%async_computation.3 | async-start | bytes 3342336 | tf_op jit(solution)/shard_map/all_gather | solution.py:152
  205.6 1.1 copy-start.2
  207.1 0.8 copy-start.3
  209.6 1.1 copy-start.2
  211.1 1.6 copy-start.3
  214.4 1.1 copy-start.2
  215.9 1.6 copy-start.3
  219.3 1.1 copy-start.2
  220.8 1.6 copy-start.3
  222.4 1.9 copy-start.4
  222.4 1.9 copy-start.6
  222.4 1.9 copy-start.8
  245.4 3.2 copy-start.9
  248.6 30.1 %copy-start.1 = (bf16[1,2048,768]{1,2,0:T(8,128)(2,1)}, bf16[1,2048,768]{1,2,0:T(8,128)(2,1)S(1)}, u32[]{:S(2)}) copy-start(bf16[1,2048,768]{1,2,0:T(8,128)(2,1)S(1)} %copy.57) | copy-start | bytes 9437188
  273.5 5.2 %copy-start.7 = (f32[4,128]{1,0:T(4,128)S(1)}, f32[4,128]{1,0:T(4,128)}, u32[]{:S(2)}) copy-start(f32[4,128]{1,0:T(4,128)} %copy-done.6) | copy-start | bytes 6148
  273.5 40.3 %copy-start.5 = (f32[4,8,128]{2,0,1:T(4,128)S(1)}, f32[4,8,128]{2,0,1:T(4,128)}, u32[]{:S(2)}) copy-start(f32[4,8,128]{2,0,1:T(4,128)} %copy-done.4) | copy-start | bytes 49156
  273.5 40.3 %copy-start.10 = (f32[128,4]{0,1:T(4,128)S(1)}, f32[128,4]{0,1:T(4,128)}, u32[]{:S(2)}) copy-start(f32[128,4]{0,1:T(4,128)} %param.15) | copy-start | bytes 6148
Sparse Core Ops, SparseCore 0:
  11.7 82.3 all-gather.8
  97.8 72.1 all-gather.10
  173.2 72.0 all-gather.12
  248.5 72.1 all-gather.14
where the time goes:
time: 442 us; the launch traced here: 441 us
  blocking collectives  195 us (44%)
  waiting for transfers between devices  142 us (32%)
  matrix products  39.3 us (9%)
  local copies, waits for them, and re-layouts  38.7 us (9%)
  between operations  13.9 us (3%)
  other arithmetic  10.8 us (2%)
    psum x1, blocking collectives, body(): grad_weight = lax.psum(weight_term, ('dp', 'seq'))  96.6 us
    all_gather x1, waiting for transfers between devices, body(): lax.all_gather(value_rows, 'seq', axis=0, tiled=True)  75.9 us
    all_gather x1, waiting for transfers between devices, body(): lax.all_gather(key_rows, 'seq', axis=0, tiled=True)  39 us
    all_gather x1, blocking collectives, body(): lax.all_gather(bias_rows, 'seq', axis=1, tiled=True)  38.5 us
    all_gather x1, blocking collectives, body(): lax.all_gather(delta, 'seq', axis=1, tiled=True)  35.1 us
    all_gather x1, blocking collectives, body(): lax.all_gather(lse, 'seq', axis=1, tiled=True)  24.9 us
    all_gather x1, waiting for transfers between devices, body(): qpiece = lax.all_gather(query_rows, 'seq', axis=0, tiled=True)  21.1 us
    dynamic_slice x8, local copies, waits for them, and re-layouts, advance(): lax.dynamic_slice_in_dim(item, start, block, 0)  11.9 us
  transfers between devices with their start and end apart: 4, of which 4 were waited for; matrix products, arithmetic and copies ran while one was open for 16% of the time, Pallas kernels for 0%

commit v1 on v0

v1 whole, which is shorter than its diff:
```python
import functools
import math

import jax
import jax.numpy as jnp
from jax import lax
from jax.experimental import pallas as pl
from jax.experimental.pallas import tpu as pltpu
from jax.sharding import PartitionSpec as P

HEADS = 4
HDIM = 192
TOK = 128
POOL = 16
PROW = TOK // POOL
PAIRS = 128
XS = 4
ZS = 2
CS = 2
QROWS = XS * TOK
KROWS = XS * ZS * CS * TOK
BLOCK = 256
SCALE = HDIM ** (-0.5)
LOG2E = 1.0 / math.log(2.0)
BF = jnp.bfloat16
F32 = jnp.float32
VMEM = pl.BlockSpec(memory_space=pltpu.VMEM)
SMEM = pl.BlockSpec(memory_space=pltpu.SMEM)

FULL_TILE = (0, 2, 3, 5)
HALF_TILE = (1, 1, 4, 4)


def nn(a, b):
    return lax.dot_general(a, b, (((1,), (0,)), ((), ())), preferred_element_type=F32)


def nt(a, b):
    return lax.dot_general(a, b, (((1,), (1,)), ((), ())), preferred_element_type=F32)


def tn(a, b):
    return lax.dot_general(a, b, (((0,), (0,)), ((), ())), preferred_element_type=F32)


def roll_half(x):
    return pltpu.roll(x, 64, 1)


def low_lanes(rows):
    return lax.broadcasted_iota(jnp.int32, (rows, 128), 1) < 64


def split2(x):
    hi = x.astype(BF)
    return hi, (x - hi.astype(F32)).astype(BF)


def split3(x):
    hi = x.astype(BF)
    rest = x - hi.astype(F32)
    mid = rest.astype(BF)
    return hi, mid, (rest - mid.astype(F32)).astype(BF)


def pack_heads(ref):
    low = low_lanes(64)
    for pair in range(2):
        tile = ref[:, (3 * pair + 1) * 128 : (3 * pair + 2) * 128].astype(F32)
        top, bottom = tile[:64], tile[64:]
        even = jnp.where(low, top, roll_half(bottom)).astype(BF)
        odd = jnp.where(low, roll_half(top), bottom).astype(BF)
        for parity, half in ((0, even), (1, odd)):
            head = 2 * pair + parity
            full = FULL_TILE[head]
            yield head, ref[:, full * 128 : (full + 1) * 128], half


def pack_kernel(q_ref, k_ref, v_ref, c_ref, pair_ref, wt_ref, kv_ref, qd_ref):
    for base, ref in ((0, k_ref), (1, v_ref)):
        for head, full, half in pack_heads(ref):
            for zs in range(ZS):
                slot = head * ZS + zs
                kv_ref[slot, base * 128 : (base + 1) * 128, :] = full
                kv_ref[slot, 256 + base * 64 : 320 + base * 64, :] = half
    for base, ref in ((0, q_ref), (1, c_ref)):
        for head, full, half in pack_heads(ref):
            qd_ref[head, base * 128 : (base + 1) * 128, :] = full
            qd_ref[head, 256 + base * 64 : 320 + base * 64, :] = half
    parts = jnp.concatenate([p.astype(F32) for p in split3(wt_ref[...])], axis=0).astype(BF)
    pair = pair_ref[...].reshape(PROW * PAIRS, 128)
    prod = nt(parts, pair)
    bias = (prod[0:8] + (prod[8:16] + prod[16:24])) * (1.0 / SCALE)
    for head in range(HEADS):
        rows = jnp.concatenate(
            [bias[head : head + 1, i * 128 : (i + 1) * 128] for i in range(PROW)], axis=0
        )
        hi = rows.astype(BF).astype(F32)
        qd_ref[head, 384:400, :] = jnp.concatenate([hi, rows - hi], axis=0).astype(BF)


def unpack(full, half, rows_low):
    half = half.astype(F32)
    top = jnp.where(rows_low, half, 0.0)
    bottom = jnp.where(rows_low, roll_half(half), 0.0)
    other = jnp.concatenate([top, bottom], axis=0).astype(BF)
    return full, other


def pack_out(block):
    rest = block[:, 128:]
    return block[:, :128].astype(BF), (rest[:64] + roll_half(rest[64:])).astype(BF)


def attn_kernel(
    core_ref, qd_ref, kvo_ref, kvx_ref, oq_ref, dko_ref, dkx_ref,
    ke, vs, qe, cs, st, ot, dqt, pool,
):
    core = core_ref[0]
    low = low_lanes(64)
    for half, ref in ((0, kvo_ref), (1, kvx_ref)):
        for m in range(8):
            base = half * 1024 + m * 128
            full, other = unpack(ref[m, 0:128, :], ref[m, 256:320, :], low)
            ke[base : base + 128, 0:128] = full
            ke[base : base + 128, 128:256] = other
            full, other = unpack(ref[m, 128:256, :], ref[m, 320:384, :], low)
            vs[base : base + 128, 0:128] = full
            vs[base : base + 128, 128:256] = other
        row = lax.broadcasted_iota(jnp.int32, (1024, 128), 0)
        col = lax.broadcasted_iota(jnp.int32, (1024, 128), 1)
        mine = core if half == 0 else 1 - core
        cell = lax.shift_right_logical(row, 7) * 16 + mine * 8 + (lax.shift_right_logical(row, 4) & 7)
        table = jnp.where(cell == col, 1.0, 0.0).astype(BF)
        ke[half * 1024 : (half + 1) * 1024, 256:384] = table
        ke[half * 1024 : (half + 1) * 1024, 384:512] = table
    for x in range(XS):
        base = x * 128
        full, other = unpack(qd_ref[x, 0:128, :], qd_ref[x, 256:320, :], low)
        qe[base : base + 128, 0:128] = full
        qe[base : base + 128, 128:256] = other
        full, other = unpack(qd_ref[x, 128:256, :], qd_ref[x, 320:384, :], low)
        cs[base : base + 128, 0:128] = full
        cs[base : base + 128, 128:256] = other
        rows = qd_ref[x, 384:400, :].astype(F32)
        for part in range(2):
            wide = jnp.broadcast_to(rows[part * 8 : part * 8 + 8, None, :], (8, POOL, 128))
            qe[base : base + 128, 256 + part * 128 : 384 + part * 128] = wide.reshape(128, 128).astype(BF)

    steps = KROWS // BLOCK

    def scores(b, top):
        at = pl.ds(pl.multiple_of(b * BLOCK, BLOCK), BLOCK)
        s = nt(ke[at, :], qe[...])
        st[at, :] = s
        return jnp.maximum(top, jnp.max(s.reshape(BLOCK // 8, 8, QROWS), axis=0))

    top = lax.fori_loop(0, steps, scores, jnp.full((8, QROWS), -jnp.inf, F32))
    top = jnp.max(top, axis=0, keepdims=True) * (SCALE * LOG2E)
    ot[...] = jnp.zeros_like(ot)

    def weigh(b, total):
        at = pl.ds(pl.multiple_of(b * BLOCK, BLOCK), BLOCK)
        w = jnp.exp2(st[at, :] * (SCALE * LOG2E) - top)
        st[at, :] = w
        ot[...] += tn(vs[at, :], w.astype(BF))
        return total + jnp.sum(w.reshape(BLOCK // 8, 8, QROWS), axis=0)

    total = lax.fori_loop(0, steps, weigh, jnp.zeros((8, QROWS), F32))
    inv = 1.0 / jnp.sum(total, axis=0, keepdims=True)
    att = (ot[...] * inv).astype(BF).astype(F32)
    cot_t = cs[...].astype(F32).T
    delta = jnp.sum(att * cot_t, axis=0, keepdims=True)
    att = att.T
    dqt[...] = jnp.zeros_like(dqt)

    for half, ref in ((0, dko_ref), (1, dkx_ref)):
        mine = core if half == 0 else 1 - core

        def back(b, carry):
            at = pl.ds(pl.multiple_of(half * 1024 + b * BLOCK, BLOCK), BLOCK)
            prob = st[at, :] * inv
            dv = nn(prob.astype(BF), cs[...])
            dprod = nt(vs[at, :], cs[...])
            ds = prob * (dprod - delta)
            low_ds = ds.astype(BF)
            dk = nn(low_ds, qe[:, 0:256]) * SCALE
            dqt[...] += tn(ke[at, 0:256], low_ds)
            pooled = jnp.sum(ds.reshape(BLOCK // POOL, POOL, QROWS), axis=1)
            for t in range(BLOCK // 128):
                m = b * (BLOCK // 128) + t
                full, rest = pack_out(dk[t * 128 : (t + 1) * 128])
                ref[m, 0:128, :] = full
                ref[m, 256:320, :] = rest
                full, rest = pack_out(dv[t * 128 : (t + 1) * 128])
                ref[m, 128:256, :] = full
                ref[m, 320:384, :] = rest
                pool[pl.ds(pl.multiple_of(m * 16 + mine * 8, 8), 8), :] = pooled[t * 8 : t * 8 + 8]
            return carry

        lax.fori_loop(0, 1024 // BLOCK, back, 0)

    row = lax.broadcasted_iota(jnp.int32, (QROWS // POOL, QROWS), 0)
    col = lax.broadcasted_iota(jnp.int32, (QROWS // POOL, QROWS), 1)
    pick = jnp.where(row == lax.shift_right_logical(col, 4), 1.0, 0.0).astype(BF)
    hi, lo = split2(pool[...])
    grad_bias = nt(pick, hi) + nt(pick, lo)
    dq = dqt[...].T * SCALE
    for x in range(XS):
        at = slice(x * 128, (x + 1) * 128)
        full, rest = pack_out(att[at])
        oq_ref[x, 0:128, :] = full
        oq_ref[x, 256:320, :] = rest
        full, rest = pack_out(dq[at])
        oq_ref[x, 128:256, :] = full
        oq_ref[x, 320:384, :] = rest
        rows = grad_bias[x * 8 : x * 8 + 8]
        hi = rows.astype(BF).astype(F32)
        oq_ref[x, 384:400, :] = jnp.concatenate([hi, rows - hi], axis=0).astype(BF)


def weight_kernel(oq_ref, pair_ref, out_ref):
    rows = []
    for part in range(2):
        for head in range(HEADS):
            block = oq_ref[head, 384:400, :].astype(F32)[part * 8 : part * 8 + 8]
            rows.append(jnp.concatenate([block[i : i + 1] for i in range(PROW)], axis=1))
    grads = jnp.concatenate(rows, axis=0).astype(BF)
    pair = pair_ref[...].reshape(PROW * PAIRS, 128)
    prod = nn(grads, pair)
    out_ref[...] = prod[0:4] + prod[4:8]


def final_kernel(oq_ref, dkv_ref, wt_ref, att_ref, dq_ref, dk_ref, dv_ref, gp_ref):
    low = low_lanes(64)

    def put(ref, fulls, halves):
        for pair in range(2):
            even, odd = halves[2 * pair], halves[2 * pair + 1]
            mid = jnp.concatenate(
                [jnp.where(low, even, roll_half(odd)), jnp.where(low, roll_half(even), odd)], axis=0
            )
            ref[:, (3 * pair) * 128 : (3 * pair + 1) * 128] = fulls[2 * pair].astype(BF)
            ref[:, (3 * pair + 1) * 128 : (3 * pair + 2) * 128] = mid.astype(BF)
            ref[:, (3 * pair + 2) * 128 : (3 * pair + 3) * 128] = fulls[2 * pair + 1].astype(BF)

    for base, ref in ((0, att_ref), (1, dq_ref)):
        put(
            ref,
            [oq_ref[h, base * 128 : (base + 1) * 128, :] for h in range(HEADS)],
            [oq_ref[h, 256 + base * 64 : 320 + base * 64, :].astype(F32) for h in range(HEADS)],
        )

    def both(h, rows):
        return dkv_ref[h * ZS, rows, :].astype(F32) + dkv_ref[h * ZS + 1, rows, :].astype(F32)

    for base, ref in ((0, dk_ref), (1, dv_ref)):
        put(
            ref,
            [both(h, slice(base * 128, (base + 1) * 128)) for h in range(HEADS)],
            [both(h, slice(256 + base * 64, 320 + base * 64)) for h in range(HEADS)],
        )
    whi, wmid, _ = split3(wt_ref[...])
    blocks = [oq_ref[h, 384:400, :].astype(F32) for h in range(HEADS)]
    wrows = jnp.concatenate([whi.astype(F32), wmid.astype(F32), whi.astype(F32)], axis=0)
    wrows = jnp.concatenate([wrows, jnp.zeros((8, 128), F32)], axis=0).astype(BF)
    zero = jnp.zeros((4, 128), F32)
    for i in range(PROW):
        hi = jnp.concatenate([b[i : i + 1] for b in blocks] + [zero], axis=0)
        lo = jnp.concatenate([b[8 + i : 9 + i] for b in blocks] + [zero], axis=0)
        grads = jnp.concatenate([hi, hi, lo, jnp.zeros((8, 128), F32)], axis=0)
        gp_ref[i] = nn(grads.T.astype(BF), wrows).astype(BF)


def shape(*dims, dtype=BF):
    return jax.ShapeDtypeStruct(dims, dtype)


def call(kernel, out_shape, args, scratch=(), flops=0, moved=0, smem=0, limit=32):
    single = not isinstance(out_shape, tuple)
    return pl.pallas_call(
        kernel,
        out_shape=out_shape,
        in_specs=[SMEM] * smem + [VMEM] * (len(args) - smem),
        out_specs=VMEM if single else (VMEM,) * len(out_shape),
        scratch_shapes=list(scratch),
        cost_estimate=pl.CostEstimate(flops=flops, bytes_accessed=moved, transcendentals=0),
        compiler_params=pltpu.CompilerParams(vmem_limit_bytes=limit * 1024 * 1024),
    )(*args)


def seq_index(x, z, c):
    return (x * ZS + z) * CS + c


def body(dp, queries, keys, values, cotangent, pair, pair_weight):
    x_groups = [[seq_index(x, z, c) for x in range(XS)] for z in range(ZS) for c in range(CS)]
    xz_groups = [[seq_index(x, z, c) for x in range(XS) for z in range(ZS)] for c in range(CS)]
    xc_groups = [[seq_index(x, z, c) for x in range(XS) for c in range(CS)] for z in range(ZS)]
    far_groups = [
        [d * 16 + seq_index(x, z, c) for d in range(dp) for z in range(ZS)]
        for x in range(XS)
        for c in range(CS)
    ]
    swap = [(s, s ^ 1) for s in range(16)]

    def exchange(array, groups, axis="seq"):
        return lax.all_to_all(array, axis, 0, 0, axis_index_groups=groups)

    core = (lax.axis_index("seq") % CS).astype(jnp.int32).reshape(1)
    pair_rows = pair[0]
    wt = jnp.concatenate([pair_weight.T, jnp.zeros((4, 128), F32)], axis=0)
    kv, qd = call(
        pack_kernel,
        (shape(8, 384, 128), shape(4, 400, 128)),
        (queries[0], keys[0], values[0], cotangent[0], pair_rows, wt),
        flops=2 * 24 * 1024 * 128,
        moved=3_000_000,
    )
    kv_own = exchange(kv, xz_groups)
    qd_own = exchange(qd, x_groups)
    kv_other = lax.ppermute(kv_own, "seq", swap)
    oq, dkv_own, dkv_other = call(
        attn_kernel,
        (shape(4, 400, 128), shape(8, 384, 128), shape(8, 384, 128)),
        (core, qd_own, kv_own, kv_other),
        scratch=(
            pltpu.VMEM((KROWS, 512), BF),
            pltpu.VMEM((KROWS, 256), BF),
            pltpu.VMEM((QROWS, 512), BF),
            pltpu.VMEM((QROWS, 256), BF),
            pltpu.VMEM((KROWS, QROWS), F32),
            pltpu.VMEM((256, QROWS), F32),
            pltpu.VMEM((256, QROWS), F32),
            pltpu.VMEM((PAIRS, QROWS), F32),
        ),
        flops=8 * 2 * QROWS * KROWS * 256,
        moved=5_000_000,
        smem=1,
        limit=40,
    )
    dkv_swapped = lax.ppermute(dkv_other, "seq", swap)
    dkv = (dkv_own.astype(F32) + dkv_swapped.astype(F32)).astype(BF)
    dkv_back = exchange(dkv, xz_groups)
    oq_back = exchange(oq, x_groups)
    term = call(
        weight_kernel, shape(4, 128, dtype=F32), (oq_back, pair_rows), flops=2 * 1024 * 128 * 8, moved=300_000
    )
    near = exchange(jnp.broadcast_to(term[None], (8, 4, 128)), xc_groups).sum(axis=0)
    count = dp * ZS
    far = exchange(jnp.broadcast_to(near[None], (count, 4, 128)), far_groups, ("dp", "seq"))
    grad_weight = far.sum(axis=0).T
    att, dq, dk, dv, gp = call(
        final_kernel,
        (shape(128, 768),) * 4 + (shape(PROW, PAIRS, 128),),
        (oq_back, dkv_back, wt),
        flops=2 * 1024 * 128 * 32,
        moved=3_000_000,
    )
    return att[None], dq[None], dk[None], dv[None], gp[None], grad_weight


def solution(mesh):
    rows = P("dp", "seq", None)
    cells = P("dp", "seq", None, None)
    return jax.shard_map(
        functools.partial(body, mesh.shape["dp"]),
        mesh=mesh,
        in_specs=(rows, rows, rows, rows, cells, P()),
        out_specs=(rows, rows, rows, rows, cells, P()),
        check_vma=False,
    )
```

time: 442 us -> 143 us (0.32)
  the two profiles are of different devices: /device:TPU:1 before, /device:TPU:64 now
where the time goes in v1:
time: 143 us
  blocking collectives  56.1 us (39%)
  waiting for transfers between devices  43.4 us (30%)
  starting transfers between devices  21 us (15%)
  Pallas kernels  13.8 us (10%)
  local copies, waits for them, and re-layouts  6.03 us (4%)
  other arithmetic  1.77 us (1%)
    all_to_all x3, blocking collectives, exchange(): return lax.all_to_all(array, axis, 0, 0, axis_index_groups=groups)  56.1 us
    all_to_all x3, waiting for transfers between devices, exchange(): return lax.all_to_all(array, axis, 0, 0, axis_index_groups=groups)  43.4 us
    all_to_all x3, starting transfers between devices, exchange(): return lax.all_to_all(array, axis, 0, 0, axis_index_groups=groups)  17 us
    pallas_call x4, Pallas kernels, call(): pl.pallas_call(kernel, out_shape=out_shape, in_specs=[SMEM] * smem + [VME...  13.8 us
    unnamed x12, local copies, waits for them, and re-layouts  4.66 us
  transfers between devices with their start and end apart: 5, of which 3 were waited for; matrix products, arithmetic and copies ran while one was open for 2% of the time, Pallas kernels for 0%

profile of v1, /device:TPU:64, one launch (start us, length us, event | category | flops | bytes accessed | tf_op | source)
XLA Modules:
  0.0 142.8 jit_solution(6601340390750517324)
XLA Ops:
  0.6 0.7 concatenate.3.wt_ref
  1.3 0.0 copy-start
  1.3 0.9 copy-done
  2.3 0.0 copy-start.2
  2.3 0.9 copy-done.2
  3.2 0.0 copy-start.3
  3.2 0.9 copy-done.3
  4.1 0.0 copy-start.4
  4.1 0.9 copy-done.4
  5.1 0.0 copy-start.5
  5.1 0.9 copy-done.5
  6.0 1.0 shard_map.109
  7.0 36.9 %all_to_all.30.kvo_ref = bf16[8,384,128]{2,1,0:T(8,128)(2,1)S(1)} all-to-all(bf16[8,384,128]{2,1,0:T(8,128)(2,1)S(1)} %get-tuple-element.17), channel_id=1, replica_groups={{0,2,4,6,8,10,12,14},{1,3,5,7,9,11,13,15},{16,18,20,22,24,26,28,30},{17..., dimensions={0} | all-to-all | bytes 1572864 | tf_op jit(solution)/shard_map/all_to_all | solution.py:308
  43.9 1.9 %collective-permute-start = (bf16[8,384,128]{2,1,0:T(8,128)(2,1)S(1)}, bf16[8,384,128]{2,1,0:T(8,128)(2,1)S(1)}, u32[]{:S(2)}, u32[]{:S(2)}) collective-permute-start(bf16[8,384,128]{2,1,0:T(8,128)(2,1)S(1)} %all_to_all.30.kvo_ref), channel_id=1, source_target_pairs={{0,1},{1,0},{2,3},{3,2},{4,5},{5,4},{6,7},{7,6},{8,9},{9,8},{10,11... | collective-permute-start | bytes 2359304 | tf_op jit(solution)/shard_map/ppermute | solution.py:322
  45.8 3.5 %all-to-all-start = ((bf16[4,400,128]{2,1,0:T(8,128)(2,1)}), bf16[4,400,128]{2,1,0:T(8,128)(2,1)S(1)}, u32[]{:S(2)}, u32[]{:S(2)}) async-start(bf16[4,400,128]{2,1,0:T(8,128)(2,1)} %get-tuple-element.16), calls=%async_computation | async-start | bytes 819200 | tf_op jit(solution)/shard_map/all_to_all | solution.py:308
  49.3 9.1 %all-to-all-done.qd_ref = bf16[4,400,128]{2,1,0:T(8,128)(2,1)S(1)} async-done(((bf16[4,400,128]{2,1,0:T(8,128)(2,1)}), bf16[4,400,128]{2,1,0:T(8,128)(2,1)S(1)}, u32[]{:S(2)}, u32[]{:S(2)}) %all-to-all-start) | async-done | bytes 409632 | tf_op jit(solution)/shard_map/all_to_all | solution.py:308
  58.4 0.0 collective-permute-done.kvx_ref
  58.4 11.4 %shard_map.110 = (bf16[4,400,128]{2,1,0:T(8,128)(2,1)S(1)}, bf16[8,384,128]{2,1,0:T(8,128)(2,1)S(1)}, bf16[8,384,128]{2,1,0:T(8,128)(2,1)}) custom-call(s32[1]{0:T(128)} %bitcast.core_ref, bf16[4,400,128]{2,1,0:T(8,128)(2,1)S(1)} %all-to-all-done.qd_ref, bf16[8,384,128]{2,1,0:T(8,128)(2,1)S(1)} %all_to_all.30.kvo_ref, ...), custom_call_target="tpu_custom_call" | custom-call | flops 4294967296 | bytes 5000000 | tf_op jit(solution)/shard_map/pallas_call | solution.py:281
  69.9 2.0 %collective-permute-start.1 = (bf16[8,384,128]{2,1,0:T(8,128)(2,1)}, bf16[8,384,128]{2,1,0:T(8,128)(2,1)S(1)}, u32[]{:S(2)}, u32[]{:S(2)}) collective-permute-start(bf16[8,384,128]{2,1,0:T(8,128)(2,1)} %get-tuple-element.20), channel_id=1, source_target_pairs={{0,1},{1,0},{2,3},{3,2},{4,5},{5,4},{6,7},{7,6},{8,9},{9,8},{10,11... | collective-permute-start | bytes 2359304 | tf_op jit(solution)/shard_map/ppermute | solution.py:342
  71.9 11.6 %all_to_all.31.oq_ref = bf16[4,400,128]{2,1,0:T(8,128)(2,1)S(1)} all-to-all(bf16[4,400,128]{2,1,0:T(8,128)(2,1)S(1)} %get-tuple-element.18), channel_id=1, replica_groups={{0,4,8,12},{1,5,9,13},{2,6,10,14},{3,7,11,15},{16,20,24,28},{17,21,25,2..., dimensions={0} | all-to-all | bytes 819200 | tf_op jit(solution)/shard_map/all_to_all | solution.py:308
  83.5 0.0 copy-done.1
  83.5 0.1 shard_map.112
  83.6 7.7 %all_to_all.32 = f32[8,4,128]{2,1,0:T(4,128)S(1)} all-to-all(f32[8,4,128]{2,1,0:T(4,128)S(1)} %broadcast_in_dim.33), channel_id=1, replica_groups={{0,1,4,5,8,9,12,13},{2,3,6,7,10,11,14,15},{16,17,20,21,24,25,28,29},{18..., dimensions={0} | all-to-all | bytes 32768 | tf_op jit(solution)/shard_map/all_to_all | solution.py:308
  91.4 0.7 broadcast_in_dim.34
  92.0 10.0 %all-to-all-start.5 = ((f32[64,4,128]{2,1,0:T(4,128)}), f32[64,4,128]{2,1,0:T(4,128)S(1)}, u32[]{:S(2)}, u32[]{:S(2)}) async-start(f32[64,4,128]{2,1,0:T(4,128)} %broadcast_in_dim.34), calls=%async_computation.5 | async-start | bytes 262144 | tf_op jit(solution)/shard_map/all_to_all | solution.py:308
  102.0 0.0 collective-permute-done.1
  102.1 1.1 add_convert_fusion
  103.2 10.9 %all-to-all-done.5 = f32[64,4,128]{2,1,0:T(4,128)S(1)} async-done(((f32[64,4,128]{2,1,0:T(4,128)}), f32[64,4,128]{2,1,0:T(4,128)S(1)}, u32[]{:S(2)}, u32[]{:S(2)}) %all-to-all-start.5) | async-done | bytes 131104 | tf_op jit(solution)/shard_map/all_to_all | solution.py:308
  114.1 3.5 %all-to-all-start.3 = ((bf16[8,384,128]{2,1,0:T(8,128)(2,1)}), bf16[8,384,128]{2,1,0:T(8,128)(2,1)S(1)}, u32[]{:S(2)}, u32[]{:S(2)}) async-start(bf16[8,384,128]{2,1,0:T(8,128)(2,1)} %add_convert_fusion), calls=%async_computation.3 | async-start | bytes 1572864 | tf_op jit(solution)/shard_map/all_to_all | solution.py:308
  117.7 0.7 reduce_sum.19
  118.3 23.3 %all-to-all-done.3.dkv_ref = bf16[8,384,128]{2,1,0:T(8,128)(2,1)S(1)} async-done(((bf16[8,384,128]{2,1,0:T(8,128)(2,1)}), bf16[8,384,128]{2,1,0:T(8,128)(2,1)S(1)}, u32[]{:S(2)}, u32[]{:S(2)}) %all-to-all-start.3) | async-done | bytes 786464 | tf_op jit(solution)/shard_map/all_to_all | solution.py:308
  141.6 1.2 shard_map.111
  (3 shorter events, 0.0 us)
Async XLA Ops:
  1.3 0.9 copy-start
  2.3 0.9 copy-start.2
  3.2 0.9 copy-start.3
  4.1 0.9 copy-start.4
  5.1 0.9 copy-start.5
  43.9 14.6 %collective-permute-start = (bf16[8,384,128]{2,1,0:T(8,128)(2,1)S(1)}, bf16[8,384,128]{2,1,0:T(8,128)(2,1)S(1)}, u32[]{:S(2)}, u32[]{:S(2)}) collective-permute-start(bf16[8,384,128]{2,1,0:T(8,128)(2,1)S(1)} %all_to_all.30.kvo_ref), channel_id=1, source_target_pairs={{0,1},{1,0},{2,3},{3,2},{4,5},{5,4},{6,7},{7,6},{8,9},{9,8},{10,11... | collective-permute-start | bytes 2359304 | tf_op jit(solution)/shard_map/ppermute | solution.py:322
  45.8 12.6 %all-to-all-start = ((bf16[4,400,128]{2,1,0:T(8,128)(2,1)}), bf16[4,400,128]{2,1,0:T(8,128)(2,1)S(1)}, u32[]{:S(2)}, u32[]{:S(2)}) async-start(bf16[4,400,128]{2,1,0:T(8,128)(2,1)} %get-tuple-element.16), calls=%async_computation | async-start | bytes 819200 | tf_op jit(solution)/shard_map/all_to_all | solution.py:308
  69.9 13.6 %copy-start.1 = (bf16[1,8,128,128]{3,2,1,0:T(8,128)(2,1)S(1)}, bf16[1,8,128,128]{3,2,1,0:T(8,128)(2,1)}, u32[]{:S(2)}) copy-start(bf16[1,8,128,128]{3,2,1,0:T(8,128)(2,1)} %param.10) | copy-start | bytes 786436
  69.9 32.2 %collective-permute-start.1 = (bf16[8,384,128]{2,1,0:T(8,128)(2,1)}, bf16[8,384,128]{2,1,0:T(8,128)(2,1)S(1)}, u32[]{:S(2)}, u32[]{:S(2)}) collective-permute-start(bf16[8,384,128]{2,1,0:T(8,128)(2,1)} %get-tuple-element.20), channel_id=1, source_target_pairs={{0,1},{1,0},{2,3},{3,2},{4,5},{5,4},{6,7},{7,6},{8,9},{9,8},{10,11... | collective-permute-start | bytes 2359304 | tf_op jit(solution)/shard_map/ppermute | solution.py:342
  92.0 22.1 %all-to-all-start.5 = ((f32[64,4,128]{2,1,0:T(4,128)}), f32[64,4,128]{2,1,0:T(4,128)S(1)}, u32[]{:S(2)}, u32[]{:S(2)}) async-start(f32[64,4,128]{2,1,0:T(4,128)} %broadcast_in_dim.34), calls=%async_computation.5 | async-start | bytes 262144 | tf_op jit(solution)/shard_map/all_to_all | solution.py:308
  114.1 27.5 %all-to-all-start.3 = ((bf16[8,384,128]{2,1,0:T(8,128)(2,1)}), bf16[8,384,128]{2,1,0:T(8,128)(2,1)S(1)}, u32[]{:S(2)}, u32[]{:S(2)}) async-start(bf16[8,384,128]{2,1,0:T(8,128)(2,1)} %add_convert_fusion), calls=%async_computation.3 | async-start | bytes 1572864 | tf_op jit(solution)/shard_map/all_to_all | solution.py:308

commit v2 on v1

v2 whole, which is shorter than its diff:
```python
import functools
import math

import jax
import jax.numpy as jnp
from jax import lax
from jax.experimental import pallas as pl
from jax.experimental.pallas import tpu as pltpu
from jax.sharding import PartitionSpec as P

HEADS = 4
HDIM = 192
TOK = 128
POOL = 16
PROW = TOK // POOL
PAIRS = 128
XS = 4
ZS = 2
CS = 2
QROWS = XS * TOK
KROWS = XS * ZS * CS * TOK
BLOCK = 256
SCALE = HDIM ** (-0.5)
LOG2E = 1.0 / math.log(2.0)
BF = jnp.bfloat16
F32 = jnp.float32
VMEM = pl.BlockSpec(memory_space=pltpu.VMEM)
SMEM = pl.BlockSpec(memory_space=pltpu.SMEM)
ANY = pl.BlockSpec(memory_space=pl.ANY)

FULL_TILE = (0, 2, 3, 5)
HALF_TILE = (1, 1, 4, 4)


def nn(a, b):
    return lax.dot_general(a, b, (((1,), (0,)), ((), ())), preferred_element_type=F32)


def nt(a, b):
    return lax.dot_general(a, b, (((1,), (1,)), ((), ())), preferred_element_type=F32)


def tn(a, b):
    return lax.dot_general(a, b, (((0,), (0,)), ((), ())), preferred_element_type=F32)


def roll_half(x):
    return pltpu.roll(x, 64, 1)


def low_lanes(rows):
    return lax.broadcasted_iota(jnp.int32, (rows, 128), 1) < 64


def split2(x):
    hi = x.astype(BF)
    return hi, (x - hi.astype(F32)).astype(BF)


def split3(x):
    hi = x.astype(BF)
    rest = x - hi.astype(F32)
    mid = rest.astype(BF)
    return hi, mid, (rest - mid.astype(F32)).astype(BF)


def pack_heads(ref):
    low = low_lanes(64)
    for pair in range(2):
        tile = ref[:, (3 * pair + 1) * 128 : (3 * pair + 2) * 128].astype(F32)
        top, bottom = tile[:64], tile[64:]
        even = jnp.where(low, top, roll_half(bottom)).astype(BF)
        odd = jnp.where(low, roll_half(top), bottom).astype(BF)
        for parity, half in ((0, even), (1, odd)):
            head = 2 * pair + parity
            full = FULL_TILE[head]
            yield head, ref[:, full * 128 : (full + 1) * 128], half


def pack_kv_kernel(k_hbm, v_hbm, kv_ref, k_vmem, v_vmem, sems):
    copies = [
        pltpu.make_async_copy(k_hbm, k_vmem, sems.at[0]),
        pltpu.make_async_copy(v_hbm, v_vmem, sems.at[1]),
    ]
    for copy in copies:
        copy.start()
    for base, copy, ref in ((0, copies[0], k_vmem), (1, copies[1], v_vmem)):
        copy.wait()
        for head, full, half in pack_heads(ref):
            for zs in range(ZS):
                slot = head * ZS + zs
                kv_ref[slot, base * 128 : (base + 1) * 128, :] = full
                kv_ref[slot, 256 + base * 64 : 320 + base * 64, :] = half


def pack_qd_kernel(
    x_ref, q_hbm, c_hbm, pair_hbm, w_hbm, out0, out1, out2, out3,
    q_vmem, c_vmem, pair_vmem, w_vmem, staged, sems,
):
    copies = [
        pltpu.make_async_copy(q_hbm, q_vmem, sems.at[0]),
        pltpu.make_async_copy(c_hbm, c_vmem, sems.at[1]),
        pltpu.make_async_copy(w_hbm, w_vmem, sems.at[2]),
        pltpu.make_async_copy(pair_hbm, pair_vmem, sems.at[3]),
    ]
    for copy in copies:
        copy.start()
    for base, copy, ref in ((0, copies[0], q_vmem), (1, copies[1], c_vmem)):
        copy.wait()
        for head, full, half in pack_heads(ref):
            staged[head, base * 128 : (base + 1) * 128, :] = full
            staged[head, 256 + base * 64 : 320 + base * 64, :] = half
    copies[2].wait()
    copies[3].wait()
    wt = weight_rows(w_vmem[...])
    parts = jnp.concatenate([p.astype(F32) for p in split3(wt)], axis=0).astype(BF)
    pair = pair_vmem[...].reshape(PROW * PAIRS, 128)
    prod = nt(parts, pair)
    bias = (prod[0:8] + (prod[8:16] + prod[16:24])) * (1.0 / SCALE)
    for head in range(HEADS):
        rows = jnp.concatenate(
            [bias[head : head + 1, i * 128 : (i + 1) * 128] for i in range(PROW)], axis=0
        )
        hi = rows.astype(BF).astype(F32)
        staged[head, 384:400, :] = jnp.concatenate([hi, rows - hi], axis=0).astype(BF)
    x = x_ref[0]
    for k, out in enumerate((out0, out1, out2, out3)):
        out[...] = staged[lax.rem(x + k, XS)]


def weight_rows(weight):
    return jnp.concatenate([weight, jnp.zeros((4, 128), F32)], axis=0)


def unpack(full, half, rows_low):
    half = half.astype(F32)
    top = jnp.where(rows_low, half, 0.0)
    bottom = jnp.where(rows_low, roll_half(half), 0.0)
    other = jnp.concatenate([top, bottom], axis=0).astype(BF)
    return full, other


def pack_out(block):
    rest = block[:, 128:]
    return block[:, :128].astype(BF), (rest[:64] + roll_half(rest[64:])).astype(BF)


def scores_kernel(
    core_ref, qd0, qd1, qd2, qd3, kv_own, kv_other, pb, dsb, ke, qe, cs, att_ref, gb_ref,
    vs, st, ot, pool,
):
    low = low_lanes(64)
    core = core_ref[0]
    for half, kv_ref in enumerate((kv_own, kv_other)):
        mine = core if half == 0 else 1 - core
        for m in range(8):
            base = half * 1024 + m * 128
            full, other = unpack(kv_ref[m, 0:128, :], kv_ref[m, 256:320, :], low)
            ke[base : base + 128, 0:128] = full
            ke[base : base + 128, 128:256] = other
            full, other = unpack(kv_ref[m, 128:256, :], kv_ref[m, 320:384, :], low)
            vs[base : base + 128, 0:128] = full
            vs[base : base + 128, 128:256] = other
        row = lax.broadcasted_iota(jnp.int32, (1024, 128), 0)
        col = lax.broadcasted_iota(jnp.int32, (1024, 128), 1)
        cell = lax.shift_right_logical(row, 7) * 16 + mine * 8 + (lax.shift_right_logical(row, 4) & 7)
        table = jnp.where(cell == col, 1.0, 0.0).astype(BF)
        ke[half * 1024 : (half + 1) * 1024, 256:384] = table
        ke[half * 1024 : (half + 1) * 1024, 384:512] = table
    for k, qd_ref in enumerate((qd0, qd1, qd2, qd3)):
        base = k * 128
        full, other = unpack(qd_ref[0:128, :], qd_ref[256:320, :], low)
        qe[base : base + 128, 0:128] = full
        qe[base : base + 128, 128:256] = other
        full, other = unpack(qd_ref[128:256, :], qd_ref[320:384, :], low)
        cs[base : base + 128, 0:128] = full
        cs[base : base + 128, 128:256] = other
        rows = qd_ref[384:400, :].astype(F32)
        for part in range(2):
            wide = jnp.broadcast_to(rows[part * 8 : part * 8 + 8, None, :], (8, POOL, 128))
            qe[base : base + 128, 256 + part * 128 : 384 + part * 128] = wide.reshape(128, 128).astype(BF)

    steps = KROWS // BLOCK

    def scores(b, top):
        at = pl.ds(pl.multiple_of(b * BLOCK, BLOCK), BLOCK)
        s = nt(ke[at, :], qe[...])
        st[at, :] = s
        return jnp.maximum(top, jnp.max(s.reshape(BLOCK // 8, 8, QROWS), axis=0))

    top = lax.fori_loop(0, steps, scores, jnp.full((8, QROWS), -jnp.inf, F32))
    top = jnp.max(top, axis=0, keepdims=True) * (SCALE * LOG2E)
    ot[...] = jnp.zeros_like(ot)

    def weigh(b, total):
        at = pl.ds(pl.multiple_of(b * BLOCK, BLOCK), BLOCK)
        w = jnp.exp2(st[at, :] * (SCALE * LOG2E) - top)
        st[at, :] = w
        ot[...] += tn(vs[at, :], w.astype(BF))
        return total + jnp.sum(w.reshape(BLOCK // 8, 8, QROWS), axis=0)

    total = lax.fori_loop(0, steps, weigh, jnp.zeros((8, QROWS), F32))
    inv = 1.0 / jnp.sum(total, axis=0, keepdims=True)
    att = (ot[...] * inv).astype(BF).astype(F32)
    delta = jnp.sum(att * cs[...].astype(F32).T, axis=0, keepdims=True)
    att_ref[...] = att.T.astype(BF)

    for half in range(CS):
        mine = core if half == 0 else 1 - core

        def back(b, carry):
            at = pl.ds(pl.multiple_of(half * 1024 + b * BLOCK, BLOCK), BLOCK)
            prob = st[at, :] * inv
            pb[at, :] = prob.astype(BF)
            ds = prob * (nt(vs[at, :], cs[...]) - delta)
            dsb[at, :] = ds.astype(BF)
            pooled = jnp.sum(ds.reshape(BLOCK // POOL, POOL, QROWS), axis=1)
            for t in range(BLOCK // 128):
                m = b * (BLOCK // 128) + t
                pool[pl.ds(pl.multiple_of(m * 16 + mine * 8, 8), 8), :] = pooled[t * 8 : t * 8 + 8]
            return carry

        lax.fori_loop(0, 1024 // BLOCK, back, 0)

    row = lax.broadcasted_iota(jnp.int32, (QROWS // POOL, QROWS), 0)
    col = lax.broadcasted_iota(jnp.int32, (QROWS // POOL, QROWS), 1)
    pick = jnp.where(row == lax.shift_right_logical(col, 4), 1.0, 0.0).astype(BF)
    hi, lo = split2(pool[...])
    grad_bias = nt(pick, hi) + nt(pick, lo)
    gb_ref[...] = grad_bias


def weight_kernel(oq_ref, pair_ref, out_ref):
    rows = []
    for part in range(2):
        for head in range(HEADS):
            block = oq_ref[head, 384:400, :].astype(F32)[part * 8 : part * 8 + 8]
            rows.append(jnp.concatenate([block[i : i + 1] for i in range(PROW)], axis=1))
    prod = nn(jnp.concatenate(rows, axis=0).astype(BF), pair_ref[...].reshape(PROW * PAIRS, 128))
    out_ref[...] = prod[0:4] + prod[4:8]


def grads_kernel(
    x_ref, pb, dsb, ke, qe, cs, att_ref, gb_ref, dko_ref, dkx_ref, oq_ref, dqt
):
    dqt[...] = jnp.zeros_like(dqt)
    for half, ref in ((1, dkx_ref), (0, dko_ref)):

        def back(b, carry):
            at = pl.ds(pl.multiple_of(half * 1024 + b * BLOCK, BLOCK), BLOCK)
            low_ds = dsb[at, :]
            dv = nn(pb[at, :], cs[...])
            dk = nn(low_ds, qe[:, 0:256]) * SCALE
            dqt[...] += tn(ke[at, 0:256], low_ds)
            for t in range(BLOCK // 128):
                m = b * (BLOCK // 128) + t
                full, rest = pack_out(dk[t * 128 : (t + 1) * 128])
                ref[m, 0:128, :] = full
                ref[m, 256:320, :] = rest
                full, rest = pack_out(dv[t * 128 : (t + 1) * 128])
                ref[m, 128:256, :] = full
                ref[m, 320:384, :] = rest
            return carry

        lax.fori_loop(0, 1024 // BLOCK, back, 0)

    dq = dqt[...].T * SCALE
    for k in range(XS):
        to = lax.rem(x_ref[0] + XS - k, XS)
        at = slice(k * 128, (k + 1) * 128)
        full, rest = pack_out(att_ref[at, :].astype(F32))
        oq_ref[to, 0:128, :] = full
        oq_ref[to, 256:320, :] = rest
        full, rest = pack_out(dq[at])
        oq_ref[to, 128:256, :] = full
        oq_ref[to, 320:384, :] = rest
        rows = gb_ref[k * PROW : (k + 1) * PROW, :]
        hi = rows.astype(BF).astype(F32)
        oq_ref[to, 384:400, :] = jnp.concatenate([hi, rows - hi], axis=0).astype(BF)


def cores_kernel(z_ref, own_ref, other_ref, send_ref, keep_ref):
    z = z_ref[0]
    for x in range(XS):
        away = x * ZS + 1 - z
        send_ref[x] = (own_ref[away].astype(F32) + other_ref[away].astype(F32)).astype(BF)
        here = x * ZS + z
        keep_ref[x] = own_ref[here].astype(F32) + other_ref[here].astype(F32)


def merge_kernel(keep_ref, come_ref, far_ref, out_ref):
    total = jnp.sum(far_ref[...], axis=0)
    hi = total.astype(BF).astype(F32)
    rest = total - hi
    mid = rest.astype(BF).astype(F32)
    rows = jnp.concatenate([hi, mid, rest - mid, jnp.zeros((4, 128), F32)], axis=0).astype(BF)
    for x in range(XS):
        out_ref[x, 0:384, :] = (keep_ref[x] + come_ref[x].astype(F32)).astype(BF)
        out_ref[x, 384:400, :] = rows


def put(ref, fulls, halves):
    low = low_lanes(64)
    for pair in range(2):
        even, odd = halves[2 * pair], halves[2 * pair + 1]
        mid = jnp.concatenate(
            [jnp.where(low, even, roll_half(odd)), jnp.where(low, roll_half(even), odd)], axis=0
        )
        ref[:, (3 * pair) * 128 : (3 * pair + 1) * 128] = fulls[2 * pair].astype(BF)
        ref[:, (3 * pair + 1) * 128 : (3 * pair + 2) * 128] = mid.astype(BF)
        ref[:, (3 * pair + 2) * 128 : (3 * pair + 3) * 128] = fulls[2 * pair + 1].astype(BF)


def query_kernel(oq_ref, w_ref, att_ref, dq_ref, gp_ref):
    for base, ref in ((0, att_ref), (1, dq_ref)):
        put(
            ref,
            [oq_ref[h, base * 128 : (base + 1) * 128, :] for h in range(HEADS)],
            [oq_ref[h, 256 + base * 64 : 320 + base * 64, :].astype(F32) for h in range(HEADS)],
        )
    whi, wmid, _ = split3(w_ref[...])
    wrows = jnp.concatenate([whi.astype(F32), wmid.astype(F32), whi.astype(F32)], axis=0)
    wrows = jnp.concatenate([wrows, jnp.zeros((4, 128), F32)], axis=0).astype(BF)
    blocks = [oq_ref[h, 384:400, :].astype(F32) for h in range(HEADS)]
    zero = jnp.zeros((4, 128), F32)
    for i in range(PROW):
        hi = jnp.concatenate([b[i : i + 1] for b in blocks], axis=0)
        lo = jnp.concatenate([b[8 + i : 9 + i] for b in blocks], axis=0)
        grads = jnp.concatenate([hi, hi, lo, zero], axis=0)
        gp_ref[i] = nn(grads.T.astype(BF), wrows).astype(BF)


def key_kernel(dkv_ref, dk_ref, dv_ref, gw_ref):
    for base, ref in ((0, dk_ref), (1, dv_ref)):
        put(
            ref,
            [dkv_ref[h, base * 128 : (base + 1) * 128, :] for h in range(HEADS)],
            [dkv_ref[h, 256 + base * 64 : 320 + base * 64, :].astype(F32) for h in range(HEADS)],
        )
    total = jnp.zeros((16, 128), F32)
    for x in range(XS):
        total += dkv_ref[x, 384:400, :].astype(F32)
    gw_ref[...] = (total[8:12] + total[4:8]) + total[0:4]


def shape(*dims, dtype=BF):
    return jax.ShapeDtypeStruct(dims, dtype)


def call(kernel, out_shape, args, scratch=(), flops=0, moved=0, smem=0, hbm=0, limit=32):
    single = not isinstance(out_shape, tuple)
    rest = len(args) - smem - hbm
    return pl.pallas_call(
        kernel,
        out_shape=out_shape,
        in_specs=[SMEM] * smem + [ANY] * hbm + [VMEM] * rest,
        out_specs=VMEM if single else (VMEM,) * len(out_shape),
        scratch_shapes=list(scratch),
        cost_estimate=pl.CostEstimate(flops=flops, bytes_accessed=moved, transcendentals=0),
        compiler_params=pltpu.CompilerParams(vmem_limit_bytes=limit * 1024 * 1024),
    )(*args)


def seq_index(x, z, c):
    return (x * ZS + z) * CS + c


def body(dp, queries, keys, values, cotangent, pair, pair_weight):
    xz_groups = [[seq_index(x, z, c) for x in range(XS) for z in range(ZS)] for c in range(CS)]
    x_groups = [[seq_index(x, z, c) for x in range(XS)] for z in range(ZS) for c in range(CS)]
    far_groups = [
        [d * 16 + seq_index(x, z, c) for d in range(dp) for z in range(ZS)]
        for x in range(XS)
        for c in range(CS)
    ]
    across = [
        (seq_index(x, z, c), seq_index(x, 1 - z, c))
        for x in range(XS)
        for z in range(ZS)
        for c in range(CS)
    ]
    swap = [(s, s ^ 1) for s in range(16)]

    def ring(k):
        return [
            (seq_index(x, z, c), seq_index((x + k) % XS, z, c))
            for x in range(XS)
            for z in range(ZS)
            for c in range(CS)
        ]

    place = lax.axis_index("seq").astype(jnp.int32)
    core = (place % CS).reshape(1)
    own_z = (place // CS % ZS).reshape(1)
    own_x = (place // (ZS * CS)).reshape(1)
    pair_rows = pair[0]
    kv = call(
        pack_kv_kernel,
        shape(8, 384, 128),
        (keys[0], values[0]),
        hbm=2,
        scratch=(pltpu.VMEM((TOK, 768), BF), pltpu.VMEM((TOK, 768), BF), pltpu.SemaphoreType.DMA((2,))),
        moved=1_500_000,
        limit=56,
    )
    kv, query_rows, cot_rows = lax.optimization_barrier((kv, queries[0], cotangent[0]))
    kv_own = lax.all_to_all(kv, "seq", 0, 0, axis_index_groups=xz_groups)
    qd = call(
        pack_qd_kernel,
        (shape(400, 128),) * XS,
        (own_x, query_rows, cot_rows, pair_rows, pair_weight.T),
        smem=1,
        hbm=4,
        scratch=(
            pltpu.VMEM((TOK, 768), BF),
            pltpu.VMEM((TOK, 768), BF),
            pltpu.VMEM((PROW, PAIRS, 128), BF),
            pltpu.VMEM((HEADS, 128), F32),
            pltpu.VMEM((HEADS, 400, 128), BF),
            pltpu.SemaphoreType.DMA((4,)),
        ),
        flops=2 * 24 * 1024 * 128,
        moved=1_500_000,
        limit=8,
    )
    qd = [qd[0]] + [lax.ppermute(qd[k], "seq", ring(k)) for k in range(1, XS)]
    kv_own, qd = lax.optimization_barrier((kv_own, qd))
    kv_other = lax.ppermute(kv_own, "seq", swap)
    pb, dsb, ke, qe, cs, att, gb = call(
        scores_kernel,
        (
            shape(KROWS, QROWS), shape(KROWS, QROWS), shape(KROWS, 512), shape(QROWS, 512),
            shape(QROWS, 256), shape(QROWS, 256), shape(XS * PROW, 128, dtype=F32),
        ),
        (core, *qd, kv_own, kv_other),
        smem=1,
        scratch=(
            pltpu.VMEM((KROWS, 256), BF),
            pltpu.VMEM((KROWS, QROWS), F32),
            pltpu.VMEM((256, QROWS), F32),
            pltpu.VMEM((PAIRS, QROWS), F32),
        ),
        flops=4 * 2 * QROWS * KROWS * 256,
        moved=8_000_000,
        limit=32,
    )
    count = dp * ZS
    dkv_own, dkv_other, oq = call(
        grads_kernel,
        (shape(8, 384, 128), shape(8, 384, 128), shape(XS, 400, 128)),
        (own_x, pb, dsb, ke, qe, cs, att, gb),
        smem=1,
        scratch=(pltpu.VMEM((256, QROWS), F32),),
        flops=3 * 2 * QROWS * KROWS * 256,
        moved=8_000_000,
        limit=16,
    )
    oq = lax.all_to_all(oq, "seq", 0, 0, axis_index_groups=x_groups)
    dkv_swapped = lax.ppermute(dkv_other, "seq", swap)
    send, keep = call(
        cores_kernel,
        (shape(XS, 384, 128), shape(XS, 384, 128, dtype=F32)),
        (own_z, dkv_own, dkv_swapped),
        smem=1,
        moved=2_400_000,
        limit=8,
    )
    send, oq = lax.optimization_barrier((send, oq))
    come = lax.ppermute(send, "seq", across)
    term = call(
        weight_kernel, shape(HEADS, 128, dtype=F32), (oq, pair_rows),
        flops=2 * 1024 * 128 * 8, moved=500_000, limit=8,
    )
    term = term + lax.ppermute(term, "seq", swap)
    spread = jnp.broadcast_to(term[None], (count, HEADS, 128))
    far = lax.all_to_all(spread, ("dp", "seq"), 0, 0, axis_index_groups=far_groups)
    att, dq, gp = call(
        query_kernel,
        (shape(128, 768), shape(128, 768), shape(PROW, PAIRS, 128)),
        (oq, pair_weight.T),
        flops=2 * 1024 * 128 * 16,
        moved=1_100_000,
        limit=8,
    )
    dkv = call(
        merge_kernel, shape(XS, 400, 128), (keep, come, far), moved=1_600_000, limit=8
    )
    dkv_back = lax.all_to_all(dkv, "seq", 0, 0, axis_index_groups=x_groups)
    dk, dv, gw = call(
        key_kernel,
        (shape(128, 768), shape(128, 768), shape(HEADS, 128, dtype=F32)),
        (dkv_back,),
        moved=800_000,
        limit=8,
    )
    return att[None], dq[None], dk[None], dv[None], gp[None], gw.T


def solution(mesh):
    rows = P("dp", "seq", None)
    cells = P("dp", "seq", None, None)
    return jax.shard_map(
        functools.partial(body, mesh.shape["dp"]),
        mesh=mesh,
        in_specs=(rows, rows, rows, rows, cells, P()),
        out_specs=(rows, rows, rows, rows, cells, P()),
        check_vma=False,
    )
```

time: 143 us -> 117 us (0.82)
  the two profiles are of different devices: /device:TPU:64 before, /device:TPU:1 now
where the time goes in v2:
time: 117 us; the launch traced here: 115 us
  starting transfers between devices  46.6 us (40%)
  blocking collectives  28.1 us (24%)
  waiting for transfers between devices  20.4 us (17%)
  Pallas kernels  19.3 us (16%)
    all_to_all x1, blocking collectives, body(): lax.all_to_all(spread, ('dp', 'seq'), 0, 0, axis_index_groups=far_groups)  28.1 us
    pallas_call x9, Pallas kernels, call(): pl.pallas_call(kernel, out_shape=out_shape, in_specs=[SMEM] * smem + [ANY...  19.3 us
    all_to_all x1, starting transfers between devices, body(): kv_own = lax.all_to_all(kv, 'seq', 0, 0, axis_index_groups=xz_groups)  13.3 us
    ppermute x3, starting transfers between devices, body(): qd = [qd[0]] + [lax.ppermute(qd[k], 'seq', ring(k)) for k in range(1, XS)]  10.8 us
    all_to_all x1, waiting for transfers between devices, body(): oq = lax.all_to_all(oq, 'seq', 0, 0, axis_index_groups=x_groups)  7.76 us
    ppermute x1, starting transfers between devices, body(): come = lax.ppermute(send, 'seq', across)  6.47 us
    all_to_all x1, waiting for transfers between devices, body(): dkv_back = lax.all_to_all(dkv, 'seq', 0, 0, axis_index_groups=x_groups)  5.2 us
    ppermute x3, waiting for transfers between devices, body(): qd = [qd[0]] + [lax.ppermute(qd[k], 'seq', ring(k)) for k in range(1, XS)]  4.8 us
  transfers between devices with their start and end apart: 10, of which 6 were waited for; matrix products, arithmetic and copies ran while one was open for 0% of the time, Pallas kernels for 2%

profile of v2, /device:TPU:1, one launch (start us, length us, event | category | flops | bytes accessed | tf_op | source)
XLA Modules:
  0.0 115.3 jit_solution(10426849417591039435)
XLA Ops:
  0.6 0.0 copy-start.2
  0.7 2.1 %shard_map.109 = bf16[8,384,128]{2,1,0:T(8,128)(2,1)} custom-call(bf16[128,768]{1,0:T(8,128)(2,1)} %bitcast.21, bf16[128,768]{1,0:T(8,128)(2,1)} %bitcast.22), custom_call_target="tpu_custom_call" | custom-call | bytes 1500000 | tf_op jit(solution)/shard_map/pallas_call | solution.py:353
  2.8 13.3 %all-to-all-start = ((bf16[8,384,128]{2,1,0:T(8,128)(2,1)}), bf16[8,384,128]{2,1,0:T(8,128)(2,1)S(1)}, u32[]{:S(2)}, u32[]{:S(2)}) async-start(bf16[8,384,128]{2,1,0:T(8,128)(2,1)} %shard_map.109), calls=%async_computation | async-start | bytes 1572864 | tf_op jit(solution)/shard_map/all_to_all | solution.py:407
  16.1 0.0 copy-done.2
  16.1 1.0 shard_map.110
  17.1 3.4 %collective-permute-start = (bf16[400,128]{1,0:T(8,128)(2,1)S(1)}, bf16[400,128]{1,0:T(8,128)(2,1)S(1)}, u32[]{:S(2)}, u32[]{:S(2)}) collective-permute-start(bf16[400,128]{1,0:T(8,128)(2,1)S(1)} %get-tuple-element.42), channel_id=1, source_target_pairs={{0,4},{1,5},{2,6},{3,7},{4,8},{5,9},{6,10},{7,11},{8,12},{9,13},{1... | collective-permute-start | bytes 307208 | tf_op jit(solution)/shard_map/ppermute | solution.py:426
  20.5 4.3 %collective-permute-start.1 = (bf16[400,128]{1,0:T(8,128)(2,1)S(1)}, bf16[400,128]{1,0:T(8,128)(2,1)S(1)}, u32[]{:S(2)}, u32[]{:S(2)}) collective-permute-start(bf16[400,128]{1,0:T(8,128)(2,1)S(1)} %get-tuple-element.43), channel_id=1, source_target_pairs={{0,8},{1,9},{2,10},{3,11},{4,12},{5,13},{6,14},{7,15},{8,0},{9,1},... | collective-permute-start | bytes 307208 | tf_op jit(solution)/shard_map/ppermute | solution.py:426
  24.8 3.1 %collective-permute-start.2 = (bf16[400,128]{1,0:T(8,128)(2,1)S(1)}, bf16[400,128]{1,0:T(8,128)(2,1)S(1)}, u32[]{:S(2)}, u32[]{:S(2)}) collective-permute-start(bf16[400,128]{1,0:T(8,128)(2,1)S(1)} %get-tuple-element.44), channel_id=1, source_target_pairs={{0,12},{1,13},{2,14},{3,15},{4,0},{5,1},{6,2},{7,3},{8,4},{9,5},{1... | collective-permute-start | bytes 307208 | tf_op jit(solution)/shard_map/ppermute | solution.py:426
  27.9 0.0 collective-permute-done.qd1
  27.9 2.1 %collective-permute-done.1.qd2 = bf16[400,128]{1,0:T(8,128)(2,1)S(1)} collective-permute-done((bf16[400,128]{1,0:T(8,128)(2,1)S(1)}, bf16[400,128]{1,0:T(8,128)(2,1)S(1)}, u32[]{:S(2)}, u32[]{:S(2)}) %collective-permute-start.1) | collective-permute-done | bytes 102432 | tf_op jit(solution)/shard_map/ppermute | solution.py:426
  30.1 2.7 %collective-permute-done.2.qd3 = bf16[400,128]{1,0:T(8,128)(2,1)S(1)} collective-permute-done((bf16[400,128]{1,0:T(8,128)(2,1)S(1)}, bf16[400,128]{1,0:T(8,128)(2,1)S(1)}, u32[]{:S(2)}, u32[]{:S(2)}) %collective-permute-start.2) | collective-permute-done | bytes 102432 | tf_op jit(solution)/shard_map/ppermute | solution.py:426
  32.7 0.0 all-to-all-done.kv_own
  32.7 3.2 %collective-permute-start.3 = (bf16[8,384,128]{2,1,0:T(8,128)(2,1)S(1)}, bf16[8,384,128]{2,1,0:T(8,128)(2,1)S(1)}, u32[]{:S(2)}, u32[]{:S(2)}) collective-permute-start(bf16[8,384,128]{2,1,0:T(8,128)(2,1)S(1)} %all-to-all-done.kv_own), channel_id=1, source_target_pairs={{0,1},{1,0},{2,3},{3,2},{4,5},{5,4},{6,7},{7,6},{8,9},{9,8},{10,11... | collective-permute-start | bytes 2359304 | tf_op jit(solution)/shard_map/ppermute | solution.py:428
  36.0 1.9 %collective-permute-done.3.kv_other = bf16[8,384,128]{2,1,0:T(8,128)(2,1)S(1)} collective-permute-done((bf16[8,384,128]{2,1,0:T(8,128)(2,1)S(1)}, bf16[8,384,128]{2,1,0:T(8,128)(2,1)S(1)}, u32[]{:S(2)}, u32[]{:S(2)}) %collective-permute-start.3) | collective-permute-done | bytes 786464 | tf_op jit(solution)/shard_map/ppermute | solution.py:428
  37.8 9.0 %shard_map.111 = (bf16[2048,512]{1,0:T(8,128)(2,1)S(1)}, bf16[2048,512]{1,0:T(8,128)(2,1)S(1)}, bf16[2048,512]{1,0:T(8,128)(2,1)S(1)}, bf16[512,512]{1,0:T(8,128...) custom-call(s32[1]{0:T(128)} %bitcast.2.core_ref, ...), custom_call_target="tpu_custom_call" | custom-call | flops 2147483648 | bytes 8000000 | tf_op jit(solution)/shard_map/pallas_call | solution.py:353
  46.8 4.1 %shard_map.112 = (bf16[8,384,128]{2,1,0:T(8,128)(2,1)S(1)}, bf16[8,384,128]{2,1,0:T(8,128)(2,1)S(1)}, bf16[4,400,128]{2,1,0:T(8,128)(2,1)}) custom-call(s32[1]{0:T(128)} %bitcast.1.x_ref, bf16[2048,512]{1,0:T(8,128)(2,1)S(1)} %get-tuple-element.50.pb, bf16[2048,512]{1,0:T(8,128)(2,1)S(1)} %get-tuple-element.51.dsb, ...), custom_call_target="tpu_custom_call" | custom-call | flops 1610612736 | bytes 8000000 | tf_op jit(solution)/shard_map/pallas_call | solution.py:353
  51.0 2.3 %collective-permute-start.4 = (bf16[8,384,128]{2,1,0:T(8,128)(2,1)S(1)}, bf16[8,384,128]{2,1,0:T(8,128)(2,1)S(1)}, u32[]{:S(2)}, u32[]{:S(2)}) collective-permute-start(bf16[8,384,128]{2,1,0:T(8,128)(2,1)S(1)} %get-tuple-element.58), channel_id=1, source_target_pairs={{0,1},{1,0},{2,3},{3,2},{4,5},{5,4},{6,7},{7,6},{8,9},{9,8},{10,11... | collective-permute-start | bytes 2359304 | tf_op jit(solution)/shard_map/ppermute | solution.py:459
  53.2 4.0 %all-to-all-start.1 = ((bf16[4,400,128]{2,1,0:T(8,128)(2,1)}), bf16[4,400,128]{2,1,0:T(8,128)(2,1)S(1)}, u32[]{:S(2)}, u32[]{:S(2)}) async-start(bf16[4,400,128]{2,1,0:T(8,128)(2,1)} %get-tuple-element.60), calls=%async_computation.1 | async-start | bytes 819200 | tf_op jit(solution)/shard_map/all_to_all | solution.py:458
  57.2 0.0 collective-permute-done.4.other_ref
  57.2 0.2 shard_map.113
  57.4 7.8 %all-to-all-done.1.oq_ref = bf16[4,400,128]{2,1,0:T(8,128)(2,1)S(1)} async-done(((bf16[4,400,128]{2,1,0:T(8,128)(2,1)}), bf16[4,400,128]{2,1,0:T(8,128)(2,1)S(1)}, u32[]{:S(2)}, u32[]{:S(2)}) %all-to-all-start.1) | async-done | bytes 409632 | tf_op jit(solution)/shard_map/all_to_all | solution.py:458
  65.1 6.5 %collective-permute-start.5 = (bf16[4,384,128]{2,1,0:T(8,128)(2,1)S(1)}, bf16[4,384,128]{2,1,0:T(8,128)(2,1)S(1)}, u32[]{:S(2)}, u32[]{:S(2)}) collective-permute-start(bf16[4,384,128]{2,1,0:T(8,128)(2,1)S(1)} %get-tuple-element.65), channel_id=1, source_target_pairs={{0,2},{1,3},{2,0},{3,1},{4,6},{5,7},{6,4},{7,5},{8,10},{9,11},{10,... | collective-permute-start | bytes 1179656 | tf_op jit(solution)/shard_map/ppermute | solution.py:469
  71.6 0.1 shard_map.115
  71.8 3.1 %collective-permute-start.6 = (f32[4,128]{1,0:T(4,128)S(1)}, f32[4,128]{1,0:T(4,128)S(1)}, u32[]{:S(2)}, u32[]{:S(2)}) collective-permute-start(f32[4,128]{1,0:T(4,128)S(1)} %shard_map.115), channel_id=1, source_target_pairs={{0,1},{1,0},{2,3},{3,2},{4,5},{5,4},{6,7},{7,6},{8,9},{9,8},{10,11... | collective-permute-start | bytes 6152 | tf_op jit(solution)/shard_map/ppermute | solution.py:474
  74.9 0.8 collective-permute-done.6
  75.7 28.1 %all_to_all.20.far_ref = f32[64,4,128]{2,1,0:T(4,128)S(1)} all-to-all(f32[64,4,128]{2,1,0:T(4,128)S(1)} %broadcast_in_dim.23), channel_id=1, replica_groups={{0,2,16,18,32,34,48,50,64,66,80,82,96,98,112,114,128,130,144,146,160,16..., dimensions={0} | all-to-all | bytes 262144 | tf_op jit(solution)/shard_map/all_to_all | solution.py:476
  103.9 0.0 collective-permute-done.5.come_ref
  103.9 0.9 shard_map.116
  104.7 3.5 %all-to-all-start.3 = ((bf16[4,400,128]{2,1,0:T(8,128)(2,1)}), bf16[4,400,128]{2,1,0:T(8,128)(2,1)S(1)}, u32[]{:S(2)}, u32[]{:S(2)}) async-start(bf16[4,400,128]{2,1,0:T(8,128)(2,1)} %shard_map.116), calls=%async_computation.3 | async-start | bytes 819200 | tf_op jit(solution)/shard_map/all_to_all | solution.py:488
  108.2 1.1 shard_map.114
  109.3 5.2 %all-to-all-done.3.dkv_ref = bf16[4,400,128]{2,1,0:T(8,128)(2,1)S(1)} async-done(((bf16[4,400,128]{2,1,0:T(8,128)(2,1)}), bf16[4,400,128]{2,1,0:T(8,128)(2,1)S(1)}, u32[]{:S(2)}, u32[]{:S(2)}) %all-to-all-start.3) | async-done | bytes 409632 | tf_op jit(solution)/shard_map/all_to_all | solution.py:488
  114.5 0.9 shard_map.117
  (8 shorter events, 0.0 us)
Async XLA Ops:
  0.6 15.5 %copy-start.2 = (bf16[1,128,768]{2,1,0:T(8,128)(2,1)S(1)}, bf16[1,128,768]{2,1,0:T(8,128)(2,1)}, u32[]{:S(2)}) copy-start(bf16[1,128,768]{2,1,0:T(8,128)(2,1)} %param.9) | copy-start | bytes 589828
  0.6 15.5 %copy-start.1 = (bf16[1,128,768]{2,1,0:T(8,128)(2,1)S(1)}, bf16[1,128,768]{2,1,0:T(8,128)(2,1)}, u32[]{:S(2)}) copy-start(bf16[1,128,768]{2,1,0:T(8,128)(2,1)} %param.6) | copy-start | bytes 589828
  0.7 15.5 %copy-start.3 = (f32[128,4]{0,1:T(4,128)S(1)}, f32[128,4]{0,1:T(4,128)}, u32[]{:S(2)}) copy-start(f32[128,4]{0,1:T(4,128)} %param.11) | copy-start | bytes 6148
  0.7 15.5 %copy-start = (bf16[1,8,128,128]{3,2,1,0:T(8,128)(2,1)S(1)}, bf16[1,8,128,128]{3,2,1,0:T(8,128)(2,1)}, u32[]{:S(2)}) copy-start(bf16[1,8,128,128]{3,2,1,0:T(8,128)(2,1)} %param.10) | copy-start | bytes 786436
  2.8 30.0 %all-to-all-start = ((bf16[8,384,128]{2,1,0:T(8,128)(2,1)}), bf16[8,384,128]{2,1,0:T(8,128)(2,1)S(1)}, u32[]{:S(2)}, u32[]{:S(2)}) async-start(bf16[8,384,128]{2,1,0:T(8,128)(2,1)} %shard_map.109), calls=%async_computation | async-start | bytes 1572864 | tf_op jit(solution)/shard_map/all_to_all | solution.py:407
  17.1 10.8 %collective-permute-start = (bf16[400,128]{1,0:T(8,128)(2,1)S(1)}, bf16[400,128]{1,0:T(8,128)(2,1)S(1)}, u32[]{:S(2)}, u32[]{:S(2)}) collective-permute-start(bf16[400,128]{1,0:T(8,128)(2,1)S(1)} %get-tuple-element.42), channel_id=1, source_target_pairs={{0,4},{1,5},{2,6},{3,7},{4,8},{5,9},{6,10},{7,11},{8,12},{9,13},{1... | collective-permute-start | bytes 307208 | tf_op jit(solution)/shard_map/ppermute | solution.py:426
  20.5 9.6 %collective-permute-start.1 = (bf16[400,128]{1,0:T(8,128)(2,1)S(1)}, bf16[400,128]{1,0:T(8,128)(2,1)S(1)}, u32[]{:S(2)}, u32[]{:S(2)}) collective-permute-start(bf16[400,128]{1,0:T(8,128)(2,1)S(1)} %get-tuple-element.43), channel_id=1, source_target_pairs={{0,8},{1,9},{2,10},{3,11},{4,12},{5,13},{6,14},{7,15},{8,0},{9,1},... | collective-permute-start | bytes 307208 | tf_op jit(solution)/shard_map/ppermute | solution.py:426
  24.8 7.9 %collective-permute-start.2 = (bf16[400,128]{1,0:T(8,128)(2,1)S(1)}, bf16[400,128]{1,0:T(8,128)(2,1)S(1)}, u32[]{:S(2)}, u32[]{:S(2)}) collective-permute-start(bf16[400,128]{1,0:T(8,128)(2,1)S(1)} %get-tuple-element.44), channel_id=1, source_target_pairs={{0,12},{1,13},{2,14},{3,15},{4,0},{5,1},{6,2},{7,3},{8,4},{9,5},{1... | collective-permute-start | bytes 307208 | tf_op jit(solution)/shard_map/ppermute | solution.py:426
  32.7 5.1 %collective-permute-start.3 = (bf16[8,384,128]{2,1,0:T(8,128)(2,1)S(1)}, bf16[8,384,128]{2,1,0:T(8,128)(2,1)S(1)}, u32[]{:S(2)}, u32[]{:S(2)}) collective-permute-start(bf16[8,384,128]{2,1,0:T(8,128)(2,1)S(1)} %all-to-all-done.kv_own), channel_id=1, source_target_pairs={{0,1},{1,0},{2,3},{3,2},{4,5},{5,4},{6,7},{7,6},{8,9},{9,8},{10,11... | collective-permute-start | bytes 2359304 | tf_op jit(solution)/shard_map/ppermute | solution.py:428
  51.0 6.2 %collective-permute-start.4 = (bf16[8,384,128]{2,1,0:T(8,128)(2,1)S(1)}, bf16[8,384,128]{2,1,0:T(8,128)(2,1)S(1)}, u32[]{:S(2)}, u32[]{:S(2)}) collective-permute-start(bf16[8,384,128]{2,1,0:T(8,128)(2,1)S(1)} %get-tuple-element.58), channel_id=1, source_target_pairs={{0,1},{1,0},{2,3},{3,2},{4,5},{5,4},{6,7},{7,6},{8,9},{9,8},{10,11... | collective-permute-start | bytes 2359304 | tf_op jit(solution)/shard_map/ppermute | solution.py:459
  53.2 11.9 %all-to-all-start.1 = ((bf16[4,400,128]{2,1,0:T(8,128)(2,1)}), bf16[4,400,128]{2,1,0:T(8,128)(2,1)S(1)}, u32[]{:S(2)}, u32[]{:S(2)}) async-start(bf16[4,400,128]{2,1,0:T(8,128)(2,1)} %get-tuple-element.60), calls=%async_computation.1 | async-start | bytes 819200 | tf_op jit(solution)/shard_map/all_to_all | solution.py:458
  65.1 38.7 %collective-permute-start.5 = (bf16[4,384,128]{2,1,0:T(8,128)(2,1)S(1)}, bf16[4,384,128]{2,1,0:T(8,128)(2,1)S(1)}, u32[]{:S(2)}, u32[]{:S(2)}) collective-permute-start(bf16[4,384,128]{2,1,0:T(8,128)(2,1)S(1)} %get-tuple-element.65), channel_id=1, source_target_pairs={{0,2},{1,3},{2,0},{3,1},{4,6},{5,7},{6,4},{7,5},{8,10},{9,11},{10,... | collective-permute-start | bytes 1179656 | tf_op jit(solution)/shard_map/ppermute | solution.py:469
  71.8 3.9 %collective-permute-start.6 = (f32[4,128]{1,0:T(4,128)S(1)}, f32[4,128]{1,0:T(4,128)S(1)}, u32[]{:S(2)}, u32[]{:S(2)}) collective-permute-start(f32[4,128]{1,0:T(4,128)S(1)} %shard_map.115), channel_id=1, source_target_pairs={{0,1},{1,0},{2,3},{3,2},{4,5},{5,4},{6,7},{7,6},{8,9},{9,8},{10,11... | collective-permute-start | bytes 6152 | tf_op jit(solution)/shard_map/ppermute | solution.py:474
  104.7 9.8 %all-to-all-start.3 = ((bf16[4,400,128]{2,1,0:T(8,128)(2,1)}), bf16[4,400,128]{2,1,0:T(8,128)(2,1)S(1)}, u32[]{:S(2)}, u32[]{:S(2)}) async-start(bf16[4,400,128]{2,1,0:T(8,128)(2,1)} %shard_map.116), calls=%async_computation.3 | async-start | bytes 819200 | tf_op jit(solution)/shard_map/all_to_all | solution.py:488

commit v3 on v2

--- a/solution.py
+++ b/solution.py
@@ -19,7 +19,8 @@
 CS = 2
 QROWS = XS * TOK
 KROWS = XS * ZS * CS * TOK
-BLOCK = 256
+BLOCK = 1024
+UNROLL = 2
 SCALE = HDIM ** (-0.5)
 LOG2E = 1.0 / math.log(2.0)
 BF = jnp.bfloat16
@@ -145,13 +146,21 @@
     return block[:, :128].astype(BF), (rest[:64] + roll_half(rest[64:])).astype(BF)
 
 
-def scores_kernel(
-    core_ref, qd0, qd1, qd2, qd3, kv_own, kv_other, pb, dsb, ke, qe, cs, att_ref, gb_ref,
-    vs, st, ot, pool,
+def loop(steps, body, init):
+    return lax.fori_loop(0, steps, body, init, unroll=UNROLL)
+
+
+def attn_kernel(
+    core_ref, x_ref, kv_other, qd0, qd1, qd2, qd3, kv_own, dko_ref, dkx_ref, oq_ref,
+    ke, vs, qe, cs, st, ot, dqt, pool, kv_vmem, sem,
 ):
     low = low_lanes(64)
     core = core_ref[0]
-    for half, kv_ref in enumerate((kv_own, kv_other)):
+    fetch = pltpu.make_async_copy(kv_other, kv_vmem, sem)
+    fetch.start()
+    for half, kv_ref in enumerate((kv_own, kv_vmem)):
+        if half == 1:
+            fetch.wait()
         mine = core if half == 0 else 1 - core
         for m in range(8):
             base = half * 1024 + m * 128
@@ -188,7 +197,7 @@
         st[at, :] = s
         return jnp.maximum(top, jnp.max(s.reshape(BLOCK // 8, 8, QROWS), axis=0))
 
-    top = lax.fori_loop(0, steps, scores, jnp.full((8, QROWS), -jnp.inf, F32))
+    top = loop(steps, scores, jnp.full((8, QROWS), -jnp.inf, F32))
     top = jnp.max(top, axis=0, keepdims=True) * (SCALE * LOG2E)
     ot[...] = jnp.zeros_like(ot)
 
@@ -199,35 +208,56 @@
         ot[...] += tn(vs[at, :], w.astype(BF))
         return total + jnp.sum(w.reshape(BLOCK // 8, 8, QROWS), axis=0)
 
-    total = lax.fori_loop(0, steps, weigh, jnp.zeros((8, QROWS), F32))
+    total = loop(steps, weigh, jnp.zeros((8, QROWS), F32))
     inv = 1.0 / jnp.sum(total, axis=0, keepdims=True)
     att = (ot[...] * inv).astype(BF).astype(F32)
     delta = jnp.sum(att * cs[...].astype(F32).T, axis=0, keepdims=True)
-    att_ref[...] = att.T.astype(BF)
-
-    for half in range(CS):
+    att = att.T
+    dqt[...] = jnp.zeros_like(dqt)
+
+    for half, ref in ((0, dko_ref), (1, dkx_ref)):
         mine = core if half == 0 else 1 - core
 
         def back(b, carry):
             at = pl.ds(pl.multiple_of(half * 1024 + b * BLOCK, BLOCK), BLOCK)
             prob = st[at, :] * inv
-            pb[at, :] = prob.astype(BF)
+            dv = nn(prob.astype(BF), cs[...])
             ds = prob * (nt(vs[at, :], cs[...]) - delta)
-            dsb[at, :] = ds.astype(BF)
+            low_ds = ds.astype(BF)
+            dk = nn(low_ds, qe[:, 0:256]) * SCALE
+            dqt[...] += tn(ke[at, 0:256], low_ds)
             pooled = jnp.sum(ds.reshape(BLOCK // POOL, POOL, QROWS), axis=1)
             for t in range(BLOCK // 128):
                 m = b * (BLOCK // 128) + t
+                full, rest = pack_out(dk[t * 128 : (t + 1) * 128])
+                ref[m, 0:128, :] = full
+                ref[m, 256:320, :] = rest
+                full, rest = pack_out(dv[t * 128 : (t + 1) * 128])
+                ref[m, 128:256, :] = full
+                ref[m, 320:384, :] = rest
                 pool[pl.ds(pl.multiple_of(m * 16 + mine * 8, 8), 8), :] = pooled[t * 8 : t * 8 + 8]
             return carry
 
-        lax.fori_loop(0, 1024 // BLOCK, back, 0)
+        loop(1024 // BLOCK, back, 0)
 
     row = lax.broadcasted_iota(jnp.int32, (QROWS // POOL, QROWS), 0)
     col = lax.broadcasted_iota(jnp.int32, (QROWS // POOL, QROWS), 1)
     pick = jnp.where(row == lax.shift_right_logical(col, 4), 1.0, 0.0).astype(BF)
     hi, lo = split2(pool[...])
     grad_bias = nt(pick, hi) + nt(pick, lo)
-    gb_ref[...] = grad_bias
+    dq = dqt[...].T * SCALE
+    for k in range(XS):
+        to = lax.rem(x_ref[0] + XS - k, XS)
+        at = slice(k * 128, (k + 1) * 128)
+        full, rest = pack_out(att[at])
+        oq_ref[to, 0:128, :] = full
+        oq_ref[to, 256:320, :] = rest
+        full, rest = pack_out(dq[at])
+        oq_ref[to, 128:256, :] = full
+        oq_ref[to, 320:384, :] = rest
+        rows = grad_bias[k * PROW : (k + 1) * PROW]
+        hi = rows.astype(BF).astype(F32)
+        oq_ref[to, 384:400, :] = jnp.concatenate([hi, rows - hi], axis=0).astype(BF)
 
 
 def weight_kernel(oq_ref, pair_ref, out_ref):
@@ -359,6 +389,31 @@
         cost_estimate=pl.CostEstimate(flops=flops, bytes_accessed=moved, transcendentals=0),
         compiler_params=pltpu.CompilerParams(vmem_limit_bytes=limit * 1024 * 1024),
     )(*args)
+
+
+def attention(*args):
+    return call(
+        attn_kernel,
+        (shape(8, 384, 128), shape(8, 384, 128), shape(XS, 400, 128)),
+        args,
+        smem=2,
+        hbm=1,
+        scratch=(
+            pltpu.VMEM((KROWS, 512), BF),
+            pltpu.VMEM((KROWS, 256), BF),
+            pltpu.VMEM((QROWS, 512), BF),
+            pltpu.VMEM((QROWS, 256), BF),
+            pltpu.VMEM((KROWS, QROWS), F32),
+            pltpu.VMEM((256, QROWS), F32),
+            pltpu.VMEM((256, QROWS), F32),
+            pltpu.VMEM((PAIRS, QROWS), F32),
+            pltpu.VMEM((8, 384, 128), BF),
+            pltpu.SemaphoreType.DMA(()),
+        ),
+        flops=8 * 2 * QROWS * KROWS * 256,
+        moved=5_000_000,
+        limit=32,
+    )
 
 
 def seq_index(x, z, c):
@@ -426,35 +481,9 @@
     qd = [qd[0]] + [lax.ppermute(qd[k], "seq", ring(k)) for k in range(1, XS)]
     kv_own, qd = lax.optimization_barrier((kv_own, qd))
     kv_other = lax.ppermute(kv_own, "seq", swap)
-    pb, dsb, ke, qe, cs, att, gb = call(
-        scores_kernel,
-        (
-            shape(KROWS, QROWS), shape(KROWS, QROWS), shape(KROWS, 512), shape(QROWS, 512),
-            shape(QROWS, 256), shape(QROWS, 256), shape(XS * PROW, 128, dtype=F32),
-        ),
-        (core, *qd, kv_own, kv_other),
-        smem=1,
-        scratch=(
-            pltpu.VMEM((KROWS, 256), BF),
-            pltpu.VMEM((KROWS, QROWS), F32),
-            pltpu.VMEM((256, QROWS), F32),
-            pltpu.VMEM((PAIRS, QROWS), F32),
-        ),
-        flops=4 * 2 * QROWS * KROWS * 256,
-        moved=8_000_000,
-        limit=32,
-    )
+    kv_other = pltpu.with_memory_space_constraint(kv_other, pltpu.MemorySpace.HBM)
     count = dp * ZS
-    dkv_own, dkv_other, oq = call(
-        grads_kernel,
-        (shape(8, 384, 128), shape(8, 384, 128), shape(XS, 400, 128)),
-        (own_x, pb, dsb, ke, qe, cs, att, gb),
-        smem=1,
-        scratch=(pltpu.VMEM((256, QROWS), F32),),
-        flops=3 * 2 * QROWS * KROWS * 256,
-        moved=8_000_000,
-        limit=16,
-    )
+    dkv_own, dkv_other, oq = attention(core, own_x, kv_other, *qd, kv_own)
     oq = lax.all_to_all(oq, "seq", 0, 0, axis_index_groups=x_groups)
     dkv_swapped = lax.ppermute(dkv_other, "seq", swap)
     send, keep = call(
@@ -465,7 +494,6 @@
         moved=2_400_000,
         limit=8,
     )
-    send, oq = lax.optimization_barrier((send, oq))
     come = lax.ppermute(send, "seq", across)
     term = call(
         weight_kernel, shape(HEADS, 128, dtype=F32), (oq, pair_rows),

time: 117 us -> 106 us (0.906)
  Pallas kernels: 19.3 us -> 13 us
  waiting for transfers between devices: 20.4 us -> 14.1 us
  local copies, waits for them, and re-layouts: 0.04 us -> 1.58 us
    pallas_call x9 -> x8, Pallas kernels: 19.3 us -> 13 us  [call(): pl.pallas_call(kernel, out_shape=out_shape, in_specs=[SMEM] * smem + [ANY...]
    all_to_all x1, waiting for transfers between devices: 7.76 us -> 1.61 us  [body(): oq = lax.all_to_all(oq, 'seq', 0, 0, axis_index_groups=x_groups)]
    unnamed x8 -> x10, local copies, waits for them, and re-layouts: 0.02 us -> 1.56 us
where the time goes in v3:
time: 106 us; the launch traced here: 105 us
  starting transfers between devices  46.3 us (44%)
  blocking collectives  28.8 us (27%)
  waiting for transfers between devices  14.1 us (13%)
  Pallas kernels  13 us (12%)
  local copies, waits for them, and re-layouts  1.58 us (1%)
    all_to_all x1, blocking collectives, body(): lax.all_to_all(spread, ('dp', 'seq'), 0, 0, axis_index_groups=far_groups)  28.8 us
    all_to_all x1, starting transfers between devices, body(): kv_own = lax.all_to_all(kv, 'seq', 0, 0, axis_index_groups=xz_groups)  13.4 us
    pallas_call x8, Pallas kernels, call(): pl.pallas_call(kernel, out_shape=out_shape, in_specs=[SMEM] * smem + [ANY...  13 us
    ppermute x3, starting transfers between devices, body(): qd = [qd[0]] + [lax.ppermute(qd[k], 'seq', ring(k)) for k in range(1, XS)]  10.8 us
    ppermute x1, starting transfers between devices, body(): come = lax.ppermute(send, 'seq', across)  6.15 us
    all_to_all x1, waiting for transfers between devices, body(): dkv_back = lax.all_to_all(dkv, 'seq', 0, 0, axis_index_groups=x_groups)  5.2 us
    ppermute x3, waiting for transfers between devices, body(): qd = [qd[0]] + [lax.ppermute(qd[k], 'seq', ring(k)) for k in range(1, XS)]  4.59 us
    all_to_all x1, starting transfers between devices, body(): oq = lax.all_to_all(oq, 'seq', 0, 0, axis_index_groups=x_groups)  3.98 us
  transfers between devices with their start and end apart: 10, of which 6 were waited for; matrix products, arithmetic and copies ran while one was open for 0% of the time, Pallas kernels for 2%

profile of v3, /device:TPU:1, one launch (start us, length us, event | category | flops | bytes accessed | tf_op | source)
XLA Modules:
  0.0 104.6 jit_solution(2509715400345900482)
XLA Ops:
  0.6 2.0 %shard_map.109 = bf16[8,384,128]{2,1,0:T(8,128)(2,1)} custom-call(bf16[128,768]{1,0:T(8,128)(2,1)} %bitcast.21, bf16[128,768]{1,0:T(8,128)(2,1)} %bitcast.22), custom_call_target="tpu_custom_call" | custom-call | bytes 1500000 | tf_op jit(solution)/shard_map/pallas_call | solution.py:383
  2.7 0.0 copy-start
  2.7 0.0 copy-start.1
  2.7 0.0 copy-start.2
  2.7 13.4 %all-to-all-start = ((bf16[8,384,128]{2,1,0:T(8,128)(2,1)}), bf16[8,384,128]{2,1,0:T(8,128)(2,1)S(1)}, u32[]{:S(2)}, u32[]{:S(2)}) async-start(bf16[8,384,128]{2,1,0:T(8,128)(2,1)} %shard_map.109), calls=%async_computation | async-start | bytes 1572864 | tf_op jit(solution)/shard_map/all_to_all | solution.py:462
  16.2 0.6 copy-done.3
  16.8 1.0 shard_map.110
  17.8 3.4 %collective-permute-start = (bf16[400,128]{1,0:T(8,128)(2,1)S(1)}, bf16[400,128]{1,0:T(8,128)(2,1)S(1)}, u32[]{:S(2)}, u32[]{:S(2)}) collective-permute-start(bf16[400,128]{1,0:T(8,128)(2,1)S(1)} %get-tuple-element.33), channel_id=1, source_target_pairs={{0,4},{1,5},{2,6},{3,7},{4,8},{5,9},{6,10},{7,11},{8,12},{9,13},{1... | collective-permute-start | bytes 307208 | tf_op jit(solution)/shard_map/ppermute | solution.py:481
  21.2 4.3 %collective-permute-start.1 = (bf16[400,128]{1,0:T(8,128)(2,1)S(1)}, bf16[400,128]{1,0:T(8,128)(2,1)S(1)}, u32[]{:S(2)}, u32[]{:S(2)}) collective-permute-start(bf16[400,128]{1,0:T(8,128)(2,1)S(1)} %get-tuple-element.34), channel_id=1, source_target_pairs={{0,8},{1,9},{2,10},{3,11},{4,12},{5,13},{6,14},{7,15},{8,0},{9,1},... | collective-permute-start | bytes 307208 | tf_op jit(solution)/shard_map/ppermute | solution.py:481
  25.5 3.1 %collective-permute-start.2 = (bf16[400,128]{1,0:T(8,128)(2,1)S(1)}, bf16[400,128]{1,0:T(8,128)(2,1)S(1)}, u32[]{:S(2)}, u32[]{:S(2)}) collective-permute-start(bf16[400,128]{1,0:T(8,128)(2,1)S(1)} %get-tuple-element.35), channel_id=1, source_target_pairs={{0,12},{1,13},{2,14},{3,15},{4,0},{5,1},{6,2},{7,3},{8,4},{9,5},{1... | collective-permute-start | bytes 307208 | tf_op jit(solution)/shard_map/ppermute | solution.py:481
  28.6 3.0 %collective-permute-done.1.qd2 = bf16[400,128]{1,0:T(8,128)(2,1)S(1)} collective-permute-done((bf16[400,128]{1,0:T(8,128)(2,1)S(1)}, bf16[400,128]{1,0:T(8,128)(2,1)S(1)}, u32[]{:S(2)}, u32[]{:S(2)}) %collective-permute-start.1) | collective-permute-done | bytes 102432 | tf_op jit(solution)/shard_map/ppermute | solution.py:481
  31.6 1.6 %collective-permute-done.2.qd3 = bf16[400,128]{1,0:T(8,128)(2,1)S(1)} collective-permute-done((bf16[400,128]{1,0:T(8,128)(2,1)S(1)}, bf16[400,128]{1,0:T(8,128)(2,1)S(1)}, u32[]{:S(2)}, u32[]{:S(2)}) %collective-permute-start.2) | collective-permute-done | bytes 102432 | tf_op jit(solution)/shard_map/ppermute | solution.py:481
  33.2 0.0 all-to-all-done.kv_own
  33.2 3.1 %collective-permute-start.3 = (bf16[8,384,128]{2,1,0:T(8,128)(2,1)S(1)}, bf16[8,384,128]{2,1,0:T(8,128)(2,1)S(1)}, u32[]{:S(2)}, u32[]{:S(2)}) collective-permute-start(bf16[8,384,128]{2,1,0:T(8,128)(2,1)S(1)} %all-to-all-done.kv_own), channel_id=1, source_target_pairs={{0,1},{1,0},{2,3},{3,2},{4,5},{5,4},{6,7},{7,6},{8,9},{9,8},{10,11... | collective-permute-start | bytes 2359304 | tf_op jit(solution)/shard_map/ppermute | solution.py:483
  36.3 1.9 %collective-permute-done.3.kv_other = bf16[8,384,128]{2,1,0:T(8,128)(2,1)S(1)} collective-permute-done((bf16[8,384,128]{2,1,0:T(8,128)(2,1)S(1)}, bf16[8,384,128]{2,1,0:T(8,128)(2,1)S(1)}, u32[]{:S(2)}, u32[]{:S(2)}) %collective-permute-start.3) | collective-permute-done | bytes 786464 | tf_op jit(solution)/shard_map/ppermute | solution.py:483
  38.2 0.9 copy-done.4
  39.1 6.9 %shard_map.111 = (bf16[8,384,128]{2,1,0:T(8,128)(2,1)S(1)}, bf16[8,384,128]{2,1,0:T(8,128)(2,1)S(1)}, bf16[4,400,128]{2,1,0:T(8,128)(2,1)}) custom-call(s32[1]{0:T(128)} %bitcast.core_ref, s32[1]{0:T(128)} %bitcast.1.x_ref, bf16[8,384,128]{2,1,0:T(8,128)(2,1)} %copy-done.4, bf16[400,128]{1,0:T(8,128)(2,1)S(1)} %get-tuple-element.37.qd0, ...), custom_call_target="tpu_custom_call" | custom-call | flops 4294967296 | bytes 5000000 | tf_op jit(solution)/shard_map/pallas_call | solution.py:383
  46.0 2.3 %collective-permute-start.4 = (bf16[8,384,128]{2,1,0:T(8,128)(2,1)S(1)}, bf16[8,384,128]{2,1,0:T(8,128)(2,1)S(1)}, u32[]{:S(2)}, u32[]{:S(2)}) collective-permute-start(bf16[8,384,128]{2,1,0:T(8,128)(2,1)S(1)} %get-tuple-element.45), channel_id=1, source_target_pairs={{0,1},{1,0},{2,3},{3,2},{4,5},{5,4},{6,7},{7,6},{8,9},{9,8},{10,11... | collective-permute-start | bytes 2359304 | tf_op jit(solution)/shard_map/ppermute | solution.py:488
  48.3 4.0 %all-to-all-start.1 = ((bf16[4,400,128]{2,1,0:T(8,128)(2,1)}), bf16[4,400,128]{2,1,0:T(8,128)(2,1)S(1)}, u32[]{:S(2)}, u32[]{:S(2)}) async-start(bf16[4,400,128]{2,1,0:T(8,128)(2,1)} %get-tuple-element.41), calls=%async_computation.1 | async-start | bytes 819200 | tf_op jit(solution)/shard_map/all_to_all | solution.py:487
  52.3 0.0 collective-permute-done.4.other_ref
  52.3 0.2 shard_map.113
  52.4 6.1 %collective-permute-start.5 = (bf16[4,384,128]{2,1,0:T(8,128)(2,1)S(1)}, bf16[4,384,128]{2,1,0:T(8,128)(2,1)S(1)}, u32[]{:S(2)}, u32[]{:S(2)}) collective-permute-start(bf16[4,384,128]{2,1,0:T(8,128)(2,1)S(1)} %get-tuple-element.47), channel_id=1, source_target_pairs={{0,2},{1,3},{2,0},{3,1},{4,6},{5,7},{6,4},{7,5},{8,10},{9,11},{10,... | collective-permute-start | bytes 1179656 | tf_op jit(solution)/shard_map/ppermute | solution.py:497
  58.6 1.6 %all-to-all-done.1.oq_ref = bf16[4,400,128]{2,1,0:T(8,128)(2,1)S(1)} async-done(((bf16[4,400,128]{2,1,0:T(8,128)(2,1)}), bf16[4,400,128]{2,1,0:T(8,128)(2,1)S(1)}, u32[]{:S(2)}, u32[]{:S(2)}) %all-to-all-start.1) | async-done | bytes 409632 | tf_op jit(solution)/shard_map/all_to_all | solution.py:487
  60.2 0.1 shard_map.114
  60.3 3.2 %collective-permute-start.6 = (f32[4,128]{1,0:T(4,128)S(1)}, f32[4,128]{1,0:T(4,128)S(1)}, u32[]{:S(2)}, u32[]{:S(2)}) collective-permute-start(f32[4,128]{1,0:T(4,128)S(1)} %shard_map.114), channel_id=1, source_target_pairs={{0,1},{1,0},{2,3},{3,2},{4,5},{5,4},{6,7},{7,6},{8,9},{9,8},{10,11... | collective-permute-start | bytes 6152 | tf_op jit(solution)/shard_map/ppermute | solution.py:502
  63.5 0.8 collective-permute-done.6
  64.4 28.8 %all_to_all.20.far_ref = f32[64,4,128]{2,1,0:T(4,128)S(1)} all-to-all(f32[64,4,128]{2,1,0:T(4,128)S(1)} %broadcast_in_dim.23), channel_id=1, replica_groups={{0,2,16,18,32,34,48,50,64,66,80,82,96,98,112,114,128,130,144,146,160,16..., dimensions={0} | all-to-all | bytes 262144 | tf_op jit(solution)/shard_map/all_to_all | solution.py:504
  93.1 0.9 shard_map.115
  94.0 3.5 %all-to-all-start.3 = ((bf16[4,400,128]{2,1,0:T(8,128)(2,1)}), bf16[4,400,128]{2,1,0:T(8,128)(2,1)S(1)}, u32[]{:S(2)}, u32[]{:S(2)}) async-start(bf16[4,400,128]{2,1,0:T(8,128)(2,1)} %shard_map.115), calls=%async_computation.3 | async-start | bytes 819200 | tf_op jit(solution)/shard_map/all_to_all | solution.py:516
  97.4 1.1 %shard_map.112 = (bf16[128,768]{1,0:T(8,128)(2,1)}, bf16[128,768]{1,0:T(8,128)(2,1)}, bf16[8,128,128]{2,1,0:T(8,128)(2,1)}) custom-call(bf16[4,400,128]{2,1,0:T(8,128)(2,1)S(1)} %all-to-all-done.1.oq_ref, f32[4,128]{1,0:T(4,128)S(1)} %bitcast.20), custom_call_target="tpu_custom_call" | custom-call | flops 4194304 | bytes 1100000 | tf_op jit(solution)/shard_map/pallas_call | solution.py:383
  98.5 5.2 %all-to-all-done.3.dkv_ref = bf16[4,400,128]{2,1,0:T(8,128)(2,1)S(1)} async-done(((bf16[4,400,128]{2,1,0:T(8,128)(2,1)}), bf16[4,400,128]{2,1,0:T(8,128)(2,1)S(1)}, u32[]{:S(2)}, u32[]{:S(2)}) %all-to-all-start.3) | async-done | bytes 409632 | tf_op jit(solution)/shard_map/all_to_all | solution.py:516
  103.7 0.9 shard_map.116
  (9 shorter events, 0.0 us)
Async XLA Ops:
  2.7 13.5 %copy-start = (bf16[1,8,128,128]{3,2,1,0:T(8,128)(2,1)S(1)}, bf16[1,8,128,128]{3,2,1,0:T(8,128)(2,1)}, u32[]{:S(2)}) copy-start(bf16[1,8,128,128]{3,2,1,0:T(8,128)(2,1)} %param.10) | copy-start | bytes 786436
  2.7 13.5 %copy-start.1 = (bf16[1,128,768]{2,1,0:T(8,128)(2,1)S(1)}, bf16[1,128,768]{2,1,0:T(8,128)(2,1)}, u32[]{:S(2)}) copy-start(bf16[1,128,768]{2,1,0:T(8,128)(2,1)} %param.6) | copy-start | bytes 589828
  2.7 13.5 %copy-start.2 = (bf16[1,128,768]{2,1,0:T(8,128)(2,1)S(1)}, bf16[1,128,768]{2,1,0:T(8,128)(2,1)}, u32[]{:S(2)}) copy-start(bf16[1,128,768]{2,1,0:T(8,128)(2,1)} %param.9) | copy-start | bytes 589828
  2.7 30.5 %all-to-all-start = ((bf16[8,384,128]{2,1,0:T(8,128)(2,1)}), bf16[8,384,128]{2,1,0:T(8,128)(2,1)S(1)}, u32[]{:S(2)}, u32[]{:S(2)}) async-start(bf16[8,384,128]{2,1,0:T(8,128)(2,1)} %shard_map.109), calls=%async_computation | async-start | bytes 1572864 | tf_op jit(solution)/shard_map/all_to_all | solution.py:462
  16.2 0.7 copy-start.3
  17.8 10.8 %collective-permute-start = (bf16[400,128]{1,0:T(8,128)(2,1)S(1)}, bf16[400,128]{1,0:T(8,128)(2,1)S(1)}, u32[]{:S(2)}, u32[]{:S(2)}) collective-permute-start(bf16[400,128]{1,0:T(8,128)(2,1)S(1)} %get-tuple-element.33), channel_id=1, source_target_pairs={{0,4},{1,5},{2,6},{3,7},{4,8},{5,9},{6,10},{7,11},{8,12},{9,13},{1... | collective-permute-start | bytes 307208 | tf_op jit(solution)/shard_map/ppermute | solution.py:481
  21.2 10.4 %collective-permute-start.1 = (bf16[400,128]{1,0:T(8,128)(2,1)S(1)}, bf16[400,128]{1,0:T(8,128)(2,1)S(1)}, u32[]{:S(2)}, u32[]{:S(2)}) collective-permute-start(bf16[400,128]{1,0:T(8,128)(2,1)S(1)} %get-tuple-element.34), channel_id=1, source_target_pairs={{0,8},{1,9},{2,10},{3,11},{4,12},{5,13},{6,14},{7,15},{8,0},{9,1},... | collective-permute-start | bytes 307208 | tf_op jit(solution)/shard_map/ppermute | solution.py:481
  25.5 7.7 %collective-permute-start.2 = (bf16[400,128]{1,0:T(8,128)(2,1)S(1)}, bf16[400,128]{1,0:T(8,128)(2,1)S(1)}, u32[]{:S(2)}, u32[]{:S(2)}) collective-permute-start(bf16[400,128]{1,0:T(8,128)(2,1)S(1)} %get-tuple-element.35), channel_id=1, source_target_pairs={{0,12},{1,13},{2,14},{3,15},{4,0},{5,1},{6,2},{7,3},{8,4},{9,5},{1... | collective-permute-start | bytes 307208 | tf_op jit(solution)/shard_map/ppermute | solution.py:481
  33.2 5.0 %collective-permute-start.3 = (bf16[8,384,128]{2,1,0:T(8,128)(2,1)S(1)}, bf16[8,384,128]{2,1,0:T(8,128)(2,1)S(1)}, u32[]{:S(2)}, u32[]{:S(2)}) collective-permute-start(bf16[8,384,128]{2,1,0:T(8,128)(2,1)S(1)} %all-to-all-done.kv_own), channel_id=1, source_target_pairs={{0,1},{1,0},{2,3},{3,2},{4,5},{5,4},{6,7},{7,6},{8,9},{9,8},{10,11... | collective-permute-start | bytes 2359304 | tf_op jit(solution)/shard_map/ppermute | solution.py:483
  38.2 0.9 copy-start.4
  46.0 6.3 %collective-permute-start.4 = (bf16[8,384,128]{2,1,0:T(8,128)(2,1)S(1)}, bf16[8,384,128]{2,1,0:T(8,128)(2,1)S(1)}, u32[]{:S(2)}, u32[]{:S(2)}) collective-permute-start(bf16[8,384,128]{2,1,0:T(8,128)(2,1)S(1)} %get-tuple-element.45), channel_id=1, source_target_pairs={{0,1},{1,0},{2,3},{3,2},{4,5},{5,4},{6,7},{7,6},{8,9},{9,8},{10,11... | collective-permute-start | bytes 2359304 | tf_op jit(solution)/shard_map/ppermute | solution.py:488
  48.3 11.9 %all-to-all-start.1 = ((bf16[4,400,128]{2,1,0:T(8,128)(2,1)}), bf16[4,400,128]{2,1,0:T(8,128)(2,1)S(1)}, u32[]{:S(2)}, u32[]{:S(2)}) async-start(bf16[4,400,128]{2,1,0:T(8,128)(2,1)} %get-tuple-element.41), calls=%async_computation.1 | async-start | bytes 819200 | tf_op jit(solution)/shard_map/all_to_all | solution.py:487
  52.4 40.7 %collective-permute-start.5 = (bf16[4,384,128]{2,1,0:T(8,128)(2,1)S(1)}, bf16[4,384,128]{2,1,0:T(8,128)(2,1)S(1)}, u32[]{:S(2)}, u32[]{:S(2)}) collective-permute-start(bf16[4,384,128]{2,1,0:T(8,128)(2,1)S(1)} %get-tuple-element.47), channel_id=1, source_target_pairs={{0,2},{1,3},{2,0},{3,1},{4,6},{5,7},{6,4},{7,5},{8,10},{9,11},{10,... | collective-permute-start | bytes 1179656 | tf_op jit(solution)/shard_map/ppermute | solution.py:497
  60.3 4.0 %collective-permute-start.6 = (f32[4,128]{1,0:T(4,128)S(1)}, f32[4,128]{1,0:T(4,128)S(1)}, u32[]{:S(2)}, u32[]{:S(2)}) collective-permute-start(f32[4,128]{1,0:T(4,128)S(1)} %shard_map.114), channel_id=1, source_target_pairs={{0,1},{1,0},{2,3},{3,2},{4,5},{5,4},{6,7},{7,6},{8,9},{9,8},{10,11... | collective-permute-start | bytes 6152 | tf_op jit(solution)/shard_map/ppermute | solution.py:502
  94.0 9.8 %all-to-all-start.3 = ((bf16[4,400,128]{2,1,0:T(8,128)(2,1)}), bf16[4,400,128]{2,1,0:T(8,128)(2,1)S(1)}, u32[]{:S(2)}, u32[]{:S(2)}) async-start(bf16[4,400,128]{2,1,0:T(8,128)(2,1)} %shard_map.115), calls=%async_computation.3 | async-start | bytes 819200 | tf_op jit(solution)/shard_map/all_to_all | solution.py:516

commit v4 on v3

--- a/solution.py
+++ b/solution.py
@@ -267,7 +267,7 @@
             block = oq_ref[head, 384:400, :].astype(F32)[part * 8 : part * 8 + 8]
             rows.append(jnp.concatenate([block[i : i + 1] for i in range(PROW)], axis=1))
     prod = nn(jnp.concatenate(rows, axis=0).astype(BF), pair_ref[...].reshape(PROW * PAIRS, 128))
-    out_ref[...] = prod[0:4] + prod[4:8]
+    out_ref[...] = jnp.broadcast_to((prod[0:4] + prod[4:8])[None], out_ref.shape)
 
 
 def grads_kernel(
@@ -318,15 +318,10 @@
         keep_ref[x] = own_ref[here].astype(F32) + other_ref[here].astype(F32)
 
 
-def merge_kernel(keep_ref, come_ref, far_ref, out_ref):
-    total = jnp.sum(far_ref[...], axis=0)
-    hi = total.astype(BF).astype(F32)
-    rest = total - hi
-    mid = rest.astype(BF).astype(F32)
-    rows = jnp.concatenate([hi, mid, rest - mid, jnp.zeros((4, 128), F32)], axis=0).astype(BF)
-    for x in range(XS):
-        out_ref[x, 0:384, :] = (keep_ref[x] + come_ref[x].astype(F32)).astype(BF)
-        out_ref[x, 384:400, :] = rows
+def merge_kernel(x_ref, keep_ref, come_ref, out0, out1, out2, out3):
+    for k, out in enumerate((out0, out1, out2, out3)):
+        to = lax.rem(x_ref[0] + k, XS)
+        out[...] = (keep_ref[to] + come_ref[to].astype(F32)).astype(BF)
 
 
 def put(ref, fulls, halves):
@@ -360,17 +355,16 @@
         gp_ref[i] = nn(grads.T.astype(BF), wrows).astype(BF)
 
 
-def key_kernel(dkv_ref, dk_ref, dv_ref, gw_ref):
+def key_kernel(x_ref, in0, in1, in2, in3, far_ref, dk_ref, dv_ref, gw_ref, staged):
+    gw_ref[...] = jnp.sum(far_ref[...], axis=0)
+    for k, ref in enumerate((in0, in1, in2, in3)):
+        staged[lax.rem(x_ref[0] + XS - k, XS)] = ref[...]
     for base, ref in ((0, dk_ref), (1, dv_ref)):
         put(
             ref,
-            [dkv_ref[h, base * 128 : (base + 1) * 128, :] for h in range(HEADS)],
-            [dkv_ref[h, 256 + base * 64 : 320 + base * 64, :].astype(F32) for h in range(HEADS)],
+            [staged[h, base * 128 : (base + 1) * 128, :] for h in range(HEADS)],
+            [staged[h, 256 + base * 64 : 320 + base * 64, :].astype(F32) for h in range(HEADS)],
         )
-    total = jnp.zeros((16, 128), F32)
-    for x in range(XS):
-        total += dkv_ref[x, 384:400, :].astype(F32)
-    gw_ref[...] = (total[8:12] + total[4:8]) + total[0:4]
 
 
 def shape(*dims, dtype=BF):
@@ -423,6 +417,7 @@
 def body(dp, queries, keys, values, cotangent, pair, pair_weight):
     xz_groups = [[seq_index(x, z, c) for x in range(XS) for z in range(ZS)] for c in range(CS)]
     x_groups = [[seq_index(x, z, c) for x in range(XS)] for z in range(ZS) for c in range(CS)]
+    xc_groups = [[seq_index(x, z, c) for x in range(XS) for c in range(CS)] for z in range(ZS)]
     far_groups = [
         [d * 16 + seq_index(x, z, c) for d in range(dp) for z in range(ZS)]
         for x in range(XS)
@@ -482,7 +477,6 @@
     kv_own, qd = lax.optimization_barrier((kv_own, qd))
     kv_other = lax.ppermute(kv_own, "seq", swap)
     kv_other = pltpu.with_memory_space_constraint(kv_other, pltpu.MemorySpace.HBM)
-    count = dp * ZS
     dkv_own, dkv_other, oq = attention(core, own_x, kv_other, *qd, kv_own)
     oq = lax.all_to_all(oq, "seq", 0, 0, axis_index_groups=x_groups)
     dkv_swapped = lax.ppermute(dkv_other, "seq", swap)
@@ -495,13 +489,14 @@
         limit=8,
     )
     come = lax.ppermute(send, "seq", across)
-    term = call(
-        weight_kernel, shape(HEADS, 128, dtype=F32), (oq, pair_rows),
+    total = call(
+        weight_kernel, shape(XS * CS, HEADS, 128, dtype=F32), (oq, pair_rows),
         flops=2 * 1024 * 128 * 8, moved=500_000, limit=8,
     )
-    term = term + lax.ppermute(term, "seq", swap)
-    spread = jnp.broadcast_to(term[None], (count, HEADS, 128))
-    far = lax.all_to_all(spread, ("dp", "seq"), 0, 0, axis_index_groups=far_groups)
+    total = lax.all_to_all(total, "seq", 0, 0, axis_index_groups=xc_groups).sum(axis=0)
+    total, keep = lax.optimization_barrier((total, keep))
+    far = jnp.broadcast_to(total[None], (len(far_groups[0]), HEADS, 128))
+    far = lax.all_to_all(far, ("dp", "seq"), 0, 0, axis_index_groups=far_groups)
     att, dq, gp = call(
         query_kernel,
         (shape(128, 768), shape(128, 768), shape(PROW, PAIRS, 128)),
@@ -511,13 +506,20 @@
         limit=8,
     )
     dkv = call(
-        merge_kernel, shape(XS, 400, 128), (keep, come, far), moved=1_600_000, limit=8
-    )
-    dkv_back = lax.all_to_all(dkv, "seq", 0, 0, axis_index_groups=x_groups)
+        merge_kernel,
+        (shape(384, 128),) * XS,
+        (own_x, keep, come),
+        smem=1,
+        moved=1_600_000,
+        limit=8,
+    )
+    dkv = [dkv[0]] + [lax.ppermute(dkv[k], "seq", ring(k)) for k in range(1, XS)]
     dk, dv, gw = call(
         key_kernel,
         (shape(128, 768), shape(128, 768), shape(HEADS, 128, dtype=F32)),
-        (dkv_back,),
+        (own_x, *dkv, far),
+        smem=1,
+        scratch=(pltpu.VMEM((HEADS, 384, 128), BF),),
         moved=800_000,
         limit=8,
     )

time: 106 us -> 100 us (0.943)
  blocking collectives: 28.8 us -> 8.66 us
  starting transfers between devices: 46.3 us -> 65.3 us
  waiting for transfers between devices: 14.1 us -> 10.2 us
    all_to_all x1, blocking collectives: 28.8 us -> 8.66 us  [body(): lax.all_to_all(total, 'seq', 0, 0, axis_index_groups=xc_groups).sum(axis=0)]
    all_to_all x1, starting transfers between devices: 3.46 us -> 16.9 us  [body(): far = lax.all_to_all(far, ('dp', 'seq'), 0, 0, axis_index_groups=far_groups)]
    ppermute x1 -> x3, starting transfers between devices: 3.17 us -> 8.65 us  [body(): lax.ppermute(dkv[k], 'seq', ring(k))]
    all_to_all x1, waiting for transfers between devices: 5.2 us -> 2.12 us  [body(): far = lax.all_to_all(far, ('dp', 'seq'), 0, 0, axis_index_groups=far_groups)]
  transfers between devices with their start and end apart: 10 -> 12, of which waited for: 6 -> 5; matrix products, arithmetic and copies ran while one was open for 0% -> 1% of each run, Pallas kernels for 2% -> 2%
where the time goes in v4:
time: 100 us; the launch traced here: 99.5 us
  starting transfers between devices  65.3 us (65%)
  Pallas kernels  12.3 us (12%)
  waiting for transfers between devices  10.2 us (10%)
  blocking collectives  8.66 us (9%)
  local copies, waits for them, and re-layouts  2.23 us (2%)
    all_to_all x1, starting transfers between devices, body(): far = lax.all_to_all(far, ('dp', 'seq'), 0, 0, axis_index_groups=far_groups)  16.9 us
    all_to_all x1, starting transfers between devices, body(): kv_own = lax.all_to_all(kv, 'seq', 0, 0, axis_index_groups=xz_groups)  13.4 us
    pallas_call x8, Pallas kernels, call(): pl.pallas_call(kernel, out_shape=out_shape, in_specs=[SMEM] * smem + [ANY...  12.3 us
    ppermute x3, starting transfers between devices, body(): qd = [qd[0]] + [lax.ppermute(qd[k], 'seq', ring(k)) for k in range(1, XS)]  10.8 us
    all_to_all x1, blocking collectives, body(): lax.all_to_all(total, 'seq', 0, 0, axis_index_groups=xc_groups).sum(axis=0)  8.66 us
    ppermute x3, starting transfers between devices, body(): lax.ppermute(dkv[k], 'seq', ring(k))  8.65 us
    ppermute x1, starting transfers between devices, body(): come = lax.ppermute(send, 'seq', across)  6.15 us
    ppermute x3, waiting for transfers between devices, body(): qd = [qd[0]] + [lax.ppermute(qd[k], 'seq', ring(k)) for k in range(1, XS)]  4.59 us
  transfers between devices with their start and end apart: 12, of which 5 were waited for; matrix products, arithmetic and copies ran while one was open for 1% of the time, Pallas kernels for 2%

profile of v4, /device:TPU:1, one launch (start us, length us, event | category | flops | bytes accessed | tf_op | source)
XLA Modules:
  0.0 99.5 jit_solution(6423464284808726064)
XLA Ops:
  0.6 2.0 %shard_map.109 = bf16[8,384,128]{2,1,0:T(8,128)(2,1)} custom-call(bf16[128,768]{1,0:T(8,128)(2,1)} %bitcast.21, bf16[128,768]{1,0:T(8,128)(2,1)} %bitcast.22), custom_call_target="tpu_custom_call" | custom-call | bytes 1500000 | tf_op jit(solution)/shard_map/pallas_call | solution.py:377
  2.7 0.0 copy-start
  2.7 0.0 copy-start.1
  2.7 0.0 copy-start.2
  2.7 13.4 %all-to-all-start = ((bf16[8,384,128]{2,1,0:T(8,128)(2,1)}), bf16[8,384,128]{2,1,0:T(8,128)(2,1)S(1)}, u32[]{:S(2)}, u32[]{:S(2)}) async-start(bf16[8,384,128]{2,1,0:T(8,128)(2,1)} %shard_map.109), calls=%async_computation | async-start | bytes 1572864 | tf_op jit(solution)/shard_map/all_to_all | solution.py:457
  16.2 0.6 copy-done.3
  16.8 1.0 shard_map.110
  17.8 3.4 %collective-permute-start = (bf16[400,128]{1,0:T(8,128)(2,1)S(1)}, bf16[400,128]{1,0:T(8,128)(2,1)S(1)}, u32[]{:S(2)}, u32[]{:S(2)}) collective-permute-start(bf16[400,128]{1,0:T(8,128)(2,1)S(1)} %get-tuple-element.39), channel_id=1, source_target_pairs={{0,4},{1,5},{2,6},{3,7},{4,8},{5,9},{6,10},{7,11},{8,12},{9,13},{1... | collective-permute-start | bytes 307208 | tf_op jit(solution)/shard_map/ppermute | solution.py:476
  21.2 4.3 %collective-permute-start.1 = (bf16[400,128]{1,0:T(8,128)(2,1)S(1)}, bf16[400,128]{1,0:T(8,128)(2,1)S(1)}, u32[]{:S(2)}, u32[]{:S(2)}) collective-permute-start(bf16[400,128]{1,0:T(8,128)(2,1)S(1)} %get-tuple-element.40), channel_id=1, source_target_pairs={{0,8},{1,9},{2,10},{3,11},{4,12},{5,13},{6,14},{7,15},{8,0},{9,1},... | collective-permute-start | bytes 307208 | tf_op jit(solution)/shard_map/ppermute | solution.py:476
  25.5 3.1 %collective-permute-start.2 = (bf16[400,128]{1,0:T(8,128)(2,1)S(1)}, bf16[400,128]{1,0:T(8,128)(2,1)S(1)}, u32[]{:S(2)}, u32[]{:S(2)}) collective-permute-start(bf16[400,128]{1,0:T(8,128)(2,1)S(1)} %get-tuple-element.41), channel_id=1, source_target_pairs={{0,12},{1,13},{2,14},{3,15},{4,0},{5,1},{6,2},{7,3},{8,4},{9,5},{1... | collective-permute-start | bytes 307208 | tf_op jit(solution)/shard_map/ppermute | solution.py:476
  28.6 3.0 %collective-permute-done.1.qd2 = bf16[400,128]{1,0:T(8,128)(2,1)S(1)} collective-permute-done((bf16[400,128]{1,0:T(8,128)(2,1)S(1)}, bf16[400,128]{1,0:T(8,128)(2,1)S(1)}, u32[]{:S(2)}, u32[]{:S(2)}) %collective-permute-start.1) | collective-permute-done | bytes 102432 | tf_op jit(solution)/shard_map/ppermute | solution.py:476
  31.6 1.6 %collective-permute-done.2.qd3 = bf16[400,128]{1,0:T(8,128)(2,1)S(1)} collective-permute-done((bf16[400,128]{1,0:T(8,128)(2,1)S(1)}, bf16[400,128]{1,0:T(8,128)(2,1)S(1)}, u32[]{:S(2)}, u32[]{:S(2)}) %collective-permute-start.2) | collective-permute-done | bytes 102432 | tf_op jit(solution)/shard_map/ppermute | solution.py:476
  33.2 3.1 %collective-permute-start.3 = (bf16[8,384,128]{2,1,0:T(8,128)(2,1)S(1)}, bf16[8,384,128]{2,1,0:T(8,128)(2,1)S(1)}, u32[]{:S(2)}, u32[]{:S(2)}) collective-permute-start(bf16[8,384,128]{2,1,0:T(8,128)(2,1)S(1)} %all-to-all-done.kv_own), channel_id=1, source_target_pairs={{0,1},{1,0},{2,3},{3,2},{4,5},{5,4},{6,7},{7,6},{8,9},{9,8},{10,11... | collective-permute-start | bytes 2359304 | tf_op jit(solution)/shard_map/ppermute | solution.py:478
  36.3 1.9 %collective-permute-done.3.kv_other = bf16[8,384,128]{2,1,0:T(8,128)(2,1)S(1)} collective-permute-done((bf16[8,384,128]{2,1,0:T(8,128)(2,1)S(1)}, bf16[8,384,128]{2,1,0:T(8,128)(2,1)S(1)}, u32[]{:S(2)}, u32[]{:S(2)}) %collective-permute-start.3) | collective-permute-done | bytes 786464 | tf_op jit(solution)/shard_map/ppermute | solution.py:478
  38.2 0.9 copy-done.4
  39.1 6.9 %shard_map.111 = (bf16[8,384,128]{2,1,0:T(8,128)(2,1)S(1)}, bf16[8,384,128]{2,1,0:T(8,128)(2,1)S(1)}, bf16[4,400,128]{2,1,0:T(8,128)(2,1)}) custom-call(s32[1]{0:T(128)} %bitcast.core_ref, s32[1]{0:T(128)} %bitcast.1.x_ref, bf16[8,384,128]{2,1,0:T(8,128)(2,1)} %copy-done.4, bf16[400,128]{1,0:T(8,128)(2,1)S(1)} %get-tuple-element.43.qd0, ...), custom_call_target="tpu_custom_call" | custom-call | flops 4294967296 | bytes 5000000 | tf_op jit(solution)/shard_map/pallas_call | solution.py:377
  46.0 2.3 %collective-permute-start.4 = (bf16[8,384,128]{2,1,0:T(8,128)(2,1)S(1)}, bf16[8,384,128]{2,1,0:T(8,128)(2,1)S(1)}, u32[]{:S(2)}, u32[]{:S(2)}) collective-permute-start(bf16[8,384,128]{2,1,0:T(8,128)(2,1)S(1)} %get-tuple-element.51), channel_id=1, source_target_pairs={{0,1},{1,0},{2,3},{3,2},{4,5},{5,4},{6,7},{7,6},{8,9},{9,8},{10,11... | collective-permute-start | bytes 2359304 | tf_op jit(solution)/shard_map/ppermute | solution.py:482
  48.3 4.0 %all-to-all-start.1 = ((bf16[4,400,128]{2,1,0:T(8,128)(2,1)}), bf16[4,400,128]{2,1,0:T(8,128)(2,1)S(1)}, u32[]{:S(2)}, u32[]{:S(2)}) async-start(bf16[4,400,128]{2,1,0:T(8,128)(2,1)} %get-tuple-element.47), calls=%async_computation.1 | async-start | bytes 819200 | tf_op jit(solution)/shard_map/all_to_all | solution.py:481
  52.2 0.2 shard_map.114
  52.4 6.1 %collective-permute-start.5 = (bf16[4,384,128]{2,1,0:T(8,128)(2,1)S(1)}, bf16[4,384,128]{2,1,0:T(8,128)(2,1)S(1)}, u32[]{:S(2)}, u32[]{:S(2)}) collective-permute-start(bf16[4,384,128]{2,1,0:T(8,128)(2,1)S(1)} %get-tuple-element.54), channel_id=1, source_target_pairs={{0,2},{1,3},{2,0},{3,1},{4,6},{5,7},{6,4},{7,5},{8,10},{9,11},{10,... | collective-permute-start | bytes 1179656 | tf_op jit(solution)/shard_map/ppermute | solution.py:491
  58.6 1.6 %all-to-all-done.1.oq_ref = bf16[4,400,128]{2,1,0:T(8,128)(2,1)S(1)} async-done(((bf16[4,400,128]{2,1,0:T(8,128)(2,1)}), bf16[4,400,128]{2,1,0:T(8,128)(2,1)S(1)}, u32[]{:S(2)}, u32[]{:S(2)}) %all-to-all-start.1) | async-done | bytes 409632 | tf_op jit(solution)/shard_map/all_to_all | solution.py:481
  60.2 0.1 shard_map.113
  60.3 8.7 %all_to_all.20 = f32[8,4,128]{2,1,0:T(4,128)S(1)} all-to-all(f32[8,4,128]{2,1,0:T(4,128)S(1)} %shard_map.113), channel_id=1, replica_groups={{0,1,4,5,8,9,12,13},{2,3,6,7,10,11,14,15},{16,17,20,21,24,25,28,29},{18..., dimensions={0} | all-to-all | bytes 32768 | tf_op jit(solution)/shard_map/all_to_all | solution.py:496
  69.0 0.7 broadcast_in_dim.23
  69.7 16.9 %all-to-all-start.3 = ((f32[64,4,128]{2,1,0:T(4,128)}), f32[64,4,128]{2,1,0:T(4,128)S(1)}, u32[]{:S(2)}, u32[]{:S(2)}) async-start(f32[64,4,128]{2,1,0:T(4,128)} %broadcast_in_dim.23), calls=%async_computation.3 | async-start | bytes 262144 | tf_op jit(solution)/shard_map/all_to_all | solution.py:499
  86.6 0.1 shard_map.115
  86.7 2.2 %collective-permute-start.6 = (bf16[384,128]{1,0:T(8,128)(2,1)S(1)}, bf16[384,128]{1,0:T(8,128)(2,1)S(1)}, u32[]{:S(2)}, u32[]{:S(2)}) collective-permute-start(bf16[384,128]{1,0:T(8,128)(2,1)S(1)} %get-tuple-element.56), channel_id=1, source_target_pairs={{0,4},{1,5},{2,6},{3,7},{4,8},{5,9},{6,10},{7,11},{8,12},{9,13},{1... | collective-permute-start | bytes 294920 | tf_op jit(solution)/shard_map/ppermute | solution.py:516
  88.9 3.7 %collective-permute-start.7 = (bf16[384,128]{1,0:T(8,128)(2,1)S(1)}, bf16[384,128]{1,0:T(8,128)(2,1)S(1)}, u32[]{:S(2)}, u32[]{:S(2)}) collective-permute-start(bf16[384,128]{1,0:T(8,128)(2,1)S(1)} %get-tuple-element.57), channel_id=1, source_target_pairs={{0,8},{1,9},{2,10},{3,11},{4,12},{5,13},{6,14},{7,15},{8,0},{9,1},... | collective-permute-start | bytes 294920 | tf_op jit(solution)/shard_map/ppermute | solution.py:516
  92.6 2.8 %collective-permute-start.8 = (bf16[384,128]{1,0:T(8,128)(2,1)S(1)}, bf16[384,128]{1,0:T(8,128)(2,1)S(1)}, u32[]{:S(2)}, u32[]{:S(2)}) collective-permute-start(bf16[384,128]{1,0:T(8,128)(2,1)S(1)} %get-tuple-element.58), channel_id=1, source_target_pairs={{0,12},{1,13},{2,14},{3,15},{4,0},{5,1},{6,2},{7,3},{8,4},{9,5},{1... | collective-permute-start | bytes 294920 | tf_op jit(solution)/shard_map/ppermute | solution.py:516
  95.4 1.1 %shard_map.112 = (bf16[128,768]{1,0:T(8,128)(2,1)}, bf16[128,768]{1,0:T(8,128)(2,1)}, bf16[8,128,128]{2,1,0:T(8,128)(2,1)}) custom-call(bf16[4,400,128]{2,1,0:T(8,128)(2,1)S(1)} %all-to-all-done.1.oq_ref, f32[4,128]{1,0:T(4,128)S(1)} %bitcast.20), custom_call_target="tpu_custom_call" | custom-call | flops 4194304 | bytes 1100000 | tf_op jit(solution)/shard_map/pallas_call | solution.py:377
  96.5 2.1 %all-to-all-done.3.far_ref = f32[64,4,128]{2,1,0:T(4,128)S(1)} async-done(((f32[64,4,128]{2,1,0:T(4,128)}), f32[64,4,128]{2,1,0:T(4,128)S(1)}, u32[]{:S(2)}, u32[]{:S(2)}) %all-to-all-start.3) | async-done | bytes 131104 | tf_op jit(solution)/shard_map/all_to_all | solution.py:499
  98.6 0.9 shard_map.116
  (13 shorter events, 0.0 us)
Async XLA Ops:
  2.7 13.5 %copy-start = (bf16[1,8,128,128]{3,2,1,0:T(8,128)(2,1)S(1)}, bf16[1,8,128,128]{3,2,1,0:T(8,128)(2,1)}, u32[]{:S(2)}) copy-start(bf16[1,8,128,128]{3,2,1,0:T(8,128)(2,1)} %param.10) | copy-start | bytes 786436
  2.7 13.5 %copy-start.1 = (bf16[1,128,768]{2,1,0:T(8,128)(2,1)S(1)}, bf16[1,128,768]{2,1,0:T(8,128)(2,1)}, u32[]{:S(2)}) copy-start(bf16[1,128,768]{2,1,0:T(8,128)(2,1)} %param.6) | copy-start | bytes 589828
  2.7 13.5 %copy-start.2 = (bf16[1,128,768]{2,1,0:T(8,128)(2,1)S(1)}, bf16[1,128,768]{2,1,0:T(8,128)(2,1)}, u32[]{:S(2)}) copy-start(bf16[1,128,768]{2,1,0:T(8,128)(2,1)} %param.9) | copy-start | bytes 589828
  2.7 30.5 %all-to-all-start = ((bf16[8,384,128]{2,1,0:T(8,128)(2,1)}), bf16[8,384,128]{2,1,0:T(8,128)(2,1)S(1)}, u32[]{:S(2)}, u32[]{:S(2)}) async-start(bf16[8,384,128]{2,1,0:T(8,128)(2,1)} %shard_map.109), calls=%async_computation | async-start | bytes 1572864 | tf_op jit(solution)/shard_map/all_to_all | solution.py:457
  16.2 0.7 copy-start.3
  17.8 10.8 %collective-permute-start = (bf16[400,128]{1,0:T(8,128)(2,1)S(1)}, bf16[400,128]{1,0:T(8,128)(2,1)S(1)}, u32[]{:S(2)}, u32[]{:S(2)}) collective-permute-start(bf16[400,128]{1,0:T(8,128)(2,1)S(1)} %get-tuple-element.39), channel_id=1, source_target_pairs={{0,4},{1,5},{2,6},{3,7},{4,8},{5,9},{6,10},{7,11},{8,12},{9,13},{1... | collective-permute-start | bytes 307208 | tf_op jit(solution)/shard_map/ppermute | solution.py:476
  21.2 10.4 %collective-permute-start.1 = (bf16[400,128]{1,0:T(8,128)(2,1)S(1)}, bf16[400,128]{1,0:T(8,128)(2,1)S(1)}, u32[]{:S(2)}, u32[]{:S(2)}) collective-permute-start(bf16[400,128]{1,0:T(8,128)(2,1)S(1)} %get-tuple-element.40), channel_id=1, source_target_pairs={{0,8},{1,9},{2,10},{3,11},{4,12},{5,13},{6,14},{7,15},{8,0},{9,1},... | collective-permute-start | bytes 307208 | tf_op jit(solution)/shard_map/ppermute | solution.py:476
  25.5 7.7 %collective-permute-start.2 = (bf16[400,128]{1,0:T(8,128)(2,1)S(1)}, bf16[400,128]{1,0:T(8,128)(2,1)S(1)}, u32[]{:S(2)}, u32[]{:S(2)}) collective-permute-start(bf16[400,128]{1,0:T(8,128)(2,1)S(1)} %get-tuple-element.41), channel_id=1, source_target_pairs={{0,12},{1,13},{2,14},{3,15},{4,0},{5,1},{6,2},{7,3},{8,4},{9,5},{1... | collective-permute-start | bytes 307208 | tf_op jit(solution)/shard_map/ppermute | solution.py:476
  33.2 5.0 %collective-permute-start.3 = (bf16[8,384,128]{2,1,0:T(8,128)(2,1)S(1)}, bf16[8,384,128]{2,1,0:T(8,128)(2,1)S(1)}, u32[]{:S(2)}, u32[]{:S(2)}) collective-permute-start(bf16[8,384,128]{2,1,0:T(8,128)(2,1)S(1)} %all-to-all-done.kv_own), channel_id=1, source_target_pairs={{0,1},{1,0},{2,3},{3,2},{4,5},{5,4},{6,7},{7,6},{8,9},{9,8},{10,11... | collective-permute-start | bytes 2359304 | tf_op jit(solution)/shard_map/ppermute | solution.py:478
  38.2 0.9 copy-start.4
  46.0 6.3 %collective-permute-start.4 = (bf16[8,384,128]{2,1,0:T(8,128)(2,1)S(1)}, bf16[8,384,128]{2,1,0:T(8,128)(2,1)S(1)}, u32[]{:S(2)}, u32[]{:S(2)}) collective-permute-start(bf16[8,384,128]{2,1,0:T(8,128)(2,1)S(1)} %get-tuple-element.51), channel_id=1, source_target_pairs={{0,1},{1,0},{2,3},{3,2},{4,5},{5,4},{6,7},{7,6},{8,9},{9,8},{10,11... | collective-permute-start | bytes 2359304 | tf_op jit(solution)/shard_map/ppermute | solution.py:482
  48.3 11.9 %all-to-all-start.1 = ((bf16[4,400,128]{2,1,0:T(8,128)(2,1)}), bf16[4,400,128]{2,1,0:T(8,128)(2,1)S(1)}, u32[]{:S(2)}, u32[]{:S(2)}) async-start(bf16[4,400,128]{2,1,0:T(8,128)(2,1)} %get-tuple-element.47), calls=%async_computation.1 | async-start | bytes 819200 | tf_op jit(solution)/shard_map/all_to_all | solution.py:481
  52.4 34.2 %collective-permute-start.5 = (bf16[4,384,128]{2,1,0:T(8,128)(2,1)S(1)}, bf16[4,384,128]{2,1,0:T(8,128)(2,1)S(1)}, u32[]{:S(2)}, u32[]{:S(2)}) collective-permute-start(bf16[4,384,128]{2,1,0:T(8,128)(2,1)S(1)} %get-tuple-element.54), channel_id=1, source_target_pairs={{0,2},{1,3},{2,0},{3,1},{4,6},{5,7},{6,4},{7,5},{8,10},{9,11},{10,... | collective-permute-start | bytes 1179656 | tf_op jit(solution)/shard_map/ppermute | solution.py:491
  69.7 28.9 %all-to-all-start.3 = ((f32[64,4,128]{2,1,0:T(4,128)}), f32[64,4,128]{2,1,0:T(4,128)S(1)}, u32[]{:S(2)}, u32[]{:S(2)}) async-start(f32[64,4,128]{2,1,0:T(4,128)} %broadcast_in_dim.23), calls=%async_computation.3 | async-start | bytes 262144 | tf_op jit(solution)/shard_map/all_to_all | solution.py:499
  86.7 11.9 %collective-permute-start.6 = (bf16[384,128]{1,0:T(8,128)(2,1)S(1)}, bf16[384,128]{1,0:T(8,128)(2,1)S(1)}, u32[]{:S(2)}, u32[]{:S(2)}) collective-permute-start(bf16[384,128]{1,0:T(8,128)(2,1)S(1)} %get-tuple-element.56), channel_id=1, source_target_pairs={{0,4},{1,5},{2,6},{3,7},{4,8},{5,9},{6,10},{7,11},{8,12},{9,13},{1... | collective-permute-start | bytes 294920 | tf_op jit(solution)/shard_map/ppermute | solution.py:516
  88.9 9.7 %collective-permute-start.7 = (bf16[384,128]{1,0:T(8,128)(2,1)S(1)}, bf16[384,128]{1,0:T(8,128)(2,1)S(1)}, u32[]{:S(2)}, u32[]{:S(2)}) collective-permute-start(bf16[384,128]{1,0:T(8,128)(2,1)S(1)} %get-tuple-element.57), channel_id=1, source_target_pairs={{0,8},{1,9},{2,10},{3,11},{4,12},{5,13},{6,14},{7,15},{8,0},{9,1},... | collective-permute-start | bytes 294920 | tf_op jit(solution)/shard_map/ppermute | solution.py:516
  92.6 6.0 %collective-permute-start.8 = (bf16[384,128]{1,0:T(8,128)(2,1)S(1)}, bf16[384,128]{1,0:T(8,128)(2,1)S(1)}, u32[]{:S(2)}, u32[]{:S(2)}) collective-permute-start(bf16[384,128]{1,0:T(8,128)(2,1)S(1)} %get-tuple-element.58), channel_id=1, source_target_pairs={{0,12},{1,13},{2,14},{3,15},{4,0},{5,1},{6,2},{7,3},{8,4},{9,5},{1... | collective-permute-start | bytes 294920 | tf_op jit(solution)/shard_map/ppermute | solution.py:516

commit v5 on v4

--- a/solution.py
+++ b/solution.py
@@ -19,8 +19,8 @@
 CS = 2
 QROWS = XS * TOK
 KROWS = XS * ZS * CS * TOK
-BLOCK = 1024
-UNROLL = 2
+HALF = KROWS // CS
+PREP = 36
 SCALE = HDIM ** (-0.5)
 LOG2E = 1.0 / math.log(2.0)
 BF = jnp.bfloat16
@@ -146,36 +146,27 @@
     return block[:, :128].astype(BF), (rest[:64] + roll_half(rest[64:])).astype(BF)
 
 
-def loop(steps, body, init):
-    return lax.fori_loop(0, steps, body, init, unroll=UNROLL)
-
-
-def attn_kernel(
-    core_ref, x_ref, kv_other, qd0, qd1, qd2, qd3, kv_own, dko_ref, dkx_ref, oq_ref,
-    ke, vs, qe, cs, st, ot, dqt, pool, kv_vmem, sem,
-):
+def unpack_keys(kv_ref, mine, ke, vs):
     low = low_lanes(64)
-    core = core_ref[0]
-    fetch = pltpu.make_async_copy(kv_other, kv_vmem, sem)
-    fetch.start()
-    for half, kv_ref in enumerate((kv_own, kv_vmem)):
-        if half == 1:
-            fetch.wait()
-        mine = core if half == 0 else 1 - core
-        for m in range(8):
-            base = half * 1024 + m * 128
-            full, other = unpack(kv_ref[m, 0:128, :], kv_ref[m, 256:320, :], low)
-            ke[base : base + 128, 0:128] = full
-            ke[base : base + 128, 128:256] = other
-            full, other = unpack(kv_ref[m, 128:256, :], kv_ref[m, 320:384, :], low)
-            vs[base : base + 128, 0:128] = full
-            vs[base : base + 128, 128:256] = other
-        row = lax.broadcasted_iota(jnp.int32, (1024, 128), 0)
-        col = lax.broadcasted_iota(jnp.int32, (1024, 128), 1)
-        cell = lax.shift_right_logical(row, 7) * 16 + mine * 8 + (lax.shift_right_logical(row, 4) & 7)
-        table = jnp.where(cell == col, 1.0, 0.0).astype(BF)
-        ke[half * 1024 : (half + 1) * 1024, 256:384] = table
-        ke[half * 1024 : (half + 1) * 1024, 384:512] = table
+    for m in range(8):
+        rows = slice(m * 128, (m + 1) * 128)
+        full, other = unpack(kv_ref[m, 0:128, :], kv_ref[m, 256:320, :], low)
+        ke[rows, 0:128] = full
+        ke[rows, 128:256] = other
+        full, other = unpack(kv_ref[m, 128:256, :], kv_ref[m, 320:384, :], low)
+        vs[rows, 0:128] = full
+        vs[rows, 128:256] = other
+    row = lax.broadcasted_iota(jnp.int32, (HALF, 128), 0)
+    col = lax.broadcasted_iota(jnp.int32, (HALF, 128), 1)
+    cell = lax.shift_right_logical(row, 7) * 16 + mine * 8 + (lax.shift_right_logical(row, 4) & 7)
+    table = jnp.where(cell == col, 1.0, 0.0).astype(BF)
+    ke[:, 256:384] = table
+    ke[:, 384:512] = table
+
+
+def prepare_kernel(core_ref, qd0, qd1, qd2, qd3, kv_own, ke, vs, qe, cs, st, top_ref):
+    low = low_lanes(64)
+    unpack_keys(kv_own, core_ref[0], ke, vs)
     for k, qd_ref in enumerate((qd0, qd1, qd2, qd3)):
         base = k * 128
         full, other = unpack(qd_ref[0:128, :], qd_ref[256:320, :], low)
@@ -188,57 +179,53 @@
         for part in range(2):
             wide = jnp.broadcast_to(rows[part * 8 : part * 8 + 8, None, :], (8, POOL, 128))
             qe[base : base + 128, 256 + part * 128 : 384 + part * 128] = wide.reshape(128, 128).astype(BF)
-
-    steps = KROWS // BLOCK
-
-    def scores(b, top):
-        at = pl.ds(pl.multiple_of(b * BLOCK, BLOCK), BLOCK)
-        s = nt(ke[at, :], qe[...])
-        st[at, :] = s
-        return jnp.maximum(top, jnp.max(s.reshape(BLOCK // 8, 8, QROWS), axis=0))
-
-    top = loop(steps, scores, jnp.full((8, QROWS), -jnp.inf, F32))
+    s = nt(ke[...], qe[...])
+    st[...] = s
+    top_ref[...] = jnp.max(s.reshape(HALF // 8, 8, QROWS), axis=0)
+
+
+def attn_kernel(
+    core_ref, x_ref, kv_other, ke_own, vs_own, qe, cs, st_own, top_ref, dko_ref, dkx_ref, oq_ref,
+    ke_other, vs_other, st, ot, dqt, pool,
+):
+    core = core_ref[0]
+    unpack_keys(kv_other, 1 - core, ke_other, vs_other)
+    halves = ((ke_own, vs_own, core, dko_ref), (ke_other, vs_other, 1 - core, dkx_ref))
+    s = nt(ke_other[...], qe[...])
+    st[HALF:, :] = s
+    top = jnp.maximum(top_ref[...], jnp.max(s.reshape(HALF // 8, 8, QROWS), axis=0))
     top = jnp.max(top, axis=0, keepdims=True) * (SCALE * LOG2E)
-    ot[...] = jnp.zeros_like(ot)
-
-    def weigh(b, total):
-        at = pl.ds(pl.multiple_of(b * BLOCK, BLOCK), BLOCK)
-        w = jnp.exp2(st[at, :] * (SCALE * LOG2E) - top)
+    total = jnp.zeros((8, QROWS), F32)
+    for half, (_, vs, _, _) in enumerate(halves):
+        at = slice(half * HALF, (half + 1) * HALF)
+        s = st_own[...] if half == 0 else st[at, :]
+        w = jnp.exp2(s * (SCALE * LOG2E) - top)
         st[at, :] = w
-        ot[...] += tn(vs[at, :], w.astype(BF))
-        return total + jnp.sum(w.reshape(BLOCK // 8, 8, QROWS), axis=0)
-
-    total = loop(steps, weigh, jnp.zeros((8, QROWS), F32))
+        part = tn(vs[...], w.astype(BF))
+        ot[...] = part if half == 0 else ot[...] + part
+        total += jnp.sum(w.reshape(HALF // 8, 8, QROWS), axis=0)
     inv = 1.0 / jnp.sum(total, axis=0, keepdims=True)
     att = (ot[...] * inv).astype(BF).astype(F32)
     delta = jnp.sum(att * cs[...].astype(F32).T, axis=0, keepdims=True)
     att = att.T
-    dqt[...] = jnp.zeros_like(dqt)
-
-    for half, ref in ((0, dko_ref), (1, dkx_ref)):
-        mine = core if half == 0 else 1 - core
-
-        def back(b, carry):
-            at = pl.ds(pl.multiple_of(half * 1024 + b * BLOCK, BLOCK), BLOCK)
-            prob = st[at, :] * inv
-            dv = nn(prob.astype(BF), cs[...])
-            ds = prob * (nt(vs[at, :], cs[...]) - delta)
-            low_ds = ds.astype(BF)
-            dk = nn(low_ds, qe[:, 0:256]) * SCALE
-            dqt[...] += tn(ke[at, 0:256], low_ds)
-            pooled = jnp.sum(ds.reshape(BLOCK // POOL, POOL, QROWS), axis=1)
-            for t in range(BLOCK // 128):
-                m = b * (BLOCK // 128) + t
-                full, rest = pack_out(dk[t * 128 : (t + 1) * 128])
-                ref[m, 0:128, :] = full
-                ref[m, 256:320, :] = rest
-                full, rest = pack_out(dv[t * 128 : (t + 1) * 128])
-                ref[m, 128:256, :] = full
-                ref[m, 320:384, :] = rest
-                pool[pl.ds(pl.multiple_of(m * 16 + mine * 8, 8), 8), :] = pooled[t * 8 : t * 8 + 8]
-            return carry
-
-        loop(1024 // BLOCK, back, 0)
+    for half, (ke, vs, mine, ref) in enumerate(halves):
+        prob = st[half * HALF : (half + 1) * HALF, :] * inv
+        dv = nn(prob.astype(BF), cs[...])
+        ds = prob * (nt(vs[...], cs[...]) - delta)
+        low_ds = ds.astype(BF)
+        dk = nn(low_ds, qe[:, 0:256]) * SCALE
+        part = tn(ke[:, 0:256], low_ds)
+        dqt[...] = part if half == 0 else dqt[...] + part
+        pooled = jnp.sum(ds.reshape(HALF // POOL, POOL, QROWS), axis=1)
+        for m in range(8):
+            rows = slice(m * 128, (m + 1) * 128)
+            full, rest = pack_out(dk[rows])
+            ref[m, 0:128, :] = full
+            ref[m, 256:320, :] = rest
+            full, rest = pack_out(dv[rows])
+            ref[m, 128:256, :] = full
+            ref[m, 320:384, :] = rest
+            pool[pl.ds(pl.multiple_of(m * 16 + mine * 8, 8), 8), :] = pooled[m * 8 : m * 8 + 8]
 
     row = lax.broadcasted_iota(jnp.int32, (QROWS // POOL, QROWS), 0)
     col = lax.broadcasted_iota(jnp.int32, (QROWS // POOL, QROWS), 1)
@@ -385,28 +372,38 @@
     )(*args)
 
 
+def prepare(*args):
+    return call(
+        prepare_kernel,
+        (
+            shape(HALF, 512), shape(HALF, 256), shape(QROWS, 512), shape(QROWS, 256),
+            shape(HALF, QROWS, dtype=F32), shape(8, QROWS, dtype=F32),
+        ),
+        args,
+        smem=1,
+        flops=2 * QROWS * KROWS * 256,
+        moved=6_000_000,
+        limit=PREP,
+    )
+
+
 def attention(*args):
     return call(
         attn_kernel,
         (shape(8, 384, 128), shape(8, 384, 128), shape(XS, 400, 128)),
         args,
         smem=2,
-        hbm=1,
         scratch=(
-            pltpu.VMEM((KROWS, 512), BF),
-            pltpu.VMEM((KROWS, 256), BF),
-            pltpu.VMEM((QROWS, 512), BF),
-            pltpu.VMEM((QROWS, 256), BF),
+            pltpu.VMEM((HALF, 512), BF),
+            pltpu.VMEM((HALF, 256), BF),
             pltpu.VMEM((KROWS, QROWS), F32),
             pltpu.VMEM((256, QROWS), F32),
             pltpu.VMEM((256, QROWS), F32),
             pltpu.VMEM((PAIRS, QROWS), F32),
-            pltpu.VMEM((8, 384, 128), BF),
-            pltpu.SemaphoreType.DMA(()),
         ),
-        flops=8 * 2 * QROWS * KROWS * 256,
-        moved=5_000_000,
-        limit=32,
+        flops=7 * 2 * QROWS * KROWS * 256,
+        moved=8_000_000,
+        limit=28,
     )
 
 
@@ -476,8 +473,8 @@
     qd = [qd[0]] + [lax.ppermute(qd[k], "seq", ring(k)) for k in range(1, XS)]
     kv_own, qd = lax.optimization_barrier((kv_own, qd))
     kv_other = lax.ppermute(kv_own, "seq", swap)
-    kv_other = pltpu.with_memory_space_constraint(kv_other, pltpu.MemorySpace.HBM)
-    dkv_own, dkv_other, oq = attention(core, own_x, kv_other, *qd, kv_own)
+    ready = prepare(core, *qd, kv_own)
+    dkv_own, dkv_other, oq = attention(core, own_x, kv_other, *ready)
     oq = lax.all_to_all(oq, "seq", 0, 0, axis_index_groups=x_groups)
     dkv_swapped = lax.ppermute(dkv_other, "seq", swap)
     send, keep = call(

time: 100 us -> 97.7 us (0.977)
  local copies, waits for them, and re-layouts: 2.23 us -> 0.69 us
    unnamed x10 -> x8, local copies, waits for them, and re-layouts: 1.55 us -> 0.02 us
    pallas_call x8 -> x9, Pallas kernels: 12.3 us -> 11.6 us  [call(): pl.pallas_call(kernel, out_shape=out_shape, in_specs=[SMEM] * smem + [ANY...]
  transfers between devices with their start and end apart: 12 -> 12, of which waited for: 5 -> 5; matrix products, arithmetic and copies ran while one was open for 1% -> 1% of each run, Pallas kernels for 2% -> 4%
where the time goes in v5:
time: 97.7 us; the launch traced here: 96.8 us
  starting transfers between devices  65.7 us (67%)
  Pallas kernels  11.6 us (12%)
  waiting for transfers between devices  9.4 us (10%)
  blocking collectives  8.57 us (9%)
    all_to_all x1, starting transfers between devices, body(): far = lax.all_to_all(far, ('dp', 'seq'), 0, 0, axis_index_groups=far_groups)  17.3 us
    all_to_all x1, starting transfers between devices, body(): kv_own = lax.all_to_all(kv, 'seq', 0, 0, axis_index_groups=xz_groups)  13.3 us
    pallas_call x9, Pallas kernels, call(): pl.pallas_call(kernel, out_shape=out_shape, in_specs=[SMEM] * smem + [ANY...  11.6 us
    ppermute x3, starting transfers between devices, body(): qd = [qd[0]] + [lax.ppermute(qd[k], 'seq', ring(k)) for k in range(1, XS)]  10.8 us
    ppermute x3, starting transfers between devices, body(): lax.ppermute(dkv[k], 'seq', ring(k))  8.65 us
    all_to_all x1, blocking collectives, body(): lax.all_to_all(total, 'seq', 0, 0, axis_index_groups=xc_groups).sum(axis=0)  8.57 us
    ppermute x1, starting transfers between devices, body(): come = lax.ppermute(send, 'seq', across)  6.24 us
    ppermute x3, waiting for transfers between devices, body(): qd = [qd[0]] + [lax.ppermute(qd[k], 'seq', ring(k)) for k in range(1, XS)]  4.8 us
  transfers between devices with their start and end apart: 12, of which 5 were waited for; matrix products, arithmetic and copies ran while one was open for 1% of the time, Pallas kernels for 4%

profile of v5, /device:TPU:1, one launch (start us, length us, event | category | flops | bytes accessed | tf_op | source)
XLA Modules:
  0.0 96.8 jit_solution(161956600474604708)
XLA Ops:
  0.7 2.1 %shard_map.109 = bf16[8,384,128]{2,1,0:T(8,128)(2,1)} custom-call(bf16[128,768]{1,0:T(8,128)(2,1)} %bitcast.21, bf16[128,768]{1,0:T(8,128)(2,1)} %bitcast.22), custom_call_target="tpu_custom_call" | custom-call | bytes 1500000 | tf_op jit(solution)/shard_map/pallas_call | solution.py:364
  2.8 13.3 %all-to-all-start = ((bf16[8,384,128]{2,1,0:T(8,128)(2,1)}), bf16[8,384,128]{2,1,0:T(8,128)(2,1)S(1)}, u32[]{:S(2)}, u32[]{:S(2)}) async-start(bf16[8,384,128]{2,1,0:T(8,128)(2,1)} %shard_map.109), calls=%async_computation | async-start | bytes 1572864 | tf_op jit(solution)/shard_map/all_to_all | solution.py:454
  16.1 1.0 %shard_map.110 = (bf16[400,128]{1,0:T(8,128)(2,1)S(1)}, bf16[400,128]{1,0:T(8,128)(2,1)S(1)}, bf16[400,128]{1,0:T(8,128)(2,1)S(1)}, bf16[400,128]{1,0:T(8,128)(2,1)S(1)}) custom-call(s32[1]{0:T(128)} %bitcast.1.x_ref, bf16[128,768]{1,0:T(8,128)(2,1)S(1)} %bitcast.17, bf16[128,768]{1,0:T(8,128)(2,1)S(1)} %bitcast.18, bf16[8,128,128]{2,1,0:T(8,128)(2,1)S(1)} %bitcast.15, ...), custom_call_target="tpu_custom_call" | custom-call | flops 6291456 | bytes 1500000 | tf_op jit(solution)/shard_map/pallas_call | solution.py:364
  17.1 3.4 %collective-permute-start = (bf16[400,128]{1,0:T(8,128)(2,1)S(1)}, bf16[400,128]{1,0:T(8,128)(2,1)S(1)}, u32[]{:S(2)}, u32[]{:S(2)}) collective-permute-start(bf16[400,128]{1,0:T(8,128)(2,1)S(1)} %get-tuple-element.45), channel_id=1, source_target_pairs={{0,4},{1,5},{2,6},{3,7},{4,8},{5,9},{6,10},{7,11},{8,12},{9,13},{1... | collective-permute-start | bytes 307208 | tf_op jit(solution)/shard_map/ppermute | solution.py:473
  20.5 4.3 %collective-permute-start.1 = (bf16[400,128]{1,0:T(8,128)(2,1)S(1)}, bf16[400,128]{1,0:T(8,128)(2,1)S(1)}, u32[]{:S(2)}, u32[]{:S(2)}) collective-permute-start(bf16[400,128]{1,0:T(8,128)(2,1)S(1)} %get-tuple-element.46), channel_id=1, source_target_pairs={{0,8},{1,9},{2,10},{3,11},{4,12},{5,13},{6,14},{7,15},{8,0},{9,1},... | collective-permute-start | bytes 307208 | tf_op jit(solution)/shard_map/ppermute | solution.py:473
  24.8 3.1 %collective-permute-start.2 = (bf16[400,128]{1,0:T(8,128)(2,1)S(1)}, bf16[400,128]{1,0:T(8,128)(2,1)S(1)}, u32[]{:S(2)}, u32[]{:S(2)}) collective-permute-start(bf16[400,128]{1,0:T(8,128)(2,1)S(1)} %get-tuple-element.47), channel_id=1, source_target_pairs={{0,12},{1,13},{2,14},{3,15},{4,0},{5,1},{6,2},{7,3},{8,4},{9,5},{1... | collective-permute-start | bytes 307208 | tf_op jit(solution)/shard_map/ppermute | solution.py:473
  27.9 0.0 collective-permute-done.qd1
  27.9 2.1 %collective-permute-done.1.qd2 = bf16[400,128]{1,0:T(8,128)(2,1)S(1)} collective-permute-done((bf16[400,128]{1,0:T(8,128)(2,1)S(1)}, bf16[400,128]{1,0:T(8,128)(2,1)S(1)}, u32[]{:S(2)}, u32[]{:S(2)}) %collective-permute-start.1) | collective-permute-done | bytes 102432 | tf_op jit(solution)/shard_map/ppermute | solution.py:473
  30.1 2.7 %collective-permute-done.2.qd3 = bf16[400,128]{1,0:T(8,128)(2,1)S(1)} collective-permute-done((bf16[400,128]{1,0:T(8,128)(2,1)S(1)}, bf16[400,128]{1,0:T(8,128)(2,1)S(1)}, u32[]{:S(2)}, u32[]{:S(2)}) %collective-permute-start.2) | collective-permute-done | bytes 102432 | tf_op jit(solution)/shard_map/ppermute | solution.py:473
  32.7 0.0 all-to-all-done.kv_own
  32.7 3.2 %collective-permute-start.3 = (bf16[8,384,128]{2,1,0:T(8,128)(2,1)S(1)}, bf16[8,384,128]{2,1,0:T(8,128)(2,1)S(1)}, u32[]{:S(2)}, u32[]{:S(2)}) collective-permute-start(bf16[8,384,128]{2,1,0:T(8,128)(2,1)S(1)} %all-to-all-done.kv_own), channel_id=1, source_target_pairs={{0,1},{1,0},{2,3},{3,2},{4,5},{5,4},{6,7},{7,6},{8,9},{9,8},{10,11... | collective-permute-start | bytes 2359304 | tf_op jit(solution)/shard_map/ppermute | solution.py:475
  36.0 0.9 shard_map.111
  36.9 1.0 collective-permute-done.3.kv_other
  37.8 5.2 %shard_map.112 = (bf16[8,384,128]{2,1,0:T(8,128)(2,1)S(1)}, bf16[8,384,128]{2,1,0:T(8,128)(2,1)S(1)}, bf16[4,400,128]{2,1,0:T(8,128)(2,1)}) custom-call(s32[1]{0:T(128)} %bitcast.core_ref, s32[1]{0:T(128)} %bitcast.1.x_ref, bf16[8,384,128]{2,1,0:T(8,128)(2,1)S(1)} %collective-permute-done.3.kv_other, bf16[1024,512]{1,0:T(8,128)(2,1)S(1)} %get-tuple-element.53.ke_own, ...), custom_call_target="tpu_custom_call" | custom-call | flops 3758096384 | bytes 8000000 | tf_op jit(solution)/shard_map/pallas_call | solution.py:364
  43.0 2.3 %collective-permute-start.4 = (bf16[8,384,128]{2,1,0:T(8,128)(2,1)S(1)}, bf16[8,384,128]{2,1,0:T(8,128)(2,1)S(1)}, u32[]{:S(2)}, u32[]{:S(2)}) collective-permute-start(bf16[8,384,128]{2,1,0:T(8,128)(2,1)S(1)} %get-tuple-element.63), channel_id=1, source_target_pairs={{0,1},{1,0},{2,3},{3,2},{4,5},{5,4},{6,7},{7,6},{8,9},{9,8},{10,11... | collective-permute-start | bytes 2359304 | tf_op jit(solution)/shard_map/ppermute | solution.py:479
  45.3 4.0 %all-to-all-start.1 = ((bf16[4,400,128]{2,1,0:T(8,128)(2,1)}), bf16[4,400,128]{2,1,0:T(8,128)(2,1)S(1)}, u32[]{:S(2)}, u32[]{:S(2)}) async-start(bf16[4,400,128]{2,1,0:T(8,128)(2,1)} %get-tuple-element.59), calls=%async_computation.1 | async-start | bytes 819200 | tf_op jit(solution)/shard_map/all_to_all | solution.py:478
  49.3 0.0 collective-permute-done.4.other_ref
  49.3 0.2 shard_map.115
  49.4 6.2 %collective-permute-start.5 = (bf16[4,384,128]{2,1,0:T(8,128)(2,1)S(1)}, bf16[4,384,128]{2,1,0:T(8,128)(2,1)S(1)}, u32[]{:S(2)}, u32[]{:S(2)}) collective-permute-start(bf16[4,384,128]{2,1,0:T(8,128)(2,1)S(1)} %get-tuple-element.66), channel_id=1, source_target_pairs={{0,2},{1,3},{2,0},{3,1},{4,6},{5,7},{6,4},{7,5},{8,10},{9,11},{10,... | collective-permute-start | bytes 1179656 | tf_op jit(solution)/shard_map/ppermute | solution.py:488
  55.7 1.5 %all-to-all-done.1.oq_ref = bf16[4,400,128]{2,1,0:T(8,128)(2,1)S(1)} async-done(((bf16[4,400,128]{2,1,0:T(8,128)(2,1)}), bf16[4,400,128]{2,1,0:T(8,128)(2,1)S(1)}, u32[]{:S(2)}, u32[]{:S(2)}) %all-to-all-start.1) | async-done | bytes 409632 | tf_op jit(solution)/shard_map/all_to_all | solution.py:478
  57.2 0.1 shard_map.114
  57.4 8.6 %all_to_all.20 = f32[8,4,128]{2,1,0:T(4,128)S(1)} all-to-all(f32[8,4,128]{2,1,0:T(4,128)S(1)} %shard_map.114), channel_id=1, replica_groups={{0,1,4,5,8,9,12,13},{2,3,6,7,10,11,14,15},{16,17,20,21,24,25,28,29},{18..., dimensions={0} | all-to-all | bytes 32768 | tf_op jit(solution)/shard_map/all_to_all | solution.py:493
  65.9 0.7 broadcast_in_dim.23
  66.6 17.3 %all-to-all-start.3 = ((f32[64,4,128]{2,1,0:T(4,128)}), f32[64,4,128]{2,1,0:T(4,128)S(1)}, u32[]{:S(2)}, u32[]{:S(2)}) async-start(f32[64,4,128]{2,1,0:T(4,128)} %broadcast_in_dim.23), calls=%async_computation.3 | async-start | bytes 262144 | tf_op jit(solution)/shard_map/all_to_all | solution.py:496
  84.0 0.1 shard_map.116
  84.1 2.2 %collective-permute-start.6 = (bf16[384,128]{1,0:T(8,128)(2,1)S(1)}, bf16[384,128]{1,0:T(8,128)(2,1)S(1)}, u32[]{:S(2)}, u32[]{:S(2)}) collective-permute-start(bf16[384,128]{1,0:T(8,128)(2,1)S(1)} %get-tuple-element.68), channel_id=1, source_target_pairs={{0,4},{1,5},{2,6},{3,7},{4,8},{5,9},{6,10},{7,11},{8,12},{9,13},{1... | collective-permute-start | bytes 294920 | tf_op jit(solution)/shard_map/ppermute | solution.py:513
  86.3 3.7 %collective-permute-start.7 = (bf16[384,128]{1,0:T(8,128)(2,1)S(1)}, bf16[384,128]{1,0:T(8,128)(2,1)S(1)}, u32[]{:S(2)}, u32[]{:S(2)}) collective-permute-start(bf16[384,128]{1,0:T(8,128)(2,1)S(1)} %get-tuple-element.69), channel_id=1, source_target_pairs={{0,8},{1,9},{2,10},{3,11},{4,12},{5,13},{6,14},{7,15},{8,0},{9,1},... | collective-permute-start | bytes 294920 | tf_op jit(solution)/shard_map/ppermute | solution.py:513
  90.0 2.8 %collective-permute-start.8 = (bf16[384,128]{1,0:T(8,128)(2,1)S(1)}, bf16[384,128]{1,0:T(8,128)(2,1)S(1)}, u32[]{:S(2)}, u32[]{:S(2)}) collective-permute-start(bf16[384,128]{1,0:T(8,128)(2,1)S(1)} %get-tuple-element.70), channel_id=1, source_target_pairs={{0,12},{1,13},{2,14},{3,15},{4,0},{5,1},{6,2},{7,3},{8,4},{9,5},{1... | collective-permute-start | bytes 294920 | tf_op jit(solution)/shard_map/ppermute | solution.py:513
  92.7 1.1 %shard_map.113 = (bf16[128,768]{1,0:T(8,128)(2,1)}, bf16[128,768]{1,0:T(8,128)(2,1)}, bf16[8,128,128]{2,1,0:T(8,128)(2,1)}) custom-call(bf16[4,400,128]{2,1,0:T(8,128)(2,1)S(1)} %all-to-all-done.1.oq_ref, f32[4,128]{1,0:T(4,128)S(1)} %bitcast.20), custom_call_target="tpu_custom_call" | custom-call | flops 4194304 | bytes 1100000 | tf_op jit(solution)/shard_map/pallas_call | solution.py:364
  93.8 2.1 %all-to-all-done.3.far_ref = f32[64,4,128]{2,1,0:T(4,128)S(1)} async-done(((f32[64,4,128]{2,1,0:T(4,128)}), f32[64,4,128]{2,1,0:T(4,128)S(1)}, u32[]{:S(2)}, u32[]{:S(2)}) %all-to-all-start.3) | async-done | bytes 131104 | tf_op jit(solution)/shard_map/all_to_all | solution.py:496
  95.9 0.0 collective-permute-done.8.in3
  95.9 0.9 shard_map.117
  (12 shorter events, 0.0 us)
Async XLA Ops:
  0.6 15.5 %copy-start.2 = (bf16[1,128,768]{2,1,0:T(8,128)(2,1)S(1)}, bf16[1,128,768]{2,1,0:T(8,128)(2,1)}, u32[]{:S(2)}) copy-start(bf16[1,128,768]{2,1,0:T(8,128)(2,1)} %param.9) | copy-start | bytes 589828
  0.6 15.5 %copy-start.1 = (bf16[1,128,768]{2,1,0:T(8,128)(2,1)S(1)}, bf16[1,128,768]{2,1,0:T(8,128)(2,1)}, u32[]{:S(2)}) copy-start(bf16[1,128,768]{2,1,0:T(8,128)(2,1)} %param.6) | copy-start | bytes 589828
  0.7 15.5 %copy-start.3 = (f32[128,4]{0,1:T(4,128)S(1)}, f32[128,4]{0,1:T(4,128)}, u32[]{:S(2)}) copy-start(f32[128,4]{0,1:T(4,128)} %param.11) | copy-start | bytes 6148
  0.7 15.5 %copy-start = (bf16[1,8,128,128]{3,2,1,0:T(8,128)(2,1)S(1)}, bf16[1,8,128,128]{3,2,1,0:T(8,128)(2,1)}, u32[]{:S(2)}) copy-start(bf16[1,8,128,128]{3,2,1,0:T(8,128)(2,1)} %param.10) | copy-start | bytes 786436
  2.8 30.0 %all-to-all-start = ((bf16[8,384,128]{2,1,0:T(8,128)(2,1)}), bf16[8,384,128]{2,1,0:T(8,128)(2,1)S(1)}, u32[]{:S(2)}, u32[]{:S(2)}) async-start(bf16[8,384,128]{2,1,0:T(8,128)(2,1)} %shard_map.109), calls=%async_computation | async-start | bytes 1572864 | tf_op jit(solution)/shard_map/all_to_all | solution.py:454
  17.1 10.8 %collective-permute-start = (bf16[400,128]{1,0:T(8,128)(2,1)S(1)}, bf16[400,128]{1,0:T(8,128)(2,1)S(1)}, u32[]{:S(2)}, u32[]{:S(2)}) collective-permute-start(bf16[400,128]{1,0:T(8,128)(2,1)S(1)} %get-tuple-element.45), channel_id=1, source_target_pairs={{0,4},{1,5},{2,6},{3,7},{4,8},{5,9},{6,10},{7,11},{8,12},{9,13},{1... | collective-permute-start | bytes 307208 | tf_op jit(solution)/shard_map/ppermute | solution.py:473
  20.5 9.6 %collective-permute-start.1 = (bf16[400,128]{1,0:T(8,128)(2,1)S(1)}, bf16[400,128]{1,0:T(8,128)(2,1)S(1)}, u32[]{:S(2)}, u32[]{:S(2)}) collective-permute-start(bf16[400,128]{1,0:T(8,128)(2,1)S(1)} %get-tuple-element.46), channel_id=1, source_target_pairs={{0,8},{1,9},{2,10},{3,11},{4,12},{5,13},{6,14},{7,15},{8,0},{9,1},... | collective-permute-start | bytes 307208 | tf_op jit(solution)/shard_map/ppermute | solution.py:473
  24.8 7.9 %collective-permute-start.2 = (bf16[400,128]{1,0:T(8,128)(2,1)S(1)}, bf16[400,128]{1,0:T(8,128)(2,1)S(1)}, u32[]{:S(2)}, u32[]{:S(2)}) collective-permute-start(bf16[400,128]{1,0:T(8,128)(2,1)S(1)} %get-tuple-element.47), channel_id=1, source_target_pairs={{0,12},{1,13},{2,14},{3,15},{4,0},{5,1},{6,2},{7,3},{8,4},{9,5},{1... | collective-permute-start | bytes 307208 | tf_op jit(solution)/shard_map/ppermute | solution.py:473
  32.7 5.1 %collective-permute-start.3 = (bf16[8,384,128]{2,1,0:T(8,128)(2,1)S(1)}, bf16[8,384,128]{2,1,0:T(8,128)(2,1)S(1)}, u32[]{:S(2)}, u32[]{:S(2)}) collective-permute-start(bf16[8,384,128]{2,1,0:T(8,128)(2,1)S(1)} %all-to-all-done.kv_own), channel_id=1, source_target_pairs={{0,1},{1,0},{2,3},{3,2},{4,5},{5,4},{6,7},{7,6},{8,9},{9,8},{10,11... | collective-permute-start | bytes 2359304 | tf_op jit(solution)/shard_map/ppermute | solution.py:475
  43.0 6.2 %collective-permute-start.4 = (bf16[8,384,128]{2,1,0:T(8,128)(2,1)S(1)}, bf16[8,384,128]{2,1,0:T(8,128)(2,1)S(1)}, u32[]{:S(2)}, u32[]{:S(2)}) collective-permute-start(bf16[8,384,128]{2,1,0:T(8,128)(2,1)S(1)} %get-tuple-element.63), channel_id=1, source_target_pairs={{0,1},{1,0},{2,3},{3,2},{4,5},{5,4},{6,7},{7,6},{8,9},{9,8},{10,11... | collective-permute-start | bytes 2359304 | tf_op jit(solution)/shard_map/ppermute | solution.py:479
  45.3 11.9 %all-to-all-start.1 = ((bf16[4,400,128]{2,1,0:T(8,128)(2,1)}), bf16[4,400,128]{2,1,0:T(8,128)(2,1)S(1)}, u32[]{:S(2)}, u32[]{:S(2)}) async-start(bf16[4,400,128]{2,1,0:T(8,128)(2,1)} %get-tuple-element.59), calls=%async_computation.1 | async-start | bytes 819200 | tf_op jit(solution)/shard_map/all_to_all | solution.py:478
  49.4 34.5 %collective-permute-start.5 = (bf16[4,384,128]{2,1,0:T(8,128)(2,1)S(1)}, bf16[4,384,128]{2,1,0:T(8,128)(2,1)S(1)}, u32[]{:S(2)}, u32[]{:S(2)}) collective-permute-start(bf16[4,384,128]{2,1,0:T(8,128)(2,1)S(1)} %get-tuple-element.66), channel_id=1, source_target_pairs={{0,2},{1,3},{2,0},{3,1},{4,6},{5,7},{6,4},{7,5},{8,10},{9,11},{10,... | collective-permute-start | bytes 1179656 | tf_op jit(solution)/shard_map/ppermute | solution.py:488
  66.6 29.3 %all-to-all-start.3 = ((f32[64,4,128]{2,1,0:T(4,128)}), f32[64,4,128]{2,1,0:T(4,128)S(1)}, u32[]{:S(2)}, u32[]{:S(2)}) async-start(f32[64,4,128]{2,1,0:T(4,128)} %broadcast_in_dim.23), calls=%async_computation.3 | async-start | bytes 262144 | tf_op jit(solution)/shard_map/all_to_all | solution.py:496
  84.1 11.9 %collective-permute-start.6 = (bf16[384,128]{1,0:T(8,128)(2,1)S(1)}, bf16[384,128]{1,0:T(8,128)(2,1)S(1)}, u32[]{:S(2)}, u32[]{:S(2)}) collective-permute-start(bf16[384,128]{1,0:T(8,128)(2,1)S(1)} %get-tuple-element.68), channel_id=1, source_target_pairs={{0,4},{1,5},{2,6},{3,7},{4,8},{5,9},{6,10},{7,11},{8,12},{9,13},{1... | collective-permute-start | bytes 294920 | tf_op jit(solution)/shard_map/ppermute | solution.py:513
  86.3 9.7 %collective-permute-start.7 = (bf16[384,128]{1,0:T(8,128)(2,1)S(1)}, bf16[384,128]{1,0:T(8,128)(2,1)S(1)}, u32[]{:S(2)}, u32[]{:S(2)}) collective-permute-start(bf16[384,128]{1,0:T(8,128)(2,1)S(1)} %get-tuple-element.69), channel_id=1, source_target_pairs={{0,8},{1,9},{2,10},{3,11},{4,12},{5,13},{6,14},{7,15},{8,0},{9,1},... | collective-permute-start | bytes 294920 | tf_op jit(solution)/shard_map/ppermute | solution.py:513
  90.0 6.0 %collective-permute-start.8 = (bf16[384,128]{1,0:T(8,128)(2,1)S(1)}, bf16[384,128]{1,0:T(8,128)(2,1)S(1)}, u32[]{:S(2)}, u32[]{:S(2)}) collective-permute-start(bf16[384,128]{1,0:T(8,128)(2,1)S(1)} %get-tuple-element.70), channel_id=1, source_target_pairs={{0,12},{1,13},{2,14},{3,15},{4,0},{5,1},{6,2},{7,3},{8,4},{9,5},{1... | collective-permute-start | bytes 294920 | tf_op jit(solution)/shard_map/ppermute | solution.py:513

commit v6 on v5

--- a/solution.py
+++ b/solution.py
@@ -164,7 +164,19 @@
     ke[:, 384:512] = table
 
 
-def prepare_kernel(core_ref, qd0, qd1, qd2, qd3, kv_own, ke, vs, qe, cs, st, top_ref):
+def soften(ke, vs, qe, st):
+    s = nt(ke[...], qe[...])
+    top = jnp.max(jnp.max(s.reshape(HALF // 8, 8, QROWS), axis=0), axis=0, keepdims=True)
+    top = top * (SCALE * LOG2E)
+    w = jnp.exp2(s * (SCALE * LOG2E) - top)
+    st[...] = w
+    total = jnp.sum(w.reshape(HALF // 8, 8, QROWS), axis=0)
+    return top, total, tn(vs[...], w.astype(BF))
+
+
+def prepare_kernel(
+    core_ref, qd0, qd1, qd2, qd3, kv_own, ke, vs, qe, cs, st, top_ref, total_ref, ot_ref
+):
     low = low_lanes(64)
     unpack_keys(kv_own, core_ref[0], ke, vs)
     for k, qd_ref in enumerate((qd0, qd1, qd2, qd3)):
@@ -179,37 +191,32 @@
         for part in range(2):
             wide = jnp.broadcast_to(rows[part * 8 : part * 8 + 8, None, :], (8, POOL, 128))
             qe[base : base + 128, 256 + part * 128 : 384 + part * 128] = wide.reshape(128, 128).astype(BF)
-    s = nt(ke[...], qe[...])
-    st[...] = s
-    top_ref[...] = jnp.max(s.reshape(HALF // 8, 8, QROWS), axis=0)
+    top, total_ref[...], ot_ref[...] = soften(ke, vs, qe, st)
+    top_ref[...] = jnp.broadcast_to(top, top_ref.shape)
 
 
 def attn_kernel(
-    core_ref, x_ref, kv_other, ke_own, vs_own, qe, cs, st_own, top_ref, dko_ref, dkx_ref, oq_ref,
-    ke_other, vs_other, st, ot, dqt, pool,
+    core_ref, x_ref, kv_other, ke_own, vs_own, qe, cs, st_own, top_ref, total_ref, ot_ref,
+    dko_ref, dkx_ref, oq_ref, ke_other, vs_other, st_other, dqt, pool,
 ):
     core = core_ref[0]
     unpack_keys(kv_other, 1 - core, ke_other, vs_other)
-    halves = ((ke_own, vs_own, core, dko_ref), (ke_other, vs_other, 1 - core, dkx_ref))
-    s = nt(ke_other[...], qe[...])
-    st[HALF:, :] = s
-    top = jnp.maximum(top_ref[...], jnp.max(s.reshape(HALF // 8, 8, QROWS), axis=0))
-    top = jnp.max(top, axis=0, keepdims=True) * (SCALE * LOG2E)
-    total = jnp.zeros((8, QROWS), F32)
-    for half, (_, vs, _, _) in enumerate(halves):
-        at = slice(half * HALF, (half + 1) * HALF)
-        s = st_own[...] if half == 0 else st[at, :]
-        w = jnp.exp2(s * (SCALE * LOG2E) - top)
-        st[at, :] = w
-        part = tn(vs[...], w.astype(BF))
-        ot[...] = part if half == 0 else ot[...] + part
-        total += jnp.sum(w.reshape(HALF // 8, 8, QROWS), axis=0)
+    top_other, total_other, ot_other = soften(ke_other, vs_other, qe, st_other)
+    top_own = top_ref[0:1, :]
+    top = jnp.maximum(top_own, top_other)
+    own, other = jnp.exp2(top_own - top), jnp.exp2(top_other - top)
+    total = total_ref[...] * own + total_other * other
     inv = 1.0 / jnp.sum(total, axis=0, keepdims=True)
-    att = (ot[...] * inv).astype(BF).astype(F32)
+    halves = (
+        (ke_own, vs_own, st_own, own * inv, core, dko_ref),
+        (ke_other, vs_other, st_other, other * inv, 1 - core, dkx_ref),
+    )
+    ot = ot_ref[...] * own + ot_other * other
+    att = (ot * inv).astype(BF).astype(F32)
     delta = jnp.sum(att * cs[...].astype(F32).T, axis=0, keepdims=True)
     att = att.T
-    for half, (ke, vs, mine, ref) in enumerate(halves):
-        prob = st[half * HALF : (half + 1) * HALF, :] * inv
+    for half, (ke, vs, st, share, mine, ref) in enumerate(halves):
+        prob = st[...] * share
         dv = nn(prob.astype(BF), cs[...])
         ds = prob * (nt(vs[...], cs[...]) - delta)
         low_ds = ds.astype(BF)
@@ -377,11 +384,12 @@
         prepare_kernel,
         (
             shape(HALF, 512), shape(HALF, 256), shape(QROWS, 512), shape(QROWS, 256),
-            shape(HALF, QROWS, dtype=F32), shape(8, QROWS, dtype=F32),
+            shape(HALF, QROWS, dtype=F32), shape(8, QROWS, dtype=F32), shape(8, QROWS, dtype=F32),
+            shape(256, QROWS, dtype=F32),
         ),
         args,
         smem=1,
-        flops=2 * QROWS * KROWS * 256,
+        flops=3 * QROWS * KROWS * 256,
         moved=6_000_000,
         limit=PREP,
     )
@@ -396,12 +404,11 @@
         scratch=(
             pltpu.VMEM((HALF, 512), BF),
             pltpu.VMEM((HALF, 256), BF),
-            pltpu.VMEM((KROWS, QROWS), F32),
-            pltpu.VMEM((256, QROWS), F32),
+            pltpu.VMEM((HALF, QROWS), F32),
             pltpu.VMEM((256, QROWS), F32),
             pltpu.VMEM((PAIRS, QROWS), F32),
         ),
-        flops=7 * 2 * QROWS * KROWS * 256,
+        flops=13 * QROWS * KROWS * 256,
         moved=8_000_000,
         limit=28,
     )

time: 97.7 us -> 97.3 us (level)
  no operation moved by 1% of the time
where the time goes in v6:
time: 97.3 us; the launch traced here: 96.5 us
  starting transfers between devices  65.7 us (68%)
  Pallas kernels  12.1 us (12%)
  blocking collectives  8.57 us (9%)
  waiting for transfers between devices  8.54 us (9%)
    all_to_all x1, starting transfers between devices, body(): far = lax.all_to_all(far, ('dp', 'seq'), 0, 0, axis_index_groups=far_groups)  17.3 us
    all_to_all x1, starting transfers between devices, body(): kv_own = lax.all_to_all(kv, 'seq', 0, 0, axis_index_groups=xz_groups)  13.3 us
    pallas_call x9, Pallas kernels, call(): pl.pallas_call(kernel, out_shape=out_shape, in_specs=[SMEM] * smem + [ANY...  12.1 us
    ppermute x3, starting transfers between devices, body(): qd = [qd[0]] + [lax.ppermute(qd[k], 'seq', ring(k)) for k in range(1, XS)]  10.8 us
    ppermute x3, starting transfers between devices, body(): lax.ppermute(dkv[k], 'seq', ring(k))  8.65 us
    all_to_all x1, blocking collectives, body(): lax.all_to_all(total, 'seq', 0, 0, axis_index_groups=xc_groups).sum(axis=0)  8.57 us
    ppermute x1, starting transfers between devices, body(): come = lax.ppermute(send, 'seq', across)  6.24 us
    ppermute x3, waiting for transfers between devices, body(): qd = [qd[0]] + [lax.ppermute(qd[k], 'seq', ring(k)) for k in range(1, XS)]  4.8 us
  transfers between devices with their start and end apart: 12, of which 5 were waited for; matrix products, arithmetic and copies ran while one was open for 1% of the time, Pallas kernels for 4%

profile of v6, /device:TPU:1, one launch (start us, length us, event | category | flops | bytes accessed | tf_op | source)
XLA Modules:
  0.0 96.5 jit_solution(15653683728388261179)
XLA Ops:
  0.7 2.1 %shard_map.109 = bf16[8,384,128]{2,1,0:T(8,128)(2,1)} custom-call(bf16[128,768]{1,0:T(8,128)(2,1)} %bitcast.21, bf16[128,768]{1,0:T(8,128)(2,1)} %bitcast.22), custom_call_target="tpu_custom_call" | custom-call | bytes 1500000 | tf_op jit(solution)/shard_map/pallas_call | solution.py:371
  2.8 13.3 %all-to-all-start = ((bf16[8,384,128]{2,1,0:T(8,128)(2,1)}), bf16[8,384,128]{2,1,0:T(8,128)(2,1)S(1)}, u32[]{:S(2)}, u32[]{:S(2)}) async-start(bf16[8,384,128]{2,1,0:T(8,128)(2,1)} %shard_map.109), calls=%async_computation | async-start | bytes 1572864 | tf_op jit(solution)/shard_map/all_to_all | solution.py:461
  16.1 1.0 %shard_map.110 = (bf16[400,128]{1,0:T(8,128)(2,1)S(1)}, bf16[400,128]{1,0:T(8,128)(2,1)S(1)}, bf16[400,128]{1,0:T(8,128)(2,1)S(1)}, bf16[400,128]{1,0:T(8,128)(2,1)S(1)}) custom-call(s32[1]{0:T(128)} %bitcast.1.x_ref, bf16[128,768]{1,0:T(8,128)(2,1)S(1)} %bitcast.17, bf16[128,768]{1,0:T(8,128)(2,1)S(1)} %bitcast.18, bf16[8,128,128]{2,1,0:T(8,128)(2,1)S(1)} %bitcast.15, ...), custom_call_target="tpu_custom_call" | custom-call | flops 6291456 | bytes 1500000 | tf_op jit(solution)/shard_map/pallas_call | solution.py:371
  17.1 3.4 %collective-permute-start = (bf16[400,128]{1,0:T(8,128)(2,1)S(1)}, bf16[400,128]{1,0:T(8,128)(2,1)S(1)}, u32[]{:S(2)}, u32[]{:S(2)}) collective-permute-start(bf16[400,128]{1,0:T(8,128)(2,1)S(1)} %get-tuple-element.47), channel_id=1, source_target_pairs={{0,4},{1,5},{2,6},{3,7},{4,8},{5,9},{6,10},{7,11},{8,12},{9,13},{1... | collective-permute-start | bytes 307208 | tf_op jit(solution)/shard_map/ppermute | solution.py:480
  20.5 4.3 %collective-permute-start.1 = (bf16[400,128]{1,0:T(8,128)(2,1)S(1)}, bf16[400,128]{1,0:T(8,128)(2,1)S(1)}, u32[]{:S(2)}, u32[]{:S(2)}) collective-permute-start(bf16[400,128]{1,0:T(8,128)(2,1)S(1)} %get-tuple-element.48), channel_id=1, source_target_pairs={{0,8},{1,9},{2,10},{3,11},{4,12},{5,13},{6,14},{7,15},{8,0},{9,1},... | collective-permute-start | bytes 307208 | tf_op jit(solution)/shard_map/ppermute | solution.py:480
  24.8 3.1 %collective-permute-start.2 = (bf16[400,128]{1,0:T(8,128)(2,1)S(1)}, bf16[400,128]{1,0:T(8,128)(2,1)S(1)}, u32[]{:S(2)}, u32[]{:S(2)}) collective-permute-start(bf16[400,128]{1,0:T(8,128)(2,1)S(1)} %get-tuple-element.49), channel_id=1, source_target_pairs={{0,12},{1,13},{2,14},{3,15},{4,0},{5,1},{6,2},{7,3},{8,4},{9,5},{1... | collective-permute-start | bytes 307208 | tf_op jit(solution)/shard_map/ppermute | solution.py:480
  27.9 2.1 %collective-permute-done.1.qd2 = bf16[400,128]{1,0:T(8,128)(2,1)S(1)} collective-permute-done((bf16[400,128]{1,0:T(8,128)(2,1)S(1)}, bf16[400,128]{1,0:T(8,128)(2,1)S(1)}, u32[]{:S(2)}, u32[]{:S(2)}) %collective-permute-start.1) | collective-permute-done | bytes 102432 | tf_op jit(solution)/shard_map/ppermute | solution.py:480
  30.1 2.7 %collective-permute-done.2.qd3 = bf16[400,128]{1,0:T(8,128)(2,1)S(1)} collective-permute-done((bf16[400,128]{1,0:T(8,128)(2,1)S(1)}, bf16[400,128]{1,0:T(8,128)(2,1)S(1)}, u32[]{:S(2)}, u32[]{:S(2)}) %collective-permute-start.2) | collective-permute-done | bytes 102432 | tf_op jit(solution)/shard_map/ppermute | solution.py:480
  32.7 0.0 all-to-all-done.kv_own
  32.7 3.2 %collective-permute-start.3 = (bf16[8,384,128]{2,1,0:T(8,128)(2,1)S(1)}, bf16[8,384,128]{2,1,0:T(8,128)(2,1)S(1)}, u32[]{:S(2)}, u32[]{:S(2)}) collective-permute-start(bf16[8,384,128]{2,1,0:T(8,128)(2,1)S(1)} %all-to-all-done.kv_own), channel_id=1, source_target_pairs={{0,1},{1,0},{2,3},{3,2},{4,5},{5,4},{6,7},{7,6},{8,9},{9,8},{10,11... | collective-permute-start | bytes 2359304 | tf_op jit(solution)/shard_map/ppermute | solution.py:482
  36.0 1.8 %shard_map.111 = (bf16[1024,512]{1,0:T(8,128)(2,1)S(1)}, bf16[1024,256]{1,0:T(8,128)(2,1)S(1)}, bf16[512,512]{1,0:T(8,128)(2,1)S(1)}, bf16[512,256]{1,0:T(8,128)...) custom-call(s32[1]{0:T(128)} %bitcast.core_ref, ...), custom_call_target="tpu_custom_call" | custom-call | flops 805306368 | bytes 6000000 | tf_op jit(solution)/shard_map/pallas_call | solution.py:371
  37.8 0.1 collective-permute-done.3.kv_other
  37.8 4.8 %shard_map.112 = (bf16[8,384,128]{2,1,0:T(8,128)(2,1)S(1)}, bf16[8,384,128]{2,1,0:T(8,128)(2,1)S(1)}, bf16[4,400,128]{2,1,0:T(8,128)(2,1)}) custom-call(s32[1]{0:T(128)} %bitcast.core_ref, s32[1]{0:T(128)} %bitcast.1.x_ref, bf16[8,384,128]{2,1,0:T(8,128)(2,1)S(1)} %collective-permute-done.3.kv_other, bf16[1024,512]{1,0:T(8,128)(2,1)S(1)} %get-tuple-element.55.ke_own, ...), custom_call_target="tpu_custom_call" | custom-call | flops 3489660928 | bytes 8000000 | tf_op jit(solution)/shard_map/pallas_call | solution.py:371
  42.7 2.3 %collective-permute-start.4 = (bf16[8,384,128]{2,1,0:T(8,128)(2,1)S(1)}, bf16[8,384,128]{2,1,0:T(8,128)(2,1)S(1)}, u32[]{:S(2)}, u32[]{:S(2)}) collective-permute-start(bf16[8,384,128]{2,1,0:T(8,128)(2,1)S(1)} %get-tuple-element.67), channel_id=1, source_target_pairs={{0,1},{1,0},{2,3},{3,2},{4,5},{5,4},{6,7},{7,6},{8,9},{9,8},{10,11... | collective-permute-start | bytes 2359304 | tf_op jit(solution)/shard_map/ppermute | solution.py:486
  44.9 4.0 %all-to-all-start.1 = ((bf16[4,400,128]{2,1,0:T(8,128)(2,1)}), bf16[4,400,128]{2,1,0:T(8,128)(2,1)S(1)}, u32[]{:S(2)}, u32[]{:S(2)}) async-start(bf16[4,400,128]{2,1,0:T(8,128)(2,1)} %get-tuple-element.63), calls=%async_computation.1 | async-start | bytes 819200 | tf_op jit(solution)/shard_map/all_to_all | solution.py:485
  48.9 0.2 shard_map.115
  49.1 6.2 %collective-permute-start.5 = (bf16[4,384,128]{2,1,0:T(8,128)(2,1)S(1)}, bf16[4,384,128]{2,1,0:T(8,128)(2,1)S(1)}, u32[]{:S(2)}, u32[]{:S(2)}) collective-permute-start(bf16[4,384,128]{2,1,0:T(8,128)(2,1)S(1)} %get-tuple-element.70), channel_id=1, source_target_pairs={{0,2},{1,3},{2,0},{3,1},{4,6},{5,7},{6,4},{7,5},{8,10},{9,11},{10,... | collective-permute-start | bytes 1179656 | tf_op jit(solution)/shard_map/ppermute | solution.py:495
  55.3 1.5 %all-to-all-done.1.oq_ref = bf16[4,400,128]{2,1,0:T(8,128)(2,1)S(1)} async-done(((bf16[4,400,128]{2,1,0:T(8,128)(2,1)}), bf16[4,400,128]{2,1,0:T(8,128)(2,1)S(1)}, u32[]{:S(2)}, u32[]{:S(2)}) %all-to-all-start.1) | async-done | bytes 409632 | tf_op jit(solution)/shard_map/all_to_all | solution.py:485
  56.8 0.1 shard_map.114
  57.0 8.6 %all_to_all.20 = f32[8,4,128]{2,1,0:T(4,128)S(1)} all-to-all(f32[8,4,128]{2,1,0:T(4,128)S(1)} %shard_map.114), channel_id=1, replica_groups={{0,1,4,5,8,9,12,13},{2,3,6,7,10,11,14,15},{16,17,20,21,24,25,28,29},{18..., dimensions={0} | all-to-all | bytes 32768 | tf_op jit(solution)/shard_map/all_to_all | solution.py:500
  65.6 0.7 broadcast_in_dim.23
  66.2 17.3 %all-to-all-start.3 = ((f32[64,4,128]{2,1,0:T(4,128)}), f32[64,4,128]{2,1,0:T(4,128)S(1)}, u32[]{:S(2)}, u32[]{:S(2)}) async-start(f32[64,4,128]{2,1,0:T(4,128)} %broadcast_in_dim.23), calls=%async_computation.3 | async-start | bytes 262144 | tf_op jit(solution)/shard_map/all_to_all | solution.py:503
  83.6 0.0 collective-permute-done.5.come_ref
  83.6 0.1 shard_map.116
  83.7 2.2 %collective-permute-start.6 = (bf16[384,128]{1,0:T(8,128)(2,1)S(1)}, bf16[384,128]{1,0:T(8,128)(2,1)S(1)}, u32[]{:S(2)}, u32[]{:S(2)}) collective-permute-start(bf16[384,128]{1,0:T(8,128)(2,1)S(1)} %get-tuple-element.72), channel_id=1, source_target_pairs={{0,4},{1,5},{2,6},{3,7},{4,8},{5,9},{6,10},{7,11},{8,12},{9,13},{1... | collective-permute-start | bytes 294920 | tf_op jit(solution)/shard_map/ppermute | solution.py:520
  85.9 3.7 %collective-permute-start.7 = (bf16[384,128]{1,0:T(8,128)(2,1)S(1)}, bf16[384,128]{1,0:T(8,128)(2,1)S(1)}, u32[]{:S(2)}, u32[]{:S(2)}) collective-permute-start(bf16[384,128]{1,0:T(8,128)(2,1)S(1)} %get-tuple-element.73), channel_id=1, source_target_pairs={{0,8},{1,9},{2,10},{3,11},{4,12},{5,13},{6,14},{7,15},{8,0},{9,1},... | collective-permute-start | bytes 294920 | tf_op jit(solution)/shard_map/ppermute | solution.py:520
  89.6 2.8 %collective-permute-start.8 = (bf16[384,128]{1,0:T(8,128)(2,1)S(1)}, bf16[384,128]{1,0:T(8,128)(2,1)S(1)}, u32[]{:S(2)}, u32[]{:S(2)}) collective-permute-start(bf16[384,128]{1,0:T(8,128)(2,1)S(1)} %get-tuple-element.74), channel_id=1, source_target_pairs={{0,12},{1,13},{2,14},{3,15},{4,0},{5,1},{6,2},{7,3},{8,4},{9,5},{1... | collective-permute-start | bytes 294920 | tf_op jit(solution)/shard_map/ppermute | solution.py:520
  92.3 1.1 %shard_map.113 = (bf16[128,768]{1,0:T(8,128)(2,1)}, bf16[128,768]{1,0:T(8,128)(2,1)}, bf16[8,128,128]{2,1,0:T(8,128)(2,1)}) custom-call(bf16[4,400,128]{2,1,0:T(8,128)(2,1)S(1)} %all-to-all-done.1.oq_ref, f32[4,128]{1,0:T(4,128)S(1)} %bitcast.20), custom_call_target="tpu_custom_call" | custom-call | flops 4194304 | bytes 1100000 | tf_op jit(solution)/shard_map/pallas_call | solution.py:371
  93.4 2.1 %all-to-all-done.3.far_ref = f32[64,4,128]{2,1,0:T(4,128)S(1)} async-done(((f32[64,4,128]{2,1,0:T(4,128)}), f32[64,4,128]{2,1,0:T(4,128)S(1)}, u32[]{:S(2)}, u32[]{:S(2)}) %all-to-all-start.3) | async-done | bytes 131104 | tf_op jit(solution)/shard_map/all_to_all | solution.py:503
  95.5 0.0 collective-permute-done.6.in1
  95.6 0.0 collective-permute-done.7.in2
  95.6 0.9 shard_map.117
  (12 shorter events, 0.0 us)
Async XLA Ops:
  0.6 15.5 %copy-start.2 = (bf16[1,128,768]{2,1,0:T(8,128)(2,1)S(1)}, bf16[1,128,768]{2,1,0:T(8,128)(2,1)}, u32[]{:S(2)}) copy-start(bf16[1,128,768]{2,1,0:T(8,128)(2,1)} %param.9) | copy-start | bytes 589828
  0.6 15.5 %copy-start.1 = (bf16[1,128,768]{2,1,0:T(8,128)(2,1)S(1)}, bf16[1,128,768]{2,1,0:T(8,128)(2,1)}, u32[]{:S(2)}) copy-start(bf16[1,128,768]{2,1,0:T(8,128)(2,1)} %param.6) | copy-start | bytes 589828
  0.7 15.5 %copy-start.3 = (f32[128,4]{0,1:T(4,128)S(1)}, f32[128,4]{0,1:T(4,128)}, u32[]{:S(2)}) copy-start(f32[128,4]{0,1:T(4,128)} %param.11) | copy-start | bytes 6148
  0.7 15.5 %copy-start = (bf16[1,8,128,128]{3,2,1,0:T(8,128)(2,1)S(1)}, bf16[1,8,128,128]{3,2,1,0:T(8,128)(2,1)}, u32[]{:S(2)}) copy-start(bf16[1,8,128,128]{3,2,1,0:T(8,128)(2,1)} %param.10) | copy-start | bytes 786436
  2.8 30.0 %all-to-all-start = ((bf16[8,384,128]{2,1,0:T(8,128)(2,1)}), bf16[8,384,128]{2,1,0:T(8,128)(2,1)S(1)}, u32[]{:S(2)}, u32[]{:S(2)}) async-start(bf16[8,384,128]{2,1,0:T(8,128)(2,1)} %shard_map.109), calls=%async_computation | async-start | bytes 1572864 | tf_op jit(solution)/shard_map/all_to_all | solution.py:461
  17.1 10.8 %collective-permute-start = (bf16[400,128]{1,0:T(8,128)(2,1)S(1)}, bf16[400,128]{1,0:T(8,128)(2,1)S(1)}, u32[]{:S(2)}, u32[]{:S(2)}) collective-permute-start(bf16[400,128]{1,0:T(8,128)(2,1)S(1)} %get-tuple-element.47), channel_id=1, source_target_pairs={{0,4},{1,5},{2,6},{3,7},{4,8},{5,9},{6,10},{7,11},{8,12},{9,13},{1... | collective-permute-start | bytes 307208 | tf_op jit(solution)/shard_map/ppermute | solution.py:480
  20.5 9.6 %collective-permute-start.1 = (bf16[400,128]{1,0:T(8,128)(2,1)S(1)}, bf16[400,128]{1,0:T(8,128)(2,1)S(1)}, u32[]{:S(2)}, u32[]{:S(2)}) collective-permute-start(bf16[400,128]{1,0:T(8,128)(2,1)S(1)} %get-tuple-element.48), channel_id=1, source_target_pairs={{0,8},{1,9},{2,10},{3,11},{4,12},{5,13},{6,14},{7,15},{8,0},{9,1},... | collective-permute-start | bytes 307208 | tf_op jit(solution)/shard_map/ppermute | solution.py:480
  24.8 7.9 %collective-permute-start.2 = (bf16[400,128]{1,0:T(8,128)(2,1)S(1)}, bf16[400,128]{1,0:T(8,128)(2,1)S(1)}, u32[]{:S(2)}, u32[]{:S(2)}) collective-permute-start(bf16[400,128]{1,0:T(8,128)(2,1)S(1)} %get-tuple-element.49), channel_id=1, source_target_pairs={{0,12},{1,13},{2,14},{3,15},{4,0},{5,1},{6,2},{7,3},{8,4},{9,5},{1... | collective-permute-start | bytes 307208 | tf_op jit(solution)/shard_map/ppermute | solution.py:480
  32.7 5.1 %collective-permute-start.3 = (bf16[8,384,128]{2,1,0:T(8,128)(2,1)S(1)}, bf16[8,384,128]{2,1,0:T(8,128)(2,1)S(1)}, u32[]{:S(2)}, u32[]{:S(2)}) collective-permute-start(bf16[8,384,128]{2,1,0:T(8,128)(2,1)S(1)} %all-to-all-done.kv_own), channel_id=1, source_target_pairs={{0,1},{1,0},{2,3},{3,2},{4,5},{5,4},{6,7},{7,6},{8,9},{9,8},{10,11... | collective-permute-start | bytes 2359304 | tf_op jit(solution)/shard_map/ppermute | solution.py:482
  42.7 6.2 %collective-permute-start.4 = (bf16[8,384,128]{2,1,0:T(8,128)(2,1)S(1)}, bf16[8,384,128]{2,1,0:T(8,128)(2,1)S(1)}, u32[]{:S(2)}, u32[]{:S(2)}) collective-permute-start(bf16[8,384,128]{2,1,0:T(8,128)(2,1)S(1)} %get-tuple-element.67), channel_id=1, source_target_pairs={{0,1},{1,0},{2,3},{3,2},{4,5},{5,4},{6,7},{7,6},{8,9},{9,8},{10,11... | collective-permute-start | bytes 2359304 | tf_op jit(solution)/shard_map/ppermute | solution.py:486
  44.9 11.9 %all-to-all-start.1 = ((bf16[4,400,128]{2,1,0:T(8,128)(2,1)}), bf16[4,400,128]{2,1,0:T(8,128)(2,1)S(1)}, u32[]{:S(2)}, u32[]{:S(2)}) async-start(bf16[4,400,128]{2,1,0:T(8,128)(2,1)} %get-tuple-element.63), calls=%async_computation.1 | async-start | bytes 819200 | tf_op jit(solution)/shard_map/all_to_all | solution.py:485
  49.1 34.5 %collective-permute-start.5 = (bf16[4,384,128]{2,1,0:T(8,128)(2,1)S(1)}, bf16[4,384,128]{2,1,0:T(8,128)(2,1)S(1)}, u32[]{:S(2)}, u32[]{:S(2)}) collective-permute-start(bf16[4,384,128]{2,1,0:T(8,128)(2,1)S(1)} %get-tuple-element.70), channel_id=1, source_target_pairs={{0,2},{1,3},{2,0},{3,1},{4,6},{5,7},{6,4},{7,5},{8,10},{9,11},{10,... | collective-permute-start | bytes 1179656 | tf_op jit(solution)/shard_map/ppermute | solution.py:495
  66.2 29.3 %all-to-all-start.3 = ((f32[64,4,128]{2,1,0:T(4,128)}), f32[64,4,128]{2,1,0:T(4,128)S(1)}, u32[]{:S(2)}, u32[]{:S(2)}) async-start(f32[64,4,128]{2,1,0:T(4,128)} %broadcast_in_dim.23), calls=%async_computation.3 | async-start | bytes 262144 | tf_op jit(solution)/shard_map/all_to_all | solution.py:503
  83.7 11.9 %collective-permute-start.6 = (bf16[384,128]{1,0:T(8,128)(2,1)S(1)}, bf16[384,128]{1,0:T(8,128)(2,1)S(1)}, u32[]{:S(2)}, u32[]{:S(2)}) collective-permute-start(bf16[384,128]{1,0:T(8,128)(2,1)S(1)} %get-tuple-element.72), channel_id=1, source_target_pairs={{0,4},{1,5},{2,6},{3,7},{4,8},{5,9},{6,10},{7,11},{8,12},{9,13},{1... | collective-permute-start | bytes 294920 | tf_op jit(solution)/shard_map/ppermute | solution.py:520
  85.9 9.7 %collective-permute-start.7 = (bf16[384,128]{1,0:T(8,128)(2,1)S(1)}, bf16[384,128]{1,0:T(8,128)(2,1)S(1)}, u32[]{:S(2)}, u32[]{:S(2)}) collective-permute-start(bf16[384,128]{1,0:T(8,128)(2,1)S(1)} %get-tuple-element.73), channel_id=1, source_target_pairs={{0,8},{1,9},{2,10},{3,11},{4,12},{5,13},{6,14},{7,15},{8,0},{9,1},... | collective-permute-start | bytes 294920 | tf_op jit(solution)/shard_map/ppermute | solution.py:520
  89.6 6.0 %collective-permute-start.8 = (bf16[384,128]{1,0:T(8,128)(2,1)S(1)}, bf16[384,128]{1,0:T(8,128)(2,1)S(1)}, u32[]{:S(2)}, u32[]{:S(2)}) collective-permute-start(bf16[384,128]{1,0:T(8,128)(2,1)S(1)} %get-tuple-element.74), channel_id=1, source_target_pairs={{0,12},{1,13},{2,14},{3,15},{4,0},{5,1},{6,2},{7,3},{8,4},{9,5},{1... | collective-permute-start | bytes 294920 | tf_op jit(solution)/shard_map/ppermute | solution.py:520

commit v7 on v6

--- a/solution.py
+++ b/solution.py
@@ -264,43 +264,9 @@
     out_ref[...] = jnp.broadcast_to((prod[0:4] + prod[4:8])[None], out_ref.shape)
 
 
-def grads_kernel(
-    x_ref, pb, dsb, ke, qe, cs, att_ref, gb_ref, dko_ref, dkx_ref, oq_ref, dqt
-):
-    dqt[...] = jnp.zeros_like(dqt)
-    for half, ref in ((1, dkx_ref), (0, dko_ref)):
-
-        def back(b, carry):
-            at = pl.ds(pl.multiple_of(half * 1024 + b * BLOCK, BLOCK), BLOCK)
-            low_ds = dsb[at, :]
-            dv = nn(pb[at, :], cs[...])
-            dk = nn(low_ds, qe[:, 0:256]) * SCALE
-            dqt[...] += tn(ke[at, 0:256], low_ds)
-            for t in range(BLOCK // 128):
-                m = b * (BLOCK // 128) + t
-                full, rest = pack_out(dk[t * 128 : (t + 1) * 128])
-                ref[m, 0:128, :] = full
-                ref[m, 256:320, :] = rest
-                full, rest = pack_out(dv[t * 128 : (t + 1) * 128])
-                ref[m, 128:256, :] = full
-                ref[m, 320:384, :] = rest
-            return carry
-
-        lax.fori_loop(0, 1024 // BLOCK, back, 0)
-
-    dq = dqt[...].T * SCALE
-    for k in range(XS):
-        to = lax.rem(x_ref[0] + XS - k, XS)
-        at = slice(k * 128, (k + 1) * 128)
-        full, rest = pack_out(att_ref[at, :].astype(F32))
-        oq_ref[to, 0:128, :] = full
-        oq_ref[to, 256:320, :] = rest
-        full, rest = pack_out(dq[at])
-        oq_ref[to, 128:256, :] = full
-        oq_ref[to, 320:384, :] = rest
-        rows = gb_ref[k * PROW : (k + 1) * PROW, :]
-        hi = rows.astype(BF).astype(F32)
-        oq_ref[to, 384:400, :] = jnp.concatenate([hi, rows - hi], axis=0).astype(BF)
+def spread_kernel(near_ref, out_ref):
+    total = jnp.sum(near_ref[...], axis=0)
+    out_ref[...] = jnp.broadcast_to(total[None], out_ref.shape)
 
 
 def cores_kernel(z_ref, own_ref, other_ref, send_ref, keep_ref):
@@ -497,9 +463,12 @@
         weight_kernel, shape(XS * CS, HEADS, 128, dtype=F32), (oq, pair_rows),
         flops=2 * 1024 * 128 * 8, moved=500_000, limit=8,
     )
-    total = lax.all_to_all(total, "seq", 0, 0, axis_index_groups=xc_groups).sum(axis=0)
+    total = lax.all_to_all(total, "seq", 0, 0, axis_index_groups=xc_groups)
     total, keep = lax.optimization_barrier((total, keep))
-    far = jnp.broadcast_to(total[None], (len(far_groups[0]), HEADS, 128))
+    far = call(
+        spread_kernel, shape(len(far_groups[0]), HEADS, 128, dtype=F32), (total,),
+        moved=150_000, limit=8,
+    )
     far = lax.all_to_all(far, ("dp", "seq"), 0, 0, axis_index_groups=far_groups)
     att, dq, gp = call(
         query_kernel,

time: 97.3 us -> 97.3 us (level)
    pallas_call x9 -> x10, Pallas kernels: 12.1 us -> 12.8 us  [call(): pl.pallas_call(kernel, out_shape=out_shape, in_specs=[SMEM] * smem + [ANY...]
  transfers between devices with their start and end apart: 12 -> 12, of which waited for: 5 -> 5; matrix products, arithmetic and copies ran while one was open for 1% -> 0% of each run, Pallas kernels for 4% -> 5%
where the time goes in v7:
time: 97.3 us; the launch traced here: 96.4 us
  starting transfers between devices  65.7 us (68%)
  Pallas kernels  12.8 us (13%)
  blocking collectives  8.57 us (9%)
  waiting for transfers between devices  8.54 us (9%)
    all_to_all x1, starting transfers between devices, body(): far = lax.all_to_all(far, ('dp', 'seq'), 0, 0, axis_index_groups=far_groups)  17.3 us
    all_to_all x1, starting transfers between devices, body(): kv_own = lax.all_to_all(kv, 'seq', 0, 0, axis_index_groups=xz_groups)  13.3 us
    pallas_call x10, Pallas kernels, call(): pl.pallas_call(kernel, out_shape=out_shape, in_specs=[SMEM] * smem + [ANY...  12.8 us
    ppermute x3, starting transfers between devices, body(): qd = [qd[0]] + [lax.ppermute(qd[k], 'seq', ring(k)) for k in range(1, XS)]  10.8 us
    ppermute x3, starting transfers between devices, body(): lax.ppermute(dkv[k], 'seq', ring(k))  8.65 us
    all_to_all x1, blocking collectives, body(): total = lax.all_to_all(total, 'seq', 0, 0, axis_index_groups=xc_groups)  8.57 us
    ppermute x1, starting transfers between devices, body(): come = lax.ppermute(send, 'seq', across)  6.23 us
    ppermute x3, waiting for transfers between devices, body(): qd = [qd[0]] + [lax.ppermute(qd[k], 'seq', ring(k)) for k in range(1, XS)]  4.8 us
  transfers between devices with their start and end apart: 12, of which 5 were waited for; matrix products, arithmetic and copies ran while one was open for 0% of the time, Pallas kernels for 5%

profile of v7, /device:TPU:1, one launch (start us, length us, event | category | flops | bytes accessed | tf_op | source)
XLA Modules:
  0.0 96.4 jit_solution(3265534678184986077)
XLA Ops:
  0.7 2.1 %shard_map.109 = bf16[8,384,128]{2,1,0:T(8,128)(2,1)} custom-call(bf16[128,768]{1,0:T(8,128)(2,1)} %bitcast.21, bf16[128,768]{1,0:T(8,128)(2,1)} %bitcast.22), custom_call_target="tpu_custom_call" | custom-call | bytes 1500000 | tf_op jit(solution)/shard_map/pallas_call | solution.py:337
  2.8 13.3 %all-to-all-start = ((bf16[8,384,128]{2,1,0:T(8,128)(2,1)}), bf16[8,384,128]{2,1,0:T(8,128)(2,1)S(1)}, u32[]{:S(2)}, u32[]{:S(2)}) async-start(bf16[8,384,128]{2,1,0:T(8,128)(2,1)} %shard_map.109), calls=%async_computation | async-start | bytes 1572864 | tf_op jit(solution)/shard_map/all_to_all | solution.py:427
  16.1 1.0 %shard_map.110 = (bf16[400,128]{1,0:T(8,128)(2,1)S(1)}, bf16[400,128]{1,0:T(8,128)(2,1)S(1)}, bf16[400,128]{1,0:T(8,128)(2,1)S(1)}, bf16[400,128]{1,0:T(8,128)(2,1)S(1)}) custom-call(s32[1]{0:T(128)} %bitcast.1.x_ref, bf16[128,768]{1,0:T(8,128)(2,1)S(1)} %bitcast.17, bf16[128,768]{1,0:T(8,128)(2,1)S(1)} %bitcast.18, bf16[8,128,128]{2,1,0:T(8,128)(2,1)S(1)} %bitcast.15, ...), custom_call_target="tpu_custom_call" | custom-call | flops 6291456 | bytes 1500000 | tf_op jit(solution)/shard_map/pallas_call | solution.py:337
  17.1 3.4 %collective-permute-start = (bf16[400,128]{1,0:T(8,128)(2,1)S(1)}, bf16[400,128]{1,0:T(8,128)(2,1)S(1)}, u32[]{:S(2)}, u32[]{:S(2)}) collective-permute-start(bf16[400,128]{1,0:T(8,128)(2,1)S(1)} %get-tuple-element.47), channel_id=1, source_target_pairs={{0,4},{1,5},{2,6},{3,7},{4,8},{5,9},{6,10},{7,11},{8,12},{9,13},{1... | collective-permute-start | bytes 307208 | tf_op jit(solution)/shard_map/ppermute | solution.py:446
  20.5 4.3 %collective-permute-start.1 = (bf16[400,128]{1,0:T(8,128)(2,1)S(1)}, bf16[400,128]{1,0:T(8,128)(2,1)S(1)}, u32[]{:S(2)}, u32[]{:S(2)}) collective-permute-start(bf16[400,128]{1,0:T(8,128)(2,1)S(1)} %get-tuple-element.48), channel_id=1, source_target_pairs={{0,8},{1,9},{2,10},{3,11},{4,12},{5,13},{6,14},{7,15},{8,0},{9,1},... | collective-permute-start | bytes 307208 | tf_op jit(solution)/shard_map/ppermute | solution.py:446
  24.8 3.1 %collective-permute-start.2 = (bf16[400,128]{1,0:T(8,128)(2,1)S(1)}, bf16[400,128]{1,0:T(8,128)(2,1)S(1)}, u32[]{:S(2)}, u32[]{:S(2)}) collective-permute-start(bf16[400,128]{1,0:T(8,128)(2,1)S(1)} %get-tuple-element.49), channel_id=1, source_target_pairs={{0,12},{1,13},{2,14},{3,15},{4,0},{5,1},{6,2},{7,3},{8,4},{9,5},{1... | collective-permute-start | bytes 307208 | tf_op jit(solution)/shard_map/ppermute | solution.py:446
  27.9 0.0 collective-permute-done.qd1
  27.9 2.1 %collective-permute-done.1.qd2 = bf16[400,128]{1,0:T(8,128)(2,1)S(1)} collective-permute-done((bf16[400,128]{1,0:T(8,128)(2,1)S(1)}, bf16[400,128]{1,0:T(8,128)(2,1)S(1)}, u32[]{:S(2)}, u32[]{:S(2)}) %collective-permute-start.1) | collective-permute-done | bytes 102432 | tf_op jit(solution)/shard_map/ppermute | solution.py:446
  30.1 2.7 %collective-permute-done.2.qd3 = bf16[400,128]{1,0:T(8,128)(2,1)S(1)} collective-permute-done((bf16[400,128]{1,0:T(8,128)(2,1)S(1)}, bf16[400,128]{1,0:T(8,128)(2,1)S(1)}, u32[]{:S(2)}, u32[]{:S(2)}) %collective-permute-start.2) | collective-permute-done | bytes 102432 | tf_op jit(solution)/shard_map/ppermute | solution.py:446
  32.7 0.0 all-to-all-done.kv_own
  32.7 3.2 %collective-permute-start.3 = (bf16[8,384,128]{2,1,0:T(8,128)(2,1)S(1)}, bf16[8,384,128]{2,1,0:T(8,128)(2,1)S(1)}, u32[]{:S(2)}, u32[]{:S(2)}) collective-permute-start(bf16[8,384,128]{2,1,0:T(8,128)(2,1)S(1)} %all-to-all-done.kv_own), channel_id=1, source_target_pairs={{0,1},{1,0},{2,3},{3,2},{4,5},{5,4},{6,7},{7,6},{8,9},{9,8},{10,11... | collective-permute-start | bytes 2359304 | tf_op jit(solution)/shard_map/ppermute | solution.py:448
  36.0 1.8 %shard_map.111 = (bf16[1024,512]{1,0:T(8,128)(2,1)S(1)}, bf16[1024,256]{1,0:T(8,128)(2,1)S(1)}, bf16[512,512]{1,0:T(8,128)(2,1)S(1)}, bf16[512,256]{1,0:T(8,128)...) custom-call(s32[1]{0:T(128)} %bitcast.core_ref, ...), custom_call_target="tpu_custom_call" | custom-call | flops 805306368 | bytes 6000000 | tf_op jit(solution)/shard_map/pallas_call | solution.py:337
  37.7 0.1 collective-permute-done.3.kv_other
  37.8 4.8 %shard_map.112 = (bf16[8,384,128]{2,1,0:T(8,128)(2,1)S(1)}, bf16[8,384,128]{2,1,0:T(8,128)(2,1)S(1)}, bf16[4,400,128]{2,1,0:T(8,128)(2,1)}) custom-call(s32[1]{0:T(128)} %bitcast.core_ref, s32[1]{0:T(128)} %bitcast.1.x_ref, bf16[8,384,128]{2,1,0:T(8,128)(2,1)S(1)} %collective-permute-done.3.kv_other, bf16[1024,512]{1,0:T(8,128)(2,1)S(1)} %get-tuple-element.55.ke_own, ...), custom_call_target="tpu_custom_call" | custom-call | flops 3489660928 | bytes 8000000 | tf_op jit(solution)/shard_map/pallas_call | solution.py:337
  42.7 2.3 %collective-permute-start.4 = (bf16[8,384,128]{2,1,0:T(8,128)(2,1)S(1)}, bf16[8,384,128]{2,1,0:T(8,128)(2,1)S(1)}, u32[]{:S(2)}, u32[]{:S(2)}) collective-permute-start(bf16[8,384,128]{2,1,0:T(8,128)(2,1)S(1)} %get-tuple-element.67), channel_id=1, source_target_pairs={{0,1},{1,0},{2,3},{3,2},{4,5},{5,4},{6,7},{7,6},{8,9},{9,8},{10,11... | collective-permute-start | bytes 2359304 | tf_op jit(solution)/shard_map/ppermute | solution.py:452
  44.9 4.0 %all-to-all-start.1 = ((bf16[4,400,128]{2,1,0:T(8,128)(2,1)}), bf16[4,400,128]{2,1,0:T(8,128)(2,1)S(1)}, u32[]{:S(2)}, u32[]{:S(2)}) async-start(bf16[4,400,128]{2,1,0:T(8,128)(2,1)} %get-tuple-element.63), calls=%async_computation.1 | async-start | bytes 819200 | tf_op jit(solution)/shard_map/all_to_all | solution.py:451
  48.9 0.0 collective-permute-done.4.other_ref
  48.9 0.2 shard_map.115
  49.1 6.2 %collective-permute-start.5 = (bf16[4,384,128]{2,1,0:T(8,128)(2,1)S(1)}, bf16[4,384,128]{2,1,0:T(8,128)(2,1)S(1)}, u32[]{:S(2)}, u32[]{:S(2)}) collective-permute-start(bf16[4,384,128]{2,1,0:T(8,128)(2,1)S(1)} %get-tuple-element.70), channel_id=1, source_target_pairs={{0,2},{1,3},{2,0},{3,1},{4,6},{5,7},{6,4},{7,5},{8,10},{9,11},{10,... | collective-permute-start | bytes 1179656 | tf_op jit(solution)/shard_map/ppermute | solution.py:461
  55.3 1.5 %all-to-all-done.1.oq_ref = bf16[4,400,128]{2,1,0:T(8,128)(2,1)S(1)} async-done(((bf16[4,400,128]{2,1,0:T(8,128)(2,1)}), bf16[4,400,128]{2,1,0:T(8,128)(2,1)S(1)}, u32[]{:S(2)}, u32[]{:S(2)}) %all-to-all-start.1) | async-done | bytes 409632 | tf_op jit(solution)/shard_map/all_to_all | solution.py:451
  56.8 0.1 shard_map.114
  57.0 8.6 %all_to_all.20.near_ref = f32[8,4,128]{2,1,0:T(4,128)S(1)} all-to-all(f32[8,4,128]{2,1,0:T(4,128)S(1)} %shard_map.114), channel_id=1, replica_groups={{0,1,4,5,8,9,12,13},{2,3,6,7,10,11,14,15},{16,17,20,21,24,25,28,29},{18..., dimensions={0} | all-to-all | bytes 32768 | tf_op jit(solution)/shard_map/all_to_all | solution.py:466
  65.5 0.7 shard_map.117
  66.2 17.3 %all-to-all-start.3 = ((f32[64,4,128]{2,1,0:T(4,128)}), f32[64,4,128]{2,1,0:T(4,128)S(1)}, u32[]{:S(2)}, u32[]{:S(2)}) async-start(f32[64,4,128]{2,1,0:T(4,128)} %shard_map.117), calls=%async_computation.3 | async-start | bytes 262144 | tf_op jit(solution)/shard_map/all_to_all | solution.py:472
  83.6 0.1 shard_map.116
  83.7 2.2 %collective-permute-start.6 = (bf16[384,128]{1,0:T(8,128)(2,1)S(1)}, bf16[384,128]{1,0:T(8,128)(2,1)S(1)}, u32[]{:S(2)}, u32[]{:S(2)}) collective-permute-start(bf16[384,128]{1,0:T(8,128)(2,1)S(1)} %get-tuple-element.72), channel_id=1, source_target_pairs={{0,4},{1,5},{2,6},{3,7},{4,8},{5,9},{6,10},{7,11},{8,12},{9,13},{1... | collective-permute-start | bytes 294920 | tf_op jit(solution)/shard_map/ppermute | solution.py:489
  85.9 3.7 %collective-permute-start.7 = (bf16[384,128]{1,0:T(8,128)(2,1)S(1)}, bf16[384,128]{1,0:T(8,128)(2,1)S(1)}, u32[]{:S(2)}, u32[]{:S(2)}) collective-permute-start(bf16[384,128]{1,0:T(8,128)(2,1)S(1)} %get-tuple-element.73), channel_id=1, source_target_pairs={{0,8},{1,9},{2,10},{3,11},{4,12},{5,13},{6,14},{7,15},{8,0},{9,1},... | collective-permute-start | bytes 294920 | tf_op jit(solution)/shard_map/ppermute | solution.py:489
  89.6 2.8 %collective-permute-start.8 = (bf16[384,128]{1,0:T(8,128)(2,1)S(1)}, bf16[384,128]{1,0:T(8,128)(2,1)S(1)}, u32[]{:S(2)}, u32[]{:S(2)}) collective-permute-start(bf16[384,128]{1,0:T(8,128)(2,1)S(1)} %get-tuple-element.74), channel_id=1, source_target_pairs={{0,12},{1,13},{2,14},{3,15},{4,0},{5,1},{6,2},{7,3},{8,4},{9,5},{1... | collective-permute-start | bytes 294920 | tf_op jit(solution)/shard_map/ppermute | solution.py:489
  92.3 1.1 %shard_map.113 = (bf16[128,768]{1,0:T(8,128)(2,1)}, bf16[128,768]{1,0:T(8,128)(2,1)}, bf16[8,128,128]{2,1,0:T(8,128)(2,1)}) custom-call(bf16[4,400,128]{2,1,0:T(8,128)(2,1)S(1)} %all-to-all-done.1.oq_ref, f32[4,128]{1,0:T(4,128)S(1)} %bitcast.20), custom_call_target="tpu_custom_call" | custom-call | flops 4194304 | bytes 1100000 | tf_op jit(solution)/shard_map/pallas_call | solution.py:337
  93.4 2.1 %all-to-all-done.3.far_ref = f32[64,4,128]{2,1,0:T(4,128)S(1)} async-done(((f32[64,4,128]{2,1,0:T(4,128)}), f32[64,4,128]{2,1,0:T(4,128)S(1)}, u32[]{:S(2)}, u32[]{:S(2)}) %all-to-all-start.3) | async-done | bytes 131104 | tf_op jit(solution)/shard_map/all_to_all | solution.py:472
  95.5 0.0 collective-permute-done.6.in1
  95.5 0.9 shard_map.118
  (11 shorter events, 0.0 us)
Async XLA Ops:
  0.6 15.4 %copy-start.2 = (bf16[1,128,768]{2,1,0:T(8,128)(2,1)S(1)}, bf16[1,128,768]{2,1,0:T(8,128)(2,1)}, u32[]{:S(2)}) copy-start(bf16[1,128,768]{2,1,0:T(8,128)(2,1)} %param.9) | copy-start | bytes 589828
  0.6 15.4 %copy-start.1 = (bf16[1,128,768]{2,1,0:T(8,128)(2,1)S(1)}, bf16[1,128,768]{2,1,0:T(8,128)(2,1)}, u32[]{:S(2)}) copy-start(bf16[1,128,768]{2,1,0:T(8,128)(2,1)} %param.6) | copy-start | bytes 589828
  0.7 15.4 %copy-start.3 = (f32[128,4]{0,1:T(4,128)S(1)}, f32[128,4]{0,1:T(4,128)}, u32[]{:S(2)}) copy-start(f32[128,4]{0,1:T(4,128)} %param.11) | copy-start | bytes 6148
  0.7 15.4 %copy-start = (bf16[1,8,128,128]{3,2,1,0:T(8,128)(2,1)S(1)}, bf16[1,8,128,128]{3,2,1,0:T(8,128)(2,1)}, u32[]{:S(2)}) copy-start(bf16[1,8,128,128]{3,2,1,0:T(8,128)(2,1)} %param.10) | copy-start | bytes 786436
  2.8 30.0 %all-to-all-start = ((bf16[8,384,128]{2,1,0:T(8,128)(2,1)}), bf16[8,384,128]{2,1,0:T(8,128)(2,1)S(1)}, u32[]{:S(2)}, u32[]{:S(2)}) async-start(bf16[8,384,128]{2,1,0:T(8,128)(2,1)} %shard_map.109), calls=%async_computation | async-start | bytes 1572864 | tf_op jit(solution)/shard_map/all_to_all | solution.py:427
  17.1 10.8 %collective-permute-start = (bf16[400,128]{1,0:T(8,128)(2,1)S(1)}, bf16[400,128]{1,0:T(8,128)(2,1)S(1)}, u32[]{:S(2)}, u32[]{:S(2)}) collective-permute-start(bf16[400,128]{1,0:T(8,128)(2,1)S(1)} %get-tuple-element.47), channel_id=1, source_target_pairs={{0,4},{1,5},{2,6},{3,7},{4,8},{5,9},{6,10},{7,11},{8,12},{9,13},{1... | collective-permute-start | bytes 307208 | tf_op jit(solution)/shard_map/ppermute | solution.py:446
  20.5 9.6 %collective-permute-start.1 = (bf16[400,128]{1,0:T(8,128)(2,1)S(1)}, bf16[400,128]{1,0:T(8,128)(2,1)S(1)}, u32[]{:S(2)}, u32[]{:S(2)}) collective-permute-start(bf16[400,128]{1,0:T(8,128)(2,1)S(1)} %get-tuple-element.48), channel_id=1, source_target_pairs={{0,8},{1,9},{2,10},{3,11},{4,12},{5,13},{6,14},{7,15},{8,0},{9,1},... | collective-permute-start | bytes 307208 | tf_op jit(solution)/shard_map/ppermute | solution.py:446
  24.8 7.9 %collective-permute-start.2 = (bf16[400,128]{1,0:T(8,128)(2,1)S(1)}, bf16[400,128]{1,0:T(8,128)(2,1)S(1)}, u32[]{:S(2)}, u32[]{:S(2)}) collective-permute-start(bf16[400,128]{1,0:T(8,128)(2,1)S(1)} %get-tuple-element.49), channel_id=1, source_target_pairs={{0,12},{1,13},{2,14},{3,15},{4,0},{5,1},{6,2},{7,3},{8,4},{9,5},{1... | collective-permute-start | bytes 307208 | tf_op jit(solution)/shard_map/ppermute | solution.py:446
  32.7 5.1 %collective-permute-start.3 = (bf16[8,384,128]{2,1,0:T(8,128)(2,1)S(1)}, bf16[8,384,128]{2,1,0:T(8,128)(2,1)S(1)}, u32[]{:S(2)}, u32[]{:S(2)}) collective-permute-start(bf16[8,384,128]{2,1,0:T(8,128)(2,1)S(1)} %all-to-all-done.kv_own), channel_id=1, source_target_pairs={{0,1},{1,0},{2,3},{3,2},{4,5},{5,4},{6,7},{7,6},{8,9},{9,8},{10,11... | collective-permute-start | bytes 2359304 | tf_op jit(solution)/shard_map/ppermute | solution.py:448
  42.7 6.2 %collective-permute-start.4 = (bf16[8,384,128]{2,1,0:T(8,128)(2,1)S(1)}, bf16[8,384,128]{2,1,0:T(8,128)(2,1)S(1)}, u32[]{:S(2)}, u32[]{:S(2)}) collective-permute-start(bf16[8,384,128]{2,1,0:T(8,128)(2,1)S(1)} %get-tuple-element.67), channel_id=1, source_target_pairs={{0,1},{1,0},{2,3},{3,2},{4,5},{5,4},{6,7},{7,6},{8,9},{9,8},{10,11... | collective-permute-start | bytes 2359304 | tf_op jit(solution)/shard_map/ppermute | solution.py:452
  44.9 11.9 %all-to-all-start.1 = ((bf16[4,400,128]{2,1,0:T(8,128)(2,1)}), bf16[4,400,128]{2,1,0:T(8,128)(2,1)S(1)}, u32[]{:S(2)}, u32[]{:S(2)}) async-start(bf16[4,400,128]{2,1,0:T(8,128)(2,1)} %get-tuple-element.63), calls=%async_computation.1 | async-start | bytes 819200 | tf_op jit(solution)/shard_map/all_to_all | solution.py:451
  49.1 34.5 %collective-permute-start.5 = (bf16[4,384,128]{2,1,0:T(8,128)(2,1)S(1)}, bf16[4,384,128]{2,1,0:T(8,128)(2,1)S(1)}, u32[]{:S(2)}, u32[]{:S(2)}) collective-permute-start(bf16[4,384,128]{2,1,0:T(8,128)(2,1)S(1)} %get-tuple-element.70), channel_id=1, source_target_pairs={{0,2},{1,3},{2,0},{3,1},{4,6},{5,7},{6,4},{7,5},{8,10},{9,11},{10,... | collective-permute-start | bytes 1179656 | tf_op jit(solution)/shard_map/ppermute | solution.py:461
  66.2 29.3 %all-to-all-start.3 = ((f32[64,4,128]{2,1,0:T(4,128)}), f32[64,4,128]{2,1,0:T(4,128)S(1)}, u32[]{:S(2)}, u32[]{:S(2)}) async-start(f32[64,4,128]{2,1,0:T(4,128)} %shard_map.117), calls=%async_computation.3 | async-start | bytes 262144 | tf_op jit(solution)/shard_map/all_to_all | solution.py:472
  83.7 11.9 %collective-permute-start.6 = (bf16[384,128]{1,0:T(8,128)(2,1)S(1)}, bf16[384,128]{1,0:T(8,128)(2,1)S(1)}, u32[]{:S(2)}, u32[]{:S(2)}) collective-permute-start(bf16[384,128]{1,0:T(8,128)(2,1)S(1)} %get-tuple-element.72), channel_id=1, source_target_pairs={{0,4},{1,5},{2,6},{3,7},{4,8},{5,9},{6,10},{7,11},{8,12},{9,13},{1... | collective-permute-start | bytes 294920 | tf_op jit(solution)/shard_map/ppermute | solution.py:489
  85.9 9.7 %collective-permute-start.7 = (bf16[384,128]{1,0:T(8,128)(2,1)S(1)}, bf16[384,128]{1,0:T(8,128)(2,1)S(1)}, u32[]{:S(2)}, u32[]{:S(2)}) collective-permute-start(bf16[384,128]{1,0:T(8,128)(2,1)S(1)} %get-tuple-element.73), channel_id=1, source_target_pairs={{0,8},{1,9},{2,10},{3,11},{4,12},{5,13},{6,14},{7,15},{8,0},{9,1},... | collective-permute-start | bytes 294920 | tf_op jit(solution)/shard_map/ppermute | solution.py:489
  89.6 6.0 %collective-permute-start.8 = (bf16[384,128]{1,0:T(8,128)(2,1)S(1)}, bf16[384,128]{1,0:T(8,128)(2,1)S(1)}, u32[]{:S(2)}, u32[]{:S(2)}) collective-permute-start(bf16[384,128]{1,0:T(8,128)(2,1)S(1)} %get-tuple-element.74), channel_id=1, source_target_pairs={{0,12},{1,13},{2,14},{3,15},{4,0},{5,1},{6,2},{7,3},{8,4},{9,5},{1... | collective-permute-start | bytes 294920 | tf_op jit(solution)/shard_map/ppermute | solution.py:489
